TPU v7x, 32 devices: a whole 2x2x4 slice. The times are simulated.
32 devices in a mesh: dp: 8 (over z, core), tm: 4 (over y, x).
Axes of the slice: x: 2, y: 2, z: 4, core: 2. Of those that a mesh axis runs over, the one named last changes fastest.
Arguments:
- video_tokens: bfloat16 [8, 32, 196, 768], P('dp', 'tm'), may hold values from -6 to 6
- norm_gain: bfloat16 [768], P('dp'), may hold values from 0.25 to 1.75
- norm_bias: bfloat16 [768], P('dp'), may hold values from -3 to 3
- qkv_weight: bfloat16 [768, 1152], P('dp'), may hold values from -16 to 16
- frame_counts: int32 [8], P('dp'), may hold values from 16 to 32, as said below
- clip_starts: int32 [8, 2], P('dp'), may hold values 0 or 1
- frame_kept: int32 [8, 32], P('dp'), may hold values 0 or 1
- attended_grad: bfloat16 [8, 32, 196, 384], P('dp', 'tm'), may hold values from -6 to 6
Outputs:
- attended: bfloat16 [8, 32, 196, 384], P('dp', 'tm')
- tokens_grad: bfloat16 [8, 32, 196, 768], P('dp', 'tm')
- qkv_weight_grad: float32 [768, 1152], P('dp')
- gain_grad: float32 [768], P('dp')
- bias_grad: float32 [768], P('dp')
Inputs may be any that keep to these rules, and one draw needn't show every extreme that they name: `frame_counts`: every count is a multiple of 16; some video has 32 frames and some video has 16.
All inputs are finite; a program needn't handle non-finite values. No bound on the sum of `clip_starts` or of `frame_kept` on one device may be relied on, other than what follows from the above.
Results may differ from a plain program's by a relative error of at most 0.02.
Values may be sent and summed in bfloat16 or wider, within the bound.
No kernel may reach another device: no remote copies, remote signals or barrier semaphores. Data moves between devices by JAX's collectives and lax.ppermute only.
A program may use at most 128 MiB of HBM per device.

v0:
```python
import jax
import jax.numpy as jnp
from jax import lax
from jax.sharding import PartitionSpec as P

HEADS = 6
BLOCK = 16


masked_value = -1e30
epsilon = 1e-05


def standardize(rows):
    centred = rows - jnp.mean(rows, axis=-1, keepdims=True)
    inverse = lax.rsqrt(jnp.mean(centred * centred, axis=-1, keepdims=True) + epsilon)
    return (centred * inverse, inverse)


def frame_masks(frame_count, starts, kept, frames):
    frame_index = jnp.arange(frames, dtype=jnp.int32)
    block_index = jnp.arange(starts.shape[0], dtype=jnp.int32)
    flags = jnp.where(block_index > 0, starts, 0)
    clip_of_block = jnp.cumsum(flags)
    member = (frame_index // BLOCK)[:, None] == block_index[None, :]
    clip_number = jnp.sum(jnp.where(member, clip_of_block[None, :], 0), axis=1)
    usable = (frame_index < frame_count) & (kept == 1)
    same_clip = clip_number[:, None] == clip_number[None, :]
    allowed = same_clip & (usable[None, :] | (frame_index[:, None] == frame_index[None, :]))
    return (allowed, frame_index < frame_count)


def split_heads(projected, start, joined):
    return projected[:, :, start : start + joined].reshape(
        projected.shape[0], projected.shape[1], HEADS, joined // HEADS
    )


def attend(projected, allowed, valid):
    frames, patch_rows = (projected.shape[0], projected.shape[1])
    joined = projected.shape[2] // 3
    scale = (joined // HEADS) ** (-0.5)
    queries = split_heads(projected, 0, joined)
    key_rows = split_heads(projected, joined, joined)
    values = split_heads(projected, 2 * joined, joined)
    scores = (
        jnp.einsum("fphd,gphd->phfg", queries, key_rows, preferred_element_type=jnp.float32) * scale
    )
    scores = jnp.where(allowed, scores, masked_value)
    shifted = jnp.exp(scores - jnp.max(scores, axis=-1, keepdims=True))
    weights = shifted / jnp.sum(shifted, axis=-1, keepdims=True)
    mixed = jnp.einsum(
        "phfg,gphd->fphd", weights.astype(jnp.bfloat16), values, preferred_element_type=jnp.float32
    )
    mixed = jnp.where(valid[:, None, None, None], mixed, 0.0)
    return (mixed.reshape(frames, patch_rows, joined).astype(jnp.bfloat16), weights)


def attend_back(projected, weights, upstream, valid):
    frames, patch_rows = (projected.shape[0], projected.shape[1])
    joined = projected.shape[2] // 3
    head_width = joined // HEADS
    scale = head_width ** (-0.5)
    queries = split_heads(projected, 0, joined)
    key_rows = split_heads(projected, joined, joined)
    values = split_heads(projected, 2 * joined, joined)
    kept_grad = jnp.where(valid[:, None, None], upstream, jnp.zeros_like(upstream))
    kept_grad = kept_grad.reshape(frames, patch_rows, HEADS, head_width)
    rounded = weights.astype(jnp.bfloat16)
    weight_grad = jnp.einsum(
        "fphd,gphd->phfg", kept_grad, values, preferred_element_type=jnp.float32
    )
    value_grad = jnp.einsum(
        "phfg,fphd->gphd", rounded, kept_grad, preferred_element_type=jnp.float32
    )
    inner = jnp.sum(weight_grad * weights, axis=-1, keepdims=True)
    score_grad = (weights * (weight_grad - inner) * scale).astype(jnp.bfloat16)
    query_grad = jnp.einsum(
        "phfg,gphd->fphd", score_grad, key_rows, preferred_element_type=jnp.float32
    )
    key_grad = jnp.einsum(
        "phfg,fphd->gphd", score_grad, queries, preferred_element_type=jnp.float32
    )
    parts = [query_grad, key_grad, value_grad]
    return jnp.concatenate(
        [piece.reshape(frames, patch_rows, joined) for piece in parts], axis=2
    ).astype(jnp.bfloat16)


def to_patches(block_rows, tm_count):
    patches = block_rows.shape[1]
    padded = -(-patches // tm_count) * tm_count
    widened = jnp.pad(block_rows, ((0, 0), (0, padded - patches), (0, 0)))
    return lax.all_to_all(widened, "tm", split_axis=1, concat_axis=0, tiled=True)


def to_frames(patch_rows, patches):
    regrouped = lax.all_to_all(patch_rows, "tm", split_axis=0, concat_axis=1, tiled=True)
    return regrouped[:, :patches]


def body(
    video_tokens,
    norm_gain,
    norm_bias,
    qkv_weight,
    frame_counts,
    clip_starts,
    frame_kept,
    attended_grad,
):
    tm_count = lax.axis_size("tm")
    weight_full, gain_full, bias_full = (
        lax.all_gather(qkv_weight, "dp", axis=0, tiled=True),
        lax.all_gather(norm_gain, "dp", axis=0, tiled=True),
        lax.all_gather(norm_bias, "dp", axis=0, tiled=True),
    )
    frames_dev, patches, model_width = (
        video_tokens.shape[1],
        video_tokens.shape[2],
        video_tokens.shape[3],
    )
    columns = weight_full.shape[1]
    frames_all = frames_dev * tm_count
    gain_wide = gain_full.astype(jnp.float32)
    standard, inverse = standardize(video_tokens.reshape(-1, model_width).astype(jnp.float32))
    normed = (standard * gain_wide + bias_full.astype(jnp.float32)).astype(jnp.bfloat16)
    allowed, valid = frame_masks(frame_counts[0], clip_starts[0], frame_kept[0], frames_all)
    upstream = attended_grad[0]
    contract_rows = (((0,), (0,)), ((), ()))
    contract_cols = (((1,), (1,)), ((), ()))
    normed_patch = to_patches(normed.reshape(frames_dev, patches, model_width), tm_count)
    flat_patch = normed_patch.reshape(-1, model_width)
    projected = jnp.dot(flat_patch, weight_full, preferred_element_type=jnp.float32).astype(
        jnp.bfloat16
    )
    projected = projected.reshape(frames_all, -1, columns)
    mixed, weights = attend(projected, allowed, valid)
    attended = to_frames(mixed, patches)
    grad_patch = to_patches(upstream, tm_count)
    projected_grad = attend_back(projected, weights, grad_patch, valid).reshape(-1, columns)
    weight_grad = lax.dot_general(
        flat_patch, projected_grad, contract_rows, preferred_element_type=jnp.float32
    )
    normed_patch_grad = lax.dot_general(
        projected_grad, weight_full, contract_cols, preferred_element_type=jnp.float32
    ).astype(jnp.bfloat16)
    normed_grad = to_frames(normed_patch_grad.reshape(frames_all, -1, model_width), patches)
    normed_grad = normed_grad.reshape(-1, model_width).astype(jnp.float32)
    gain_part = jnp.sum(normed_grad * standard, axis=0)
    bias_part = jnp.sum(normed_grad, axis=0)
    scaled = normed_grad * gain_wide
    tokens_grad = inverse * (
        scaled
        - jnp.mean(scaled, axis=-1, keepdims=True)
        - standard * jnp.mean(scaled * standard, axis=-1, keepdims=True)
    )
    tokens_grad = tokens_grad.astype(jnp.bfloat16).reshape(1, frames_dev, patches, model_width)
    shares = (
        lax.psum_scatter(
            weight_grad.astype(jnp.bfloat16), "dp", scatter_dimension=0, tiled=True
        ).astype(jnp.float32),
        lax.psum_scatter(
            gain_part.astype(jnp.bfloat16), "dp", scatter_dimension=0, tiled=True
        ).astype(jnp.float32),
        lax.psum_scatter(
            bias_part.astype(jnp.bfloat16), "dp", scatter_dimension=0, tiled=True
        ).astype(jnp.float32),
    )
    weight_total, gain_total, bias_total = (
        lax.psum(shares[0].astype(jnp.bfloat16), "tm").astype(jnp.float32),
        lax.psum(shares[1].astype(jnp.bfloat16), "tm").astype(jnp.float32),
        lax.psum(shares[2].astype(jnp.bfloat16), "tm").astype(jnp.float32),
    )
    attended = attended.reshape(1, frames_dev, patches, attended.shape[2])
    return (attended, tokens_grad, weight_total, gain_total, bias_total)


def solution(mesh):
    placed = (
        P("dp", "tm", None, None),
        P("dp"),
        P("dp"),
        P("dp", None),
        P("dp"),
        P("dp", None),
        P("dp", None),
        P("dp", "tm", None, None),
    )
    return jax.shard_map(
        body,
        mesh=mesh,
        in_specs=placed,
        out_specs=(
            P("dp", "tm", None, None),
            P("dp", "tm", None, None),
            P("dp", None),
            P("dp"),
            P("dp"),
        ),
        check_vma=False,
    )
```

profile of v0, /device:TPU:0, one launch (start us, length us, event | category | flops | bytes accessed | tf_op | source)
XLA Modules:
  0.0 311.6 jit_solution(17849778376511438299)
XLA Ops:
  7.9 5.3 %all-to-all-start.2 = ((bf16[8,196,384]{2,0,1:T(8,128)(2,1)}), bf16[8,196,384]{2,0,1:T(8,128)(2,1)}, u32[]{:S(2)}, u32[]{:S(2)}) async-start(bf16[8,196,384]{2,0,1:T(8,128)(2,1)} %bitcast.80), calls=%async_computation.2 | async-start | bytes 2408448 | tf_op jit(solution)/shard_map/all_to_all | solution.py:94
  15.4 17.4 %all-reduce.5 = (bf16[768]{0:T(1024)(128)(2,1)S(1)}, bf16[768]{0:T(1024)(128)(2,1)S(1)}) all-reduce(bf16[768]{0:T(1024)(128)(2,1)S(1)} %dynamic-update-slice.1, bf16[768]{0:T(1024)(128)(2,1)S(1)} %dynamic-update-slice), channel_id=1, replica_groups=mesh['dp'=8,'tm'=4] {'dp'}, use_global_device_ids=true, to_apply=%add.1 | all-reduce | flops 1536 | bytes 6144
  35.8 5.2 %all-to-all-start = ((bf16[8,196,768]{2,0,1:T(8,128)(2,1)}), bf16[8,196,768]{2,0,1:T(8,128)(2,1)}, u32[]{:S(2)}, u32[]{:S(2)}) async-start(bf16[8,196,768]{2,0,1:T(8,128)(2,1)} %fusion.10), calls=%async_computation | async-start | bytes 4816896 | tf_op jit(solution)/shard_map/all_to_all | solution.py:94
  44.4 4.7 %all_to_all.51 = bf16[32,49,6,64]{3,2,0,1:T(8,128)(2,1)} reshape(bf16[4,8,49,384]{3,1,0,2:T(8,128)(2,1)} %bitcast.78) | data formatting | bytes 2408448 | tf_op jit(solution)/shard_map/all_to_all | solution.py:94
  53.1 13.9 %all-to-all-done = bf16[8,196,768]{2,0,1:T(8,128)(2,1)} async-done(((bf16[8,196,768]{2,0,1:T(8,128)(2,1)}), bf16[8,196,768]{2,0,1:T(8,128)(2,1)}, u32[]{:S(2)}, u32[]{:S(2)}) %all-to-all-start) | async-done | bytes 2408480 | tf_op jit(solution)/shard_map/all_to_all | solution.py:94
  75.0 7.3 %convolution_convert_fusion = bf16[1568,1152]{1,0:T(8,128)(2,1)} fusion(bf16[1568,768]{1,0:T(8,128)(2,1)} %reshape.297, bf16[768,1152]{1,0:T(8,128)(2,1)} %all-gather.2.cloned.1.call-done), kind=kOutput, calls=%fused_computation.2 | convolution fusion | flops 2776338432 | bytes 7790592 | tf_op jit(solution)/shard_map/dot_general | solution.py:134
  82.3 5.0 %reshape.298 = bf16[32,49,1152]{2,1,0:T(8,128)(2,1)} reshape(bf16[1568,1152]{1,0:T(8,128)(2,1)} %convolution_convert_fusion) | data formatting | bytes 7225344 | tf_op jit(solution)/shard_map/reshape | solution.py:137
  91.6 4.7 %reshape.324 = bf16[32,49,6,64]{3,2,1,0:T(8,128)(2,1)} reshape(bf16[32,49,384]{2,1,0:T(8,128)(2,1)} %get-tuple-element.16) | data formatting | bytes 2408448 | tf_op jit(solution)/shard_map/reshape | solution.py:34
  96.2 4.7 %reshape.326 = bf16[32,49,6,64]{3,2,1,0:T(8,128)(2,1)} reshape(bf16[32,49,384]{2,1,0:T(8,128)(2,1)} %get-tuple-element.15) | data formatting | bytes 2408448 | tf_op jit(solution)/shard_map/reshape | solution.py:34
  100.9 4.8 %reshape.325 = bf16[32,49,6,64]{3,2,1,0:T(8,128)(2,1)} reshape(bf16[32,49,384]{2,1,0:T(8,128)(2,1)} %get-tuple-element.14) | data formatting | bytes 2408448 | tf_op jit(solution)/shard_map/reshape | solution.py:34
  119.3 11.1 %convert_bitcast_fusion.3 = bf16[32,49,6,64]{3,0,2,1:T(8,128)(2,1)} fusion(f32[49,6,32,32]{2,3,1,0:T(8,128)} %fusion.34, bf16[32,49,6,64]{3,2,1,0:T(8,128)(2,1)} %reshape.326, f32[49,6,32,32]{2,3,1,0:T(8,128)} %copy-done.11, f32[49,6,32]{2,1,0:T(8,128)S(1)} %get-tuple-element.21), kind=kOutput, calls=%fused_computation.35 | convolution fusion | flops 41254112 | bytes 4854528 | tf_op jit(solution)/shard_map/phfg,gphd->fphd/dot_general | solution.py:78
  130.4 10.8 %convert_bitcast_fusion.2 = bf16[32,49,6,64]{3,0,2,1:T(8,128)(2,1)} fusion(f32[49,6,32,32]{2,3,1,0:T(8,128)} %fusion.34, bf16[32,49,6,64]{3,2,1,0:T(8,128)(2,1)} %reshape.325, f32[49,6,32,32]{2,3,1,0:T(8,128)} %copy-done.11, f32[49,6,32]{2,1,0:T(8,128)S(1)} %get-tuple-element.21), kind=kOutput, calls=%fused_computation.34 | convolution fusion | flops 41254112 | bytes 4854528 | tf_op jit(solution)/shard_map/phfg,fphd->gphd/dot_general | solution.py:81
  141.3 5.8 %convert_bitcast_fusion.1 = bf16[32,49,6,64]{3,0,2,1:T(8,128)(2,1)} fusion(bf16[32,49,6,64]{3,2,0,1:T(8,128)(2,1)} %broadcast_select_fusion, f32[49,6,32,32]{2,3,1,0:T(8,128)} %copy-done.11, f32[49,6,32]{2,1,0:T(8,128)S(1)} %get-tuple-element.21), kind=kOutput, calls=%fused_computation.33 | convolution fusion | flops 39739392 | bytes 3650304 | tf_op jit(solution)/shard_map/phfg,fphd->gphd/dot_general | solution.py:73
  149.8 4.9 %reshape.321 = bf16[32,49,384]{2,1,0:T(8,128)(2,1)} reshape(bf16[32,49,6,64]{3,2,1,0:T(8,128)(2,1)} %copy.141) | data formatting | bytes 2408448 | tf_op jit(solution)/shard_map/convert_element_type | solution.py:56
  163.5 5.4 %concatenate.11 = bf16[1568,384]{1,0:T(8,128)(2,1)} reshape(bf16[32,49,6,64]{3,2,1,0:T(8,128)(2,1)} %copy.124) | data formatting | bytes 2408448 | tf_op jit(solution)/shard_map/concatenate | solution.py:85
  174.2 5.2 %concatenate.12 = bf16[1568,384]{1,0:T(8,128)(2,1)} reshape(bf16[32,49,6,64]{3,2,1,0:T(8,128)(2,1)} %copy.126) | data formatting | bytes 2408448 | tf_op jit(solution)/shard_map/concatenate | solution.py:85
  183.8 5.2 %concatenate.13 = bf16[1568,384]{1,0:T(8,128)(2,1)} reshape(bf16[32,49,6,64]{3,2,1,0:T(8,128)(2,1)} %copy.128) | data formatting | bytes 2408448 | tf_op jit(solution)/shard_map/concatenate | solution.py:85
  194.0 6.9 %convolution_convert_fusion.1 = bf16[768,1152]{1,0:T(8,128)(2,1)} fusion(bf16[1568,768]{1,0:T(8,128)(2,1)S(1)} %copy-done.3, bf16[1568,1152]{1,0:T(8,128)(2,1)} %constant_dynamic-update-slice_fusion), kind=kOutput, calls=%fused_computation.28 | convolution fusion | flops 2775416832 | bytes 7790592 | tf_op jit(solution)/shard_map/dot_general | solution.py:142
  200.9 7.3 %convolution_convert_fusion.2 = bf16[1568,768]{1,0:T(8,128)(2,1)} fusion(bf16[1568,1152]{1,0:T(8,128)(2,1)} %constant_dynamic-update-slice_fusion, bf16[768,1152]{1,0:T(8,128)(2,1)} %all-gather.2.cloned.1.call-done), kind=kOutput, calls=%fused_computation.29 | convolution fusion | flops 2775736320 | bytes 7790592 | tf_op jit(solution)/shard_map/dot_general | solution.py:145
  223.2 25.3 %all-to-all-done.3 = bf16[32,49,768]{2,1,0:T(8,128)(2,1)} async-done(((bf16[32,49,768]{2,1,0:T(8,128)(2,1)}), bf16[32,49,768]{2,1,0:T(8,128)(2,1)}, u32[]{:S(2)}, u32[]{:S(2)}) %all-to-all-start.3) | async-done | bytes 2408480 | tf_op jit(solution)/shard_map/all_to_all | solution.py:98
  254.8 5.6 %multiply_reduce_fusion = (bf16[768]{0:T(1024)(128)(2,1)S(1)}, f32[8,4,49]{2,0,1:T(8,128)S(1)}, f32[8,4,49]{2,0,1:T(8,128)S(1)}) fusion(f32[8,4,49,768]{3,0,2,1:T(8,128)S(1)} %bitcast.76, bf16[4,8,49,768]{3,2,1,0:T(8,128)(2,1)} %bitcast.22, f32[8,4,49]{2,0,1:T(8,128)S(1)} %copy.136, f32[8,4,49]{2,0,1:T(8,128)S(1)} %copy.133, f32[768]{0:T(1024)S(1)} %convert_element_type.108), kind=kLoop, calls=%fused_computation.6 | loop fusion | flops 10834112 | bytes 7255040 | tf_op jit(solution)/shard_map/reduce_sum | solution.py:150
  265.1 15.4 %all-reduce.4 = (bf16[768]{0:T(1024)(128)(2,1)S(1)}, bf16[768]{0:T(1024)(128)(2,1)S(1)}) all-reduce(bf16[768]{0:T(1024)(128)(2,1)S(1)} %get-tuple-element.5, bf16[768]{0:T(1024)(128)(2,1)S(1)} %get-tuple-element.17), channel_id=3, replica_groups=mesh['dp'=8,'tm'=4] {'dp'}, use_global_device_ids=true, to_apply=%region_12.13.clone | all-reduce | flops 1536 | bytes 6144
  280.7 9.0 %all-reduce.6 = (bf16[96]{0:T(256)(128)(2,1)S(1)}, bf16[96]{0:T(256)(128)(2,1)S(1)}) all-reduce(bf16[96]{0:T(256)(128)(2,1)S(1)} %dynamic-slice.3, bf16[96]{0:T(256)(128)(2,1)S(1)} %dynamic-slice.5), channel_id=1, replica_groups=mesh['dp'=8,'tm'=4] {'tm'}, use_global_device_ids=true, to_apply=%region_13.14 | all-reduce | flops 192 | bytes 768 | tf_op jit(solution)/shard_map/psum | solution.py:172
  290.8 12.3 %all-reduce.9.cloned.1.call-done = bf16[96,1152]{1,0:T(8,128)(2,1)} async-done(((bf16[96,1152]{1,0:T(8,128)(2,1)}), bf16[96,1152]{1,0:T(8,128)(2,1)}) %all-reduce.9.cloned.1.call-update) | async-done | bytes 221200 | tf_op jit(solution)/shard_map/psum | solution.py:171
  (100 shorter events, 92.3 us)
Async XLA Ops:
  7.2 6.5 %copy-start.6 = (u32[32]{0:T(128)S(1)}, u32[32]{0:T(128)}, u32[]{:S(2)}) copy-start(u32[32]{0:T(128)} %constant.50) | copy-start | bytes 388
  7.2 6.1 %copy-start = (bf16[1,8,196,768]{3,1,2,0:T(8,128)(2,1)S(1)}, bf16[1,8,196,768]{3,1,2,0:T(8,128)(2,1)}, u32[]{:S(2)}) copy-start(bf16[1,8,196,768]{3,1,2,0:T(8,128)(2,1)} %param.8) | copy-start | bytes 7225348
  7.2 7.7 %copy-start.7 = (bf16[96]{0:T(256)(128)(2,1)S(1)}, bf16[96]{0:T(256)(128)(2,1)}, u32[]{:S(2)}) copy-start(bf16[96]{0:T(256)(128)(2,1)} %param.10) | copy-start | bytes 580
  7.2 8.0 %copy-start.8 = (bf16[96]{0:T(256)(128)(2,1)S(1)}, bf16[96]{0:T(256)(128)(2,1)}, u32[]{:S(2)}) copy-start(bf16[96]{0:T(256)(128)(2,1)} %param.9) | copy-start | bytes 580
  7.2 67.8 %all-gather.2.cloned.1.call-start = ((), (), s32[]{:S(2)}) async-start(), calls=%async_computation.5 | async-start | bytes 1990656 | tf_op jit(solution)/shard_map/all_gather | solution.py:114
  7.9 27.8 %all-to-all-start.2 = ((bf16[8,196,384]{2,0,1:T(8,128)(2,1)}), bf16[8,196,384]{2,0,1:T(8,128)(2,1)}, u32[]{:S(2)}, u32[]{:S(2)}) async-start(bf16[8,196,384]{2,0,1:T(8,128)(2,1)} %bitcast.80), calls=%async_computation.2 | async-start | bytes 2408448 | tf_op jit(solution)/shard_map/all_to_all | solution.py:94
  35.8 5.8 %copy-start.9 = (s32[1,2]{1,0:T(1,128)S(1)}, s32[1,2]{1,0:T(1,128)}, u32[]{:S(2)}) copy-start(s32[1,2]{1,0:T(1,128)} %param.13) | copy-start | bytes 28
  35.8 6.1 %copy-start.10 = (s32[1,32]{1,0:T(1,128)S(1)}, s32[1,32]{1,0:T(1,128)}, u32[]{:S(2)}) copy-start(s32[1,32]{1,0:T(1,128)} %param.14) | copy-start | bytes 388
  35.8 31.2 %all-to-all-start = ((bf16[8,196,768]{2,0,1:T(8,128)(2,1)}), bf16[8,196,768]{2,0,1:T(8,128)(2,1)}, u32[]{:S(2)}, u32[]{:S(2)}) async-start(bf16[8,196,768]{2,0,1:T(8,128)(2,1)} %fusion.10), calls=%async_computation | async-start | bytes 4816896 | tf_op jit(solution)/shard_map/all_to_all | solution.py:94
  110.0 1.9 copy-start.1
  110.0 2.9 copy-start.2
  112.9 3.7 %copy-start.11 = (f32[49,6,32,32]{2,3,1,0:T(8,128)}, f32[49,6,32,32]{2,3,1,0:T(8,128)S(1)}, u32[]{:S(2)}) copy-start(f32[49,6,32,32]{2,3,1,0:T(8,128)S(1)} %get-tuple-element.22) | copy-start | bytes 3612676
  141.3 5.8 %copy-start.5 = (bf16[32,49,6,64]{3,0,2,1:T(8,128)(2,1)S(1)}, bf16[32,49,6,64]{3,0,2,1:T(8,128)(2,1)}, u32[]{:S(2)}) copy-start(bf16[32,49,6,64]{3,0,2,1:T(8,128)(2,1)} %fusion.15) | copy-start | bytes 3612676
  154.7 57.8 %all-to-all-start.1 = ((bf16[32,49,384]{2,1,0:T(8,128)(2,1)}), bf16[32,49,384]{2,1,0:T(8,128)(2,1)}, u32[]{:S(2)}, u32[]{:S(2)}) async-start(bf16[32,49,384]{2,1,0:T(8,128)(2,1)} %reshape.321), calls=%async_computation.1 | async-start | bytes 2752512 | tf_op jit(solution)/shard_map/all_to_all | solution.py:98
  159.0 101.8 %reduce-scatter.2.cloned.1.call-start = ((), (), s32[]{:S(2)}) async-start(), calls=%async_computation.6 | async-start | bytes 1990656 | tf_op jit(solution)/shard_map/reduce_scatter | solution.py:160
  168.8 2.6 copy-start.4
  188.9 5.1 %copy-start.3 = (bf16[1568,768]{1,0:T(8,128)(2,1)S(1)}, bf16[1568,768]{1,0:T(8,128)(2,1)}, u32[]{:S(2)}) copy-start(bf16[1568,768]{1,0:T(8,128)(2,1)} %reshape.297) | copy-start | bytes 7225348
  212.5 36.0 %all-to-all-start.3 = ((bf16[32,49,768]{2,1,0:T(8,128)(2,1)}), bf16[32,49,768]{2,1,0:T(8,128)(2,1)}, u32[]{:S(2)}, u32[]{:S(2)}) async-start(bf16[32,49,768]{2,1,0:T(8,128)(2,1)} %reshape.305), calls=%async_computation.3 | async-start | bytes 5505024 | tf_op jit(solution)/shard_map/all_to_all | solution.py:98
  217.1 86.0 %all-reduce.9.cloned.1.call-start = ((), (), s32[]{:S(2)}) async-start(), calls=%async_computation.7 | async-start | bytes 442368 | tf_op jit(solution)/shard_map/psum | solution.py:171
  248.5 6.3 %slice-start = ((s8[4816896]{0:T(1024)(128)(4,1)}), s8[4194304]{0:T(1024)(128)(4,1)S(1)}, s32[]{:S(2)}) async-start(s8[4816896]{0:T(1024)(128)(4,1)} %bitcast.75), calls=%async_computation.8 | async-start | bytes 8388608
  251.1 3.6 %slice-start.1 = ((s8[4816896]{0:T(1024)(128)(4,1)}), s8[622592]{0:T(1024)(128)(4,1)S(1)}, s32[]{:S(2)}) async-start(s8[4816896]{0:T(1024)(128)(4,1)} %bitcast.75), calls=%async_computation.9 | async-start | bytes 1245184
Sparse Core Ops, SparseCore 0:
  9.7 29.2 all-gather.1
  201.0 34.4 reduce-scatter.1
  261.0 42.0 all-reduce.8
where the time goes:
time: 316 us; the launch traced here: 312 us
  local copies, waits for them, and re-layouts  94.6 us (30%)
  matrix products  60 us (19%)
  waiting for transfers between devices  52.3 us (17%)
  blocking collectives  41.9 us (13%)
  other arithmetic  27.2 us (9%)
  starting transfers between devices  19.5 us (6%)
  between operations  16.2 us (5%)
    unnamed x2, blocking collectives  32.8 us
    all_to_all x2, waiting for transfers between devices, to_frames(): lax.all_to_all(patch_rows, 'tm', split_axis=0, concat_axis=1, tiled=True)  25.3 us
    concatenate x4, local copies, waits for them, and re-layouts, attend_back(): jnp.concatenate([piece.reshape(frames, patch_rows, joined) for piece in p...  18.1 us
    reshape x3, local copies, waits for them, and re-layouts, split_heads(): projected[:, :, start:start + joined]  14.2 us
    all_to_all x2, waiting for transfers between devices, to_patches(): lax.all_to_all(widened, 'tm', split_axis=1, concat_axis=0, tiled=True)  13.9 us
    psum x1, waiting for transfers between devices, body(): lax.psum(shares[0].astype(jnp.bfloat16), 'tm').astype(jnp.float32)  12.3 us
    dot_general x1, matrix products, attend_back(): jnp.einsum('phfg,gphd->fphd', score_grad, key_rows, preferred_element_typ...  11.1 us
    all_to_all x3, local copies, waits for them, and re-layouts, to_patches(): lax.all_to_all(widened, 'tm', split_axis=1, concat_axis=0, tiled=True)  10.9 us
  transfers between devices with their start and end apart: 7, of which 3 were waited for; matrix products, arithmetic and copies ran while one was open for 31% of the time, Pallas kernels for 0%

commit v1 on v0

v1 whole, which is shorter than its diff:
```python
import functools

import jax
import jax.numpy as jnp
from jax import lax
from jax.experimental import pallas as pl
from jax.experimental.pallas import tpu as pltpu
from jax.sharding import PartitionSpec as P

HEADS = 6
BLOCK = 16
CORES = 2
EXTRA = 16

masked_value = -1e30
epsilon = 1e-05
vmem_limit = 56 * 1024 * 1024
f32 = jnp.float32
bf16 = jnp.bfloat16


def round_up(value, step):
    return -(-value // step) * step


def chunk_sizes(patches_dev, group, count):
    groups = -(-patches_dev // group)
    count = min(count, groups)
    sizes = []
    left = patches_dev
    for index in range(count - 1):
        taken = (groups // count) * group
        sizes.append((taken, taken))
        left -= taken
    sizes.append((left, round_up(left, 2)))
    return sizes


def pack_kernel(
    tm_count, patches_dev, offset, real, sent, padded, x_ref, grad_ref, *rest
):
    outs, wide = rest[:-1], rest[-1]
    frames, patches, width = x_ref.shape[1:]
    me = lax.axis_index("tm")
    lanes = wide.shape[0]
    for f in range(frames):
        for c in range(lanes):
            at = c * 128
            ref, at = (x_ref, at) if at < width else (grad_ref, at - width)
            wide[c, f * padded : f * padded + patches] = ref[0, f, :, at : at + 128].astype(f32)
            if padded > patches:
                wide[c, f * padded + patches : (f + 1) * padded] = jnp.zeros(
                    (padded - patches, 128), f32
                )
    for r in range(tm_count):
        base = (me ^ r) * patches_dev + offset

        def two(k, base=base, out=outs[r]):
            place = pl.ds(pl.multiple_of(k * 2 * frames, 2 * frames), 2 * frames)
            for c in range(lanes):
                rows = []
                for i in range(2):
                    q = 2 * k + i
                    got = wide[c, pl.ds(base + q, frames, stride=padded), :]
                    rows.append(got if real == sent else jnp.where(q < real, got, 0.0))
                both = jnp.concatenate(rows, axis=0).astype(bf16)
                out[place, c * 128 : (c + 1) * 128] = both

        pl.loop(0, sent // 2)(two)


def pack(tm_count, patches_dev, offset, real, sent, tokens, grads):
    _, frames, patches, width = tokens.shape
    joined = grads.shape[3]
    padded = round_up(max(patches, tm_count * patches_dev) + 2, 8)
    return pl.pallas_call(
        functools.partial(pack_kernel, tm_count, patches_dev, offset, real, sent, padded),
        out_shape=[jax.ShapeDtypeStruct((sent * frames, width + joined), bf16)] * tm_count,
        in_specs=[pl.BlockSpec(memory_space=pltpu.VMEM)] * 2,
        out_specs=[pl.BlockSpec(memory_space=pltpu.VMEM)] * tm_count,
        scratch_shapes=[pltpu.VMEM(((width + joined) // 128, frames * padded, 128), f32)],
        compiler_params=pltpu.CompilerParams(vmem_limit_bytes=vmem_limit),
        cost_estimate=pl.CostEstimate(flops=0, bytes_accessed=8_000_000, transcendentals=0),
    )(tokens, grads)


def unpack_kernel(tm_count, patches_dev, chunks, padded, joined, *refs):
    count = tm_count * len(chunks)
    ins = refs[:count]
    mixed_ref, grad_ref, wide = refs[count:]
    frames, patches = mixed_ref.shape[1:3]
    me = lax.axis_index("tm")

    def spread(place, values):
        for c in range(wide.shape[0]):
            wide[c, pl.ds(place, frames, stride=padded), :] = values[:, c * 128 : (c + 1) * 128]

    offset = 0
    for c, (real, sent) in enumerate(chunks):
        for r in range(tm_count):
            source = ins[c * tm_count + r]
            base = (me ^ r) * patches_dev + offset

            def two(k, base=base, source=source):
                both = source[
                    pl.ds(pl.multiple_of(k * 2 * frames, 2 * frames), 2 * frames), :
                ].astype(f32)
                for i in range(2):
                    spread(base + 2 * k + i, both[i * frames : (i + 1) * frames])

            pl.loop(0, real // 2)(two)
            if real % 2:
                k = real // 2
                both = source[k * 2 * frames : (k + 1) * 2 * frames, :].astype(f32)
                spread(base + real - 1, both[:frames])
        offset += real
    for f in range(frames):
        rows = slice(f * padded, f * padded + patches)
        for c in range(wide.shape[0]):
            at = c * 128
            ref, at = (mixed_ref, at) if at < joined else (grad_ref, at - joined)
            ref[0, f, :, at : at + 128] = wide[c, rows].astype(bf16)


def unpack(tm_count, patches_dev, chunks, frames, patches, joined, width, pieces):
    padded = round_up(max(patches, tm_count * patches_dev) + 2, 8)
    return pl.pallas_call(
        functools.partial(unpack_kernel, tm_count, patches_dev, chunks, padded, joined),
        out_shape=[
            jax.ShapeDtypeStruct((1, frames, patches, joined), bf16),
            jax.ShapeDtypeStruct((1, frames, patches, width), bf16),
        ],
        in_specs=[pl.BlockSpec(memory_space=pltpu.VMEM)] * len(pieces),
        out_specs=[pl.BlockSpec(memory_space=pltpu.VMEM)] * 2,
        scratch_shapes=[pltpu.VMEM(((width + joined) // 128, frames * padded, 128), f32)],
        compiler_params=pltpu.CompilerParams(vmem_limit_bytes=vmem_limit),
        cost_estimate=pl.CostEstimate(flops=0, bytes_accessed=12_000_000, transcendentals=0),
    )(*pieces)


def frame_facts(frame, count_ref, starts_ref, kept_ref):
    clip = jnp.zeros_like(frame)
    for b in range(1, starts_ref.shape[1]):
        clip = clip + jnp.where(frame >= b * BLOCK, starts_ref[0, b], 0)
    kept = jnp.zeros_like(frame)
    for g in range(kept_ref.shape[1]):
        kept = jnp.where(frame == g, kept_ref[0, g], kept)
    usable = (frame < count_ref[0]) & (kept == 1)
    return clip, usable


def chunk_kernel(
    tm_count,
    dp_count,
    frames,
    group,
    groups,
    first,
    last,
    count_ref,
    starts_ref,
    kept_ref,
    *rest,
):
    rest = list(rest)
    take = lambda n: [rest.pop(0) for _ in range(n)]
    pieces = take(dp_count)
    sources = take(tm_count)
    before = None if first else take(1)[0]
    outs = take(tm_count)
    sums = take(2) if last else take(1)
    (xs, weight, extra, normed, standard, proj, pgrad, back, acc, ends, allow, sems) = rest
    sent_rows = sources[0].shape[0]
    width = weight.shape[0]
    columns = weight.shape[1]
    joined = columns // 3
    tokens = groups * group * frames * tm_count
    span = group * frames
    shard = width // dp_count
    me = lax.axis_index("tm")
    dp = lax.axis_index("dp")
    z, core = dp // CORES, dp % CORES
    nz = dp_count // CORES

    started = []

    def bring(src, dst):
        copy = pltpu.make_async_copy(src, dst, sems.at[len(started)])
        copy.start()
        started.append(copy)
        return copy

    rows_in = [bring(sources[r], xs.at[r, pl.ds(0, sent_rows)]) for r in range(tm_count)]
    weights_in = []
    for side in range(CORES):
        for k in range(nz):
            owner = lax.rem(z + nz - k, nz) * CORES + (core ^ side)
            piece = pieces[side * nz + k]
            place = pl.ds(pl.multiple_of(owner * shard, shard), shard)
            weights_in.append(bring(piece.at[pl.ds(0, shard)], weight.at[place]))
            weights_in.append(
                bring(piece.at[pl.ds(shard, EXTRA)], extra.at[side * nz + k])
            )
    if not first:
        acc_in = bring(before, acc)
    if xs.shape[1] > sent_rows:
        for r in range(tm_count):
            xs[r, sent_rows:, :] = jnp.zeros((xs.shape[1] - sent_rows, columns), bf16)

    row = lax.broadcasted_iota(jnp.int32, (tm_count * frames, tokens // groups), 0)
    lane = lax.broadcasted_iota(jnp.int32, (tm_count * frames, tokens // groups), 1)
    key_frame = (me ^ (row // frames)) * frames + row % frames
    query_frame = (me ^ (lane // span)) * frames + lane % frames
    key_clip, key_usable = frame_facts(key_frame, count_ref, starts_ref, kept_ref)
    query_clip, _ = frame_facts(query_frame, count_ref, starts_ref, kept_ref)
    ok = (key_clip == query_clip) & (key_usable | (key_frame == query_frame))
    allow[...] = jnp.where(ok, 1.0, 0.0)
    token = lax.broadcasted_iota(jnp.int32, (tokens // groups, 128), 0)
    token_frame = (me ^ (token // span)) * frames + token % frames
    token_valid = token_frame < count_ref[0]

    for copy in weights_in:
        copy.wait()
    gain = functools.reduce(
        lambda a, b: a + b, [extra[i, 0:1, :width].astype(f32) for i in range(dp_count)]
    )
    bias = functools.reduce(
        lambda a, b: a + b, [extra[i, 1:2, :width].astype(f32) for i in range(dp_count)]
    )
    for copy in rows_in:
        copy.wait()

    unit = tokens // groups

    @pl.loop(0, groups)
    def _(j):
        rows = pl.ds(pl.multiple_of(j * span, span), span)
        x = jnp.concatenate([xs[r, rows, :width] for r in range(tm_count)], axis=0).astype(f32)
        centred = x - jnp.mean(x, axis=-1, keepdims=True)
        inverse = lax.rsqrt(jnp.mean(centred * centred, axis=-1, keepdims=True) + epsilon)
        std = centred * inverse
        at = pl.ds(pl.multiple_of(j * unit, unit), unit)
        standard[at, :] = std
        ends[at, :] = jnp.broadcast_to(inverse, (unit, 128))
        normed[at, :] = (std * gain + bias).astype(bf16)

    for part in range(3):
        cut = slice(part * joined, (part + 1) * joined)
        proj[:, cut] = jnp.dot(
            normed[...], weight[:, cut], preferred_element_type=f32
        ).astype(bf16)

    pairs = joined // 128
    wide = joined // HEADS
    scale = wide ** (-0.5)
    low = lax.broadcasted_iota(jnp.int32, (unit, 128), 1) < wide
    patch_lane = (lax.broadcasted_iota(jnp.int32, (1, unit), 1) // frames) % group

    def stack(block):
        zero = jnp.zeros_like(block)
        return jnp.concatenate(
            [jnp.where(low, block, zero), jnp.where(low, zero, block)], axis=0
        )

    def compact(full):
        parts = full.reshape(2, tm_count, group, frames, unit)
        got = parts[:, :, 0]
        for p in range(1, group):
            got = jnp.where(patch_lane == p, parts[:, :, p], got)
        return got.reshape(2, tm_count * frames, unit)

    def expand(small):
        small = small.reshape(2, tm_count, 1, frames, unit)
        pieces = [jnp.where(patch_lane == p, small, 0.0) for p in range(group)]
        return jnp.concatenate(pieces, axis=2).reshape(2 * unit, unit).astype(bf16)

    nt = (((1,), (1,)), ((), ()))
    tn = (((0,), (0,)), ((), ()))

    @pl.loop(0, groups)
    def _(j):
        rows = pl.ds(pl.multiple_of(j * span, span), span)
        at = pl.ds(pl.multiple_of(j * unit, unit), unit)
        allowed = allow[...] > 0.5
        for pair in range(pairs):
            col = slice(pair * 128, (pair + 1) * 128)
            q2 = proj[at, pair * 128 : (pair + 1) * 128]
            k2 = proj[at, joined + pair * 128 : joined + (pair + 1) * 128]
            v2 = proj[at, 2 * joined + pair * 128 : 2 * joined + (pair + 1) * 128]
            up = jnp.concatenate(
                [
                    xs[r, rows, width + pair * 128 : width + (pair + 1) * 128]
                    for r in range(tm_count)
                ],
                axis=0,
            )
            up = jnp.where(token_valid, up, jnp.zeros_like(up))
            kcat, vcat, qcat, ucat = stack(k2), stack(v2), stack(q2), stack(up)
            scores = compact(lax.dot_general(kcat, q2, nt, preferred_element_type=f32))
            scores = jnp.where(allowed, scores * scale, masked_value)
            shifted = jnp.exp(scores - jnp.max(scores, axis=1, keepdims=True))
            probs = shifted / jnp.sum(shifted, axis=1, keepdims=True)
            full = expand(probs)
            mixed = lax.dot_general(full, vcat, tn, preferred_element_type=f32)
            mixed = jnp.where(token_valid, mixed, 0.0).astype(bf16)
            across = jnp.concatenate([full[:unit], full[unit:]], axis=1)
            value_grad = jnp.dot(across, ucat, preferred_element_type=f32)
            wgrad = compact(lax.dot_general(vcat, up, nt, preferred_element_type=f32))
            inner = jnp.sum(wgrad * probs, axis=1, keepdims=True)
            sgrad = expand(probs * (wgrad - inner) * scale)
            query_grad = lax.dot_general(sgrad, kcat, tn, preferred_element_type=f32)
            sacross = jnp.concatenate([sgrad[:unit], sgrad[unit:]], axis=1)
            key_grad = jnp.dot(sacross, qcat, preferred_element_type=f32)
            for r in range(tm_count):
                back[r, rows, col] = mixed[r * span : (r + 1) * span]
            pgrad[at, pair * 128 : (pair + 1) * 128] = query_grad.astype(bf16)
            pgrad[at, joined + pair * 128 : joined + (pair + 1) * 128] = key_grad.astype(bf16)
            pgrad[at, 2 * joined + pair * 128 : 2 * joined + (pair + 1) * 128] = (
                value_grad.astype(bf16)
            )

    if not first:
        acc_in.wait()
    for part in range(3):
        cut = slice(part * joined, (part + 1) * joined)
        share = lax.dot_general(normed[...], pgrad[:, cut], tn, preferred_element_type=f32)
        if first:
            acc[:width, cut] = share
        else:
            acc[:width, cut] += share

    if first:
        acc[width:, :] = jnp.zeros((acc.shape[0] - width, columns), f32)

    @pl.loop(0, groups)
    def _(j):
        rows = pl.ds(pl.multiple_of(j * span, span), span)
        at = pl.ds(pl.multiple_of(j * unit, unit), unit)
        ngrad = lax.dot_general(
            pgrad[at, :], weight[...], nt, preferred_element_type=f32
        )
        ngrad = ngrad.astype(bf16).astype(f32)
        std = standard[at, :]
        product = ngrad * std
        acc[width : width + 8, :width] += jnp.sum(product.reshape(unit // 8, 8, width), axis=0)
        acc[width + 8 : width + 16, :width] += jnp.sum(
            ngrad.reshape(unit // 8, 8, width), axis=0
        )
        scaled = ngrad * gain
        grad = ends[at, 0:1] * (
            scaled
            - jnp.mean(scaled, axis=-1, keepdims=True)
            - std * jnp.mean(product * gain, axis=-1, keepdims=True)
        )
        grad = grad.astype(bf16)
        for r in range(tm_count):
            back[r, rows, joined:] = grad[r * span : (r + 1) * span]

    gone = [bring(back.at[r, pl.ds(0, sent_rows)], outs[r]) for r in range(tm_count)]
    if not last:
        gone.append(bring(acc, sums[0]))
    else:
        keep, send = sums
        extra_rows = jnp.concatenate(
            [
                jnp.sum(acc[width : width + 8, :], axis=0, keepdims=True),
                jnp.sum(acc[width + 8 : width + 16, :], axis=0, keepdims=True),
                jnp.zeros((EXTRA - 2, columns), f32),
            ],
            axis=0,
        ).astype(bf16)
        for k in range(nz):
            owner = lax.rem(z + k, nz) * CORES
            for ref, side in ((keep, core), (send, 1 - core)):
                place = pl.ds(pl.multiple_of((owner + side) * shard, shard), shard)
                ref[k, :shard, :] = acc[place, :].astype(bf16)
                ref[k, shard:, :] = extra_rows
    for copy in gone:
        copy.wait()


def chunk(tm_count, dp_count, frames, group, first, last, facts, pieces, sources, before):
    sent_rows, total = sources[0].shape
    shard, columns = pieces[0].shape[0] - EXTRA, pieces[0].shape[1]
    width = shard * dp_count
    span = group * frames
    groups = -(-sent_rows // span)
    tokens = groups * span * tm_count
    nz = dp_count // CORES
    outs = [jax.ShapeDtypeStruct((sent_rows, total), bf16)] * tm_count
    anywhere = pl.BlockSpec(memory_space=pl.ANY)
    out_specs = [anywhere] * tm_count
    if last:
        outs += [jax.ShapeDtypeStruct((nz, shard + EXTRA, columns), bf16)] * 2
        out_specs += [pl.BlockSpec(memory_space=pltpu.VMEM)] * 2
    else:
        outs += [jax.ShapeDtypeStruct((width + 16, columns), f32)]
        out_specs += [anywhere]
    args = list(facts) + list(pieces) + list(sources) + ([] if first else [before])
    scratch = [
        pltpu.VMEM((tm_count, groups * span, total), bf16),
        pltpu.VMEM((width, columns), bf16),
        pltpu.VMEM((dp_count, EXTRA, columns), bf16),
        pltpu.VMEM((tokens, width), bf16),
        pltpu.VMEM((tokens, width), f32),
        pltpu.VMEM((tokens, columns), bf16),
        pltpu.VMEM((tokens, columns), bf16),
        pltpu.VMEM((tm_count, groups * span, total), bf16),
        pltpu.VMEM((width + 16, columns), f32),
        pltpu.VMEM((tokens, 128), f32),
        pltpu.VMEM((tm_count * frames, tokens // groups), f32),
        pltpu.SemaphoreType.DMA((2 * tm_count + 2 * dp_count + 2,)),
    ]
    return pl.pallas_call(
        functools.partial(
            chunk_kernel, tm_count, dp_count, frames, group, groups, first, last
        ),
        out_shape=outs,
        in_specs=[pl.BlockSpec(memory_space=pltpu.SMEM)] * 3 + [anywhere] * (len(args) - 3),
        out_specs=out_specs,
        scratch_shapes=scratch,
        compiler_params=pltpu.CompilerParams(vmem_limit_bytes=vmem_limit),
        cost_estimate=pl.CostEstimate(
            flops=6 * tokens * width * columns, bytes_accessed=10_000_000, transcendentals=0
        ),
    )(*args)


def partner(count, r):
    return [(i, i ^ r) for i in range(count)]


def body(
    video_tokens,
    norm_gain,
    norm_bias,
    qkv_weight,
    frame_counts,
    clip_starts,
    frame_kept,
    attended_grad,
):
    tm_count, dp_count = lax.axis_size("tm"), lax.axis_size("dp")
    nz = dp_count // CORES
    _, frames, patches, width = video_tokens.shape
    joined = attended_grad.shape[3]
    shard, columns = qkv_weight.shape
    patches_dev = -(-patches // tm_count)
    group = max(2, 128 // (frames * tm_count))
    chunks = chunk_sizes(patches_dev, group, 2)
    dp = lax.axis_index("dp")

    def swap(array, r):
        return lax.ppermute(array, "tm", partner(tm_count, r))

    packed, offset = [], 0
    for real, sent in chunks:
        packed.append(
            pack(tm_count, patches_dev, offset, real, sent, video_tokens, attended_grad)
        )
        offset += real
    gathered = [
        [part if r == 0 else swap(part, r) for r, part in enumerate(blocks)]
        for blocks in packed
    ]

    lines = jnp.zeros((EXTRA, columns), bf16)
    lines = lax.dynamic_update_slice(lines, norm_gain[None], (0, dp * shard))
    lines = lax.dynamic_update_slice(lines, norm_bias[None], (1, dp * shard))
    own = jnp.concatenate([qkv_weight, lines], axis=0)
    along = [own] + [
        lax.ppermute(own, "dp", [(i, (i + CORES * k) % dp_count) for i in range(dp_count)])
        for k in range(1, nz)
    ]
    pieces = along + [lax.ppermute(a, "dp", partner(dp_count, 1)) for a in along]

    facts = (frame_counts, clip_starts, frame_kept)
    results, total = [], None
    for c, sources in enumerate(gathered):
        first, last = c == 0, c == len(chunks) - 1
        got = chunk(
            tm_count, dp_count, frames, group, first, last, facts, pieces, sources, total
        )
        results.append([part if r == 0 else swap(part, r) for r, part in enumerate(got[:tm_count])])
        total = got[tm_count]
        sent_half = got[-1]

    other = lax.ppermute(sent_half, "dp", partner(dp_count, 1))
    blocks = [
        lax.optimization_barrier(
            (total[k].astype(f32) + other[k].astype(f32)).astype(bf16)
        )
        for k in range(nz)
    ]
    summed = blocks[0].astype(f32)
    for k in range(1, nz):
        summed = summed + lax.ppermute(
            blocks[k], "dp", [(i, (i + CORES * k) % dp_count) for i in range(dp_count)]
        ).astype(f32)
    r = 1
    while r < tm_count:
        mine = lax.optimization_barrier(summed.astype(bf16))
        summed = mine.astype(f32) + swap(mine, r).astype(f32)
        r *= 2

    attended, tokens_grad = unpack(
        tm_count,
        patches_dev,
        chunks,
        frames,
        patches,
        joined,
        width,
        [part for blocks_out in results for part in blocks_out],
    )
    weight_total = summed[:shard]
    gain_total = lax.dynamic_slice(summed[shard], (dp * shard,), (shard,))
    bias_total = lax.dynamic_slice(summed[shard + 1], (dp * shard,), (shard,))
    return (attended, tokens_grad, weight_total, gain_total, bias_total)


def solution(mesh):
    placed = (
        P("dp", "tm", None, None),
        P("dp"),
        P("dp"),
        P("dp", None),
        P("dp"),
        P("dp", None),
        P("dp", None),
        P("dp", "tm", None, None),
    )
    return jax.shard_map(
        body,
        mesh=mesh,
        in_specs=placed,
        out_specs=(
            P("dp", "tm", None, None),
            P("dp", "tm", None, None),
            P("dp", None),
            P("dp"),
            P("dp"),
        ),
        check_vma=False,
    )
```

time: 316 us -> 189 us (0.60); the launches traced: 312 us -> 189 us
  local copies, waits for them, and re-layouts: 94.6 us -> 16.6 us
  Pallas kernels: 0 us -> 68.4 us
  matrix products: 60 us -> 0 us
  blocking collectives: 41.9 us -> 0 us
  other arithmetic: 27.2 us -> 2.83 us
  waiting for transfers between devices: 52.3 us -> 72.8 us
  between operations: 16.2 us -> 1.63 us
  starting transfers between devices: 19.5 us -> 26.4 us
    ppermute x0 -> x25, waiting for transfers between devices: none -> 72.8 us  [the longest x14 39.8 us: swap(): return lax.ppermute(array, 'tm', partner(tm_count, r))]
    pallas_call x0 -> x5, Pallas kernels: none -> 68.4 us  [the longest x2 52.9 us: chunk(): pl.pallas_call(functools.partial(chunk_kernel, tm_count, dp_count, frames...]
    dot_general x9 -> x0, matrix products: 60 us -> none  [the longest x1 11.1 us: attend_back(): jnp.einsum('phfg,gphd->fphd', score_grad, key_rows, preferred_element_typ...]
    all_to_all x4 -> x0, waiting for transfers between devices: 39.2 us -> none  [the longest x2 25.3 us: to_frames(): lax.all_to_all(patch_rows, 'tm', split_axis=0, concat_axis=1, tiled=True)]
    unnamed x2 -> x0, blocking collectives: 32.8 us -> none
    reshape x6 -> x0, local copies, waits for them, and re-layouts: 27.7 us -> none  [the longest x3 14.2 us: split_heads(): projected[:, :, start:start + joined]]
    ppermute x0 -> x25, starting transfers between devices: none -> 26.4 us  [the longest x14 16.2 us: swap(): return lax.ppermute(array, 'tm', partner(tm_count, r))]
    all_to_all x4 -> x0, starting transfers between devices: 19.4 us -> none  [the longest x2 10.5 us: to_patches(): lax.all_to_all(widened, 'tm', split_axis=1, concat_axis=0, tiled=True)]
  transfers between devices with their start and end apart: 7 -> 25, of which waited for: 3 -> 10; matrix products, arithmetic and copies ran while one was open for 31% -> 6% of each run, Pallas kernels for 0% -> 21%
where the time goes in v1:
time: 189 us
  waiting for transfers between devices  72.8 us (39%)
  Pallas kernels  68.4 us (36%)
  starting transfers between devices  26.4 us (14%)
  local copies, waits for them, and re-layouts  16.6 us (9%)
  other arithmetic  2.83 us (1%)
    pallas_call x2, Pallas kernels, chunk(): pl.pallas_call(functools.partial(chunk_kernel, tm_count, dp_count, frames...  52.9 us
    ppermute x14, waiting for transfers between devices, swap(): return lax.ppermute(array, 'tm', partner(tm_count, r))  39.8 us
    ppermute x3, waiting for transfers between devices, body(): lax.ppermute(blocks[k], 'dp', [(i, (i + CORES * k) % dp_count) for i in r...  21.9 us
    ppermute x14, starting transfers between devices, swap(): return lax.ppermute(array, 'tm', partner(tm_count, r))  16.2 us
    unnamed x58, local copies, waits for them, and re-layouts  13.6 us
    pallas_call x2, Pallas kernels, pack(): pl.pallas_call(functools.partial(pack_kernel, tm_count, patches_dev, offs...  9.56 us
    ppermute x3, waiting for transfers between devices, body(): lax.ppermute(own, 'dp', [(i, (i + CORES * k) % dp_count) for i in range(d...  8.21 us
    ppermute x3, starting transfers between devices, body(): lax.ppermute(own, 'dp', [(i, (i + CORES * k) % dp_count) for i in range(d...  7.01 us
  transfers between devices with their start and end apart: 25, of which 10 were waited for; matrix products, arithmetic and copies ran while one was open for 6% of the time, Pallas kernels for 21%

profile of v1, /device:TPU:0, one launch (start us, length us, event | category | flops | bytes accessed | tf_op | source)
XLA Modules:
  0.0 188.7 jit_solution(6473924824265832850)
XLA Ops:
  3.2 3.3 %collective-permute-start = (bf16[112,1152]{1,0:T(8,128)(2,1)S(1)}, bf16[112,1152]{1,0:T(8,128)(2,1)S(1)}, u32[]{:S(2)}, u32[]{:S(2)}) collective-permute-start(bf16[112,1152]{1,0:T(8,128)(2,1)S(1)} %pad_maximum_fusion.rest_0_), channel_id=1, source_target_pairs={{0,8},{4,12},{8,16},{12,20},{16,24},{20,28},{24,0},{28,4},{1,9},{5... | collective-permute-start | bytes 774152 | tf_op jit(solution)/shard_map/ppermute | solution.py:472
  6.5 2.6 %collective-permute-start.1 = (bf16[112,1152]{1,0:T(8,128)(2,1)S(1)}, bf16[112,1152]{1,0:T(8,128)(2,1)S(1)}, u32[]{:S(2)}, u32[]{:S(2)}) collective-permute-start(bf16[112,1152]{1,0:T(8,128)(2,1)S(1)} %pad_maximum_fusion.rest_0_), channel_id=1, source_target_pairs={{0,16},{4,20},{8,24},{12,28},{16,0},{20,4},{24,8},{28,12},{1,17},{... | collective-permute-start | bytes 774152 | tf_op jit(solution)/shard_map/ppermute | solution.py:472
  9.1 3.6 %copy.13.x_ref = bf16[1,8,196,768]{3,2,1,0:T(8,128)(2,1)} copy(bf16[1,8,196,768]{3,1,2,0:T(8,128)(2,1)} %param.8) | data formatting | bytes 4816896 | tf_op args[0]
  13.9 4.6 %shard_map.119 = (bf16[192,1152]{1,0:T(8,128)(2,1)}, bf16[192,1152]{1,0:T(8,128)(2,1)}, bf16[192,1152]{1,0:T(8,128)(2,1)}, bf16[192,1152]{1,0:T(8,128)(2,1)}) custom-call(bf16[1,8,196,768]{3,2,1,0:T(8,128)(2,1)} %copy.13.x_ref, bf16[1,8,196,384]{3,2,1,0:T(8,128)(2,1)} %copy.14.grad_ref), custom_call_target="tpu_custom_call" | custom-call | bytes 8000000 | tf_op jit(solution)/shard_map/pallas_call | solution.py:76
  23.1 2.8 %collective-permute-done.1.rest_2_ = bf16[112,1152]{1,0:T(8,128)(2,1)S(1)} collective-permute-done((bf16[112,1152]{1,0:T(8,128)(2,1)S(1)}, bf16[112,1152]{1,0:T(8,128)(2,1)S(1)}, u32[]{:S(2)}, u32[]{:S(2)}) %collective-permute-start.1) | collective-permute-done | bytes 258080 | tf_op jit(solution)/shard_map/ppermute | solution.py:472
  26.0 5.4 %collective-permute-done.2.rest_3_ = bf16[112,1152]{1,0:T(8,128)(2,1)S(1)} collective-permute-done((bf16[112,1152]{1,0:T(8,128)(2,1)S(1)}, bf16[112,1152]{1,0:T(8,128)(2,1)S(1)}, u32[]{:S(2)}, u32[]{:S(2)}) %collective-permute-start.2) | collective-permute-done | bytes 258080 | tf_op jit(solution)/shard_map/ppermute | solution.py:472
  31.9 5.0 %shard_map.121 = (bf16[208,1152]{1,0:T(8,128)(2,1)}, bf16[208,1152]{1,0:T(8,128)(2,1)}, bf16[208,1152]{1,0:T(8,128)(2,1)}, bf16[208,1152]{1,0:T(8,128)(2,1)}) custom-call(bf16[1,8,196,768]{3,2,1,0:T(8,128)(2,1)} %copy.13.x_ref, bf16[1,8,196,384]{3,2,1,0:T(8,128)(2,1)} %copy.14.grad_ref), custom_call_target="tpu_custom_call" | custom-call | bytes 8000000 | tf_op jit(solution)/shard_map/pallas_call | solution.py:76
  36.9 4.8 %collective-permute-done.8.rest_10_ = bf16[192,1152]{1,0:T(8,128)(2,1)S(1)} collective-permute-done((bf16[192,1152]{1,0:T(8,128)(2,1)}, bf16[192,1152]{1,0:T(8,128)(2,1)S(1)}, u32[]{:S(2)}, u32[]{:S(2)}) %collective-permute-start.8) | collective-permute-done | bytes 442400 | tf_op jit(solution)/shard_map/ppermute | solution.py:454
  42.3 1.5 collective-permute-start.14
  46.8 24.6 %shard_map.120 = (bf16[192,1152]{1,0:T(8,128)(2,1)}, bf16[192,1152]{1,0:T(8,128)(2,1)}, bf16[192,1152]{1,0:T(8,128)(2,1)}, bf16[192,1152]{1,0:T(8,128)(2,1)}, f32[784,1152]{1,0:T(8,128)}) custom-call(s32[1]{0:T(128)S(6)} %copy.21.count_ref, s32[1,2]{1,0:T(1,128)} %starts_ref.3, s32[1,32]{1,0:T(1,128)} %kept_ref.3, bf16[112,1152]{1,0:T(8,128)(2,1)} %copy-done.7, ...), custom_call_target="tpu_custom_call" | custom-call | flops 4076863488 | bytes 10000000 | tf_op jit(solution)/shard_map/pallas_call | solution.py:414
  72.5 28.2 %shard_map.122 = (bf16[208,1152]{1,0:T(8,128)(2,1)}, bf16[208,1152]{1,0:T(8,128)(2,1)}, bf16[208,1152]{1,0:T(8,128)(2,1)}, bf16[208,1152]{1,0:T(8,128)(2,1)}, bf...) custom-call(s32[1]{0:T(128)S(6)} %copy.21.count_ref, s32[1,2]{1,0:T(1,128)} %starts_ref.3, s32[1,32]{1,0:T(1,128)} %kept_ref.3, ...), custom_call_target="tpu_custom_call" | custom-call | flops 4756340736 | bytes 10000000 | tf_op jit(solution)/shard_map/pallas_call | solution.py:414
  100.9 2.8 %collective-permute-done.19 = bf16[4,112,1152]{2,1,0:T(8,128)(2,1)S(1)} collective-permute-done((bf16[4,112,1152]{2,1,0:T(8,128)(2,1)}, bf16[4,112,1152]{2,1,0:T(8,128)(2,1)S(1)}, u32[]{:S(2)}, u32[]{:S(2)}) %collective-permute-start.19) | collective-permute-done | bytes 1032224 | tf_op jit(solution)/shard_map/ppermute | solution.py:488
  103.8 1.6 fusion
  105.9 1.7 collective-permute-start.21
  108.5 5.4 %collective-permute-done.22 = bf16[112,1152]{1,0:T(8,128)(2,1)S(1)} collective-permute-done((bf16[112,1152]{1,0:T(8,128)(2,1)S(1)}, bf16[112,1152]{1,0:T(8,128)(2,1)S(1)}, u32[]{:S(2)}, u32[]{:S(2)}) %collective-permute-start.22) | collective-permute-done | bytes 258080 | tf_op jit(solution)/shard_map/ppermute | solution.py:497
  113.9 16.5 %collective-permute-done.21 = bf16[112,1152]{1,0:T(8,128)(2,1)S(1)} collective-permute-done((bf16[112,1152]{1,0:T(8,128)(2,1)S(1)}, bf16[112,1152]{1,0:T(8,128)(2,1)S(1)}, u32[]{:S(2)}, u32[]{:S(2)}) %collective-permute-start.21) | collective-permute-done | bytes 258080 | tf_op jit(solution)/shard_map/ppermute | solution.py:497
  134.7 1.6 collective-permute-start.17
  136.2 3.5 %collective-permute-done.23 = bf16[112,1152]{1,0:T(8,128)(2,1)S(1)} collective-permute-done((bf16[112,1152]{1,0:T(8,128)(2,1)S(1)}, bf16[112,1152]{1,0:T(8,128)(2,1)S(1)}, u32[]{:S(2)}, u32[]{:S(2)}) %collective-permute-start.23) | collective-permute-done | bytes 258080 | tf_op jit(solution)/shard_map/ppermute | solution.py:454
  141.3 12.4 %collective-permute-done.11.refs_2_ = bf16[192,1152]{1,0:T(8,128)(2,1)S(1)} collective-permute-done((bf16[192,1152]{1,0:T(8,128)(2,1)S(1)}, bf16[192,1152]{1,0:T(8,128)(2,1)S(1)}, u32[]{:S(2)}, u32[]{:S(2)}) %collective-permute-start.11) | collective-permute-done | bytes 442400 | tf_op jit(solution)/shard_map/ppermute | solution.py:454
  155.3 4.3 %collective-permute-done.16.refs_5_ = bf16[208,1152]{1,0:T(8,128)(2,1)S(1)} collective-permute-done((bf16[208,1152]{1,0:T(8,128)(2,1)S(1)}, bf16[208,1152]{1,0:T(8,128)(2,1)S(1)}, u32[]{:S(2)}, u32[]{:S(2)}) %collective-permute-start.16) | collective-permute-done | bytes 479264 | tf_op jit(solution)/shard_map/ppermute | solution.py:454
  159.6 14.7 %collective-permute-done.17.refs_6_ = bf16[208,1152]{1,0:T(8,128)(2,1)S(1)} collective-permute-done((bf16[208,1152]{1,0:T(8,128)(2,1)S(1)}, bf16[208,1152]{1,0:T(8,128)(2,1)S(1)}, u32[]{:S(2)}, u32[]{:S(2)}) %collective-permute-start.17) | collective-permute-done | bytes 479264 | tf_op jit(solution)/shard_map/ppermute | solution.py:454
  175.3 6.0 %shard_map.123 = (bf16[1,8,196,384]{3,2,1,0:T(8,128)(2,1)}, bf16[1,8,196,768]{3,2,1,0:T(8,128)(2,1)}) custom-call(bf16[192,1152]{1,0:T(8,128)(2,1)} %get-tuple-element.30.refs_0_, bf16[192,1152]{1,0:T(8,128)(2,1)} %copy-done.4, bf16[192,1152]{1,0:T(8,128)(2,1)} %copy-done.5, bf16[192,1152]{1,0:T(8,128)(2,1)} %copy-done.6, ...), custom_call_target="tpu_custom_call" | custom-call | bytes 12000000 | tf_op jit(solution)/shard_map/pallas_call | solution.py:127
  181.3 2.5 %copy.17 = bf16[1,8,196,384]{3,1,2,0:T(8,128)(2,1)} copy(bf16[1,8,196,384]{3,2,1,0:T(8,128)(2,1)} %get-tuple-element.47) | data formatting | bytes 2408448
  183.7 3.6 %copy.18 = bf16[1,8,196,768]{3,1,2,0:T(8,128)(2,1)} copy(bf16[1,8,196,768]{3,2,1,0:T(8,128)(2,1)} %get-tuple-element.48) | data formatting | bytes 4816896
  (100 shorter events, 24.0 us)
Async XLA Ops:
  3.2 19.4 %collective-permute-start = (bf16[112,1152]{1,0:T(8,128)(2,1)S(1)}, bf16[112,1152]{1,0:T(8,128)(2,1)S(1)}, u32[]{:S(2)}, u32[]{:S(2)}) collective-permute-start(bf16[112,1152]{1,0:T(8,128)(2,1)S(1)} %pad_maximum_fusion.rest_0_), channel_id=1, source_target_pairs={{0,8},{4,12},{8,16},{12,20},{16,24},{20,28},{24,0},{28,4},{1,9},{5... | collective-permute-start | bytes 774152 | tf_op jit(solution)/shard_map/ppermute | solution.py:472
  6.5 19.4 %collective-permute-start.1 = (bf16[112,1152]{1,0:T(8,128)(2,1)S(1)}, bf16[112,1152]{1,0:T(8,128)(2,1)S(1)}, u32[]{:S(2)}, u32[]{:S(2)}) collective-permute-start(bf16[112,1152]{1,0:T(8,128)(2,1)S(1)} %pad_maximum_fusion.rest_0_), channel_id=1, source_target_pairs={{0,16},{4,20},{8,24},{12,28},{16,0},{20,4},{24,8},{28,12},{1,17},{... | collective-permute-start | bytes 774152 | tf_op jit(solution)/shard_map/ppermute | solution.py:472
  18.5 13.4 %collective-permute-start.7 = (bf16[192,1152]{1,0:T(8,128)(2,1)}, bf16[192,1152]{1,0:T(8,128)(2,1)S(1)}, u32[]{:S(2)}, u32[]{:S(2)}) collective-permute-start(bf16[192,1152]{1,0:T(8,128)(2,1)} %get-tuple-element.27), channel_id=1, source_target_pairs={{0,1},{1,0},{2,3},{3,2},{4,5},{5,4},{6,7},{7,6},{8,9},{9,8},{10,11... | collective-permute-start | bytes 1327112 | tf_op jit(solution)/shard_map/ppermute | solution.py:454
  20.0 11.4 %collective-permute-start.2 = (bf16[112,1152]{1,0:T(8,128)(2,1)S(1)}, bf16[112,1152]{1,0:T(8,128)(2,1)S(1)}, u32[]{:S(2)}, u32[]{:S(2)}) collective-permute-start(bf16[112,1152]{1,0:T(8,128)(2,1)S(1)} %pad_maximum_fusion.rest_0_), channel_id=1, source_target_pairs={{0,24},{4,28},{8,0},{12,4},{16,8},{20,12},{24,16},{28,20},{1,25},{... | collective-permute-start | bytes 774152 | tf_op jit(solution)/shard_map/ppermute | solution.py:472
  21.1 20.7 %collective-permute-start.8 = (bf16[192,1152]{1,0:T(8,128)(2,1)}, bf16[192,1152]{1,0:T(8,128)(2,1)S(1)}, u32[]{:S(2)}, u32[]{:S(2)}) collective-permute-start(bf16[192,1152]{1,0:T(8,128)(2,1)} %get-tuple-element.28), channel_id=1, source_target_pairs={{0,2},{1,3},{2,0},{3,1},{4,6},{5,7},{6,4},{7,5},{8,10},{9,11},{10,... | collective-permute-start | bytes 1327112 | tf_op jit(solution)/shard_map/ppermute | solution.py:454
  22.6 19.7 %collective-permute-start.9 = (bf16[192,1152]{1,0:T(8,128)(2,1)}, bf16[192,1152]{1,0:T(8,128)(2,1)S(1)}, u32[]{:S(2)}, u32[]{:S(2)}) collective-permute-start(bf16[192,1152]{1,0:T(8,128)(2,1)} %get-tuple-element.29), channel_id=1, source_target_pairs={{0,3},{1,2},{2,1},{3,0},{4,7},{5,6},{6,5},{7,4},{8,11},{9,10},{10,... | collective-permute-start | bytes 1327112 | tf_op jit(solution)/shard_map/ppermute | solution.py:454
  26.0 5.4 %collective-permute-start.3 = (bf16[112,1152]{1,0:T(8,128)(2,1)S(1)}, bf16[112,1152]{1,0:T(8,128)(2,1)S(1)}, u32[]{:S(2)}, u32[]{:S(2)}) collective-permute-start(bf16[112,1152]{1,0:T(8,128)(2,1)S(1)} %pad_maximum_fusion.rest_0_), channel_id=1, source_target_pairs={{0,4},{4,0},{8,12},{12,8},{16,20},{20,16},{24,28},{28,24},{1,5},{5... | collective-permute-start | bytes 774152 | tf_op jit(solution)/shard_map/ppermute | solution.py:475
  31.3 12.5 %collective-permute-start.4 = (bf16[112,1152]{1,0:T(8,128)(2,1)S(1)}, bf16[112,1152]{1,0:T(8,128)(2,1)S(1)}, u32[]{:S(2)}, u32[]{:S(2)}) collective-permute-start(bf16[112,1152]{1,0:T(8,128)(2,1)S(1)} %collective-permute-done.rest_1_), channel_id=1, source_target_pairs={{0,4},{4,0},{8,12},{12,8},{16,20},{20,16},{24,28},{28,24},{1,5},{5... | collective-permute-start | bytes 774152 | tf_op jit(solution)/shard_map/ppermute | solution.py:475
  31.4 14.6 %collective-permute-start.5 = (bf16[112,1152]{1,0:T(8,128)(2,1)S(1)}, bf16[112,1152]{1,0:T(8,128)(2,1)S(1)}, u32[]{:S(2)}, u32[]{:S(2)}) collective-permute-start(bf16[112,1152]{1,0:T(8,128)(2,1)S(1)} %collective-permute-done.1.rest_2_), channel_id=1, source_target_pairs={{0,4},{4,0},{8,12},{12,8},{16,20},{20,16},{24,28},{28,24},{1,5},{5... | collective-permute-start | bytes 774152 | tf_op jit(solution)/shard_map/ppermute | solution.py:475
  31.9 14.1 %collective-permute-start.6 = (bf16[112,1152]{1,0:T(8,128)(2,1)S(1)}, bf16[112,1152]{1,0:T(8,128)(2,1)S(1)}, u32[]{:S(2)}, u32[]{:S(2)}) collective-permute-start(bf16[112,1152]{1,0:T(8,128)(2,1)S(1)} %collective-permute-done.2.rest_3_), channel_id=1, source_target_pairs={{0,4},{4,0},{8,12},{12,8},{16,20},{20,16},{24,28},{28,24},{1,5},{5... | collective-permute-start | bytes 774152 | tf_op jit(solution)/shard_map/ppermute | solution.py:475
  41.8 29.7 %collective-permute-start.13 = (bf16[208,1152]{1,0:T(8,128)(2,1)}, bf16[208,1152]{1,0:T(8,128)(2,1)S(1)}, u32[]{:S(2)}, u32[]{:S(2)}) collective-permute-start(bf16[208,1152]{1,0:T(8,128)(2,1)} %get-tuple-element.35), channel_id=1, source_target_pairs={{0,1},{1,0},{2,3},{3,2},{4,5},{5,4},{6,7},{7,6},{8,9},{9,8},{10,11... | collective-permute-start | bytes 1437704 | tf_op jit(solution)/shard_map/ppermute | solution.py:454
  42.3 29.1 %collective-permute-start.14 = (bf16[208,1152]{1,0:T(8,128)(2,1)}, bf16[208,1152]{1,0:T(8,128)(2,1)S(1)}, u32[]{:S(2)}, u32[]{:S(2)}) collective-permute-start(bf16[208,1152]{1,0:T(8,128)(2,1)} %get-tuple-element.36), channel_id=1, source_target_pairs={{0,2},{1,3},{2,0},{3,1},{4,6},{5,7},{6,4},{7,5},{8,10},{9,11},{10,... | collective-permute-start | bytes 1437704 | tf_op jit(solution)/shard_map/ppermute | solution.py:454
  43.9 27.6 %collective-permute-start.15 = (bf16[208,1152]{1,0:T(8,128)(2,1)}, bf16[208,1152]{1,0:T(8,128)(2,1)S(1)}, u32[]{:S(2)}, u32[]{:S(2)}) collective-permute-start(bf16[208,1152]{1,0:T(8,128)(2,1)} %get-tuple-element.37), channel_id=1, source_target_pairs={{0,3},{1,2},{2,1},{3,0},{4,7},{5,6},{6,5},{7,4},{8,11},{9,10},{10,... | collective-permute-start | bytes 1437704 | tf_op jit(solution)/shard_map/ppermute | solution.py:454
  105.4 8.5 %collective-permute-start.22 = (bf16[112,1152]{1,0:T(8,128)(2,1)S(1)}, bf16[112,1152]{1,0:T(8,128)(2,1)S(1)}, u32[]{:S(2)}, u32[]{:S(2)}) collective-permute-start(bf16[112,1152]{1,0:T(8,128)(2,1)S(1)} %get-tuple-element.53), channel_id=1, source_target_pairs={{0,24},{4,28},{8,0},{12,4},{16,8},{20,12},{24,16},{28,20},{1,25},{... | collective-permute-start | bytes 774152 | tf_op jit(solution)/shard_map/ppermute | solution.py:497
  105.9 24.5 %collective-permute-start.21 = (bf16[112,1152]{1,0:T(8,128)(2,1)S(1)}, bf16[112,1152]{1,0:T(8,128)(2,1)S(1)}, u32[]{:S(2)}, u32[]{:S(2)}) collective-permute-start(bf16[112,1152]{1,0:T(8,128)(2,1)S(1)} %get-tuple-element.54), channel_id=1, source_target_pairs={{0,16},{4,20},{8,24},{12,28},{16,0},{20,4},{24,8},{28,12},{1,17},{... | collective-permute-start | bytes 774152 | tf_op jit(solution)/shard_map/ppermute | solution.py:497
  107.6 22.8 %collective-permute-start.20 = (bf16[112,1152]{1,0:T(8,128)(2,1)S(1)}, bf16[112,1152]{1,0:T(8,128)(2,1)S(1)}, u32[]{:S(2)}, u32[]{:S(2)}) collective-permute-start(bf16[112,1152]{1,0:T(8,128)(2,1)S(1)} %get-tuple-element.55), channel_id=1, source_target_pairs={{0,8},{4,12},{8,16},{12,20},{16,24},{20,28},{24,0},{28,4},{1,9},{5... | collective-permute-start | bytes 774152 | tf_op jit(solution)/shard_map/ppermute | solution.py:497
  107.9 26.7 %collective-permute-start.10 = (bf16[192,1152]{1,0:T(8,128)(2,1)S(1)}, bf16[192,1152]{1,0:T(8,128)(2,1)S(1)}, u32[]{:S(2)}, u32[]{:S(2)}) collective-permute-start(bf16[192,1152]{1,0:T(8,128)(2,1)S(1)} %copy-done.16), channel_id=1, source_target_pairs={{0,1},{1,0},{2,3},{3,2},{4,5},{5,4},{6,7},{7,6},{8,9},{9,8},{10,11... | collective-permute-start | bytes 1327112 | tf_op jit(solution)/shard_map/ppermute | solution.py:454
  130.6 9.2 %collective-permute-start.23 = (bf16[112,1152]{1,0:T(8,128)(2,1)S(1)}, bf16[112,1152]{1,0:T(8,128)(2,1)S(1)}, u32[]{:S(2)}, u32[]{:S(2)}) collective-permute-start(bf16[112,1152]{1,0:T(8,128)(2,1)S(1)} %add_convert_fusion.1), channel_id=1, source_target_pairs={{0,1},{1,0},{2,3},{3,2},{4,5},{5,4},{6,7},{7,6},{8,9},{9,8},{10,11... | collective-permute-start | bytes 774152 | tf_op jit(solution)/shard_map/ppermute | solution.py:454
  131.2 22.6 %collective-permute-start.11 = (bf16[192,1152]{1,0:T(8,128)(2,1)S(1)}, bf16[192,1152]{1,0:T(8,128)(2,1)S(1)}, u32[]{:S(2)}, u32[]{:S(2)}) collective-permute-start(bf16[192,1152]{1,0:T(8,128)(2,1)S(1)} %copy-done.15), channel_id=1, source_target_pairs={{0,2},{1,3},{2,0},{3,1},{4,6},{5,7},{6,4},{7,5},{8,10},{9,11},{10,... | collective-permute-start | bytes 1327112 | tf_op jit(solution)/shard_map/ppermute | solution.py:454
  132.7 22.6 %collective-permute-start.12 = (bf16[192,1152]{1,0:T(8,128)(2,1)S(1)}, bf16[192,1152]{1,0:T(8,128)(2,1)S(1)}, u32[]{:S(2)}, u32[]{:S(2)}) collective-permute-start(bf16[192,1152]{1,0:T(8,128)(2,1)S(1)} %copy-done.14), channel_id=1, source_target_pairs={{0,3},{1,2},{2,1},{3,0},{4,7},{5,6},{6,5},{7,4},{8,11},{9,10},{10,... | collective-permute-start | bytes 1327112 | tf_op jit(solution)/shard_map/ppermute | solution.py:454
  134.1 25.5 %collective-permute-start.16 = (bf16[208,1152]{1,0:T(8,128)(2,1)S(1)}, bf16[208,1152]{1,0:T(8,128)(2,1)S(1)}, u32[]{:S(2)}, u32[]{:S(2)}) collective-permute-start(bf16[208,1152]{1,0:T(8,128)(2,1)S(1)} %copy-done.10), channel_id=1, source_target_pairs={{0,1},{1,0},{2,3},{3,2},{4,5},{5,4},{6,7},{7,6},{8,9},{9,8},{10,11... | collective-permute-start | bytes 1437704 | tf_op jit(solution)/shard_map/ppermute | solution.py:454
  134.7 39.6 %collective-permute-start.17 = (bf16[208,1152]{1,0:T(8,128)(2,1)S(1)}, bf16[208,1152]{1,0:T(8,128)(2,1)S(1)}, u32[]{:S(2)}, u32[]{:S(2)}) collective-permute-start(bf16[208,1152]{1,0:T(8,128)(2,1)S(1)} %copy-done.9), channel_id=1, source_target_pairs={{0,2},{1,3},{2,0},{3,1},{4,6},{5,7},{6,4},{7,5},{8,10},{9,11},{10,... | collective-permute-start | bytes 1437704 | tf_op jit(solution)/shard_map/ppermute | solution.py:454
  139.8 34.5 %collective-permute-start.18 = (bf16[208,1152]{1,0:T(8,128)(2,1)S(1)}, bf16[208,1152]{1,0:T(8,128)(2,1)S(1)}, u32[]{:S(2)}, u32[]{:S(2)}) collective-permute-start(bf16[208,1152]{1,0:T(8,128)(2,1)S(1)} %copy-done.8), channel_id=1, source_target_pairs={{0,3},{1,2},{2,1},{3,0},{4,7},{5,6},{6,5},{7,4},{8,11},{9,10},{10,... | collective-permute-start | bytes 1437704 | tf_op jit(solution)/shard_map/ppermute | solution.py:454
  153.8 33.5 %collective-permute-start.24 = (bf16[112,1152]{1,0:T(8,128)(2,1)S(1)}, bf16[112,1152]{1,0:T(8,128)(2,1)S(1)}, u32[]{:S(2)}, u32[]{:S(2)}) collective-permute-start(bf16[112,1152]{1,0:T(8,128)(2,1)S(1)} %add_convert_fusion), channel_id=1, source_target_pairs={{0,2},{1,3},{2,0},{3,1},{4,6},{5,7},{6,4},{7,5},{8,10},{9,11},{10,... | collective-permute-start | bytes 774152 | tf_op jit(solution)/shard_map/ppermute | solution.py:454
  (28 other events, 407.6 us)

commit v2 on v1

v2 whole, which is shorter than its diff:
```python
import functools

import jax
import jax.numpy as jnp
from jax import lax
from jax.experimental import pallas as pl
from jax.experimental.pallas import tpu as pltpu
from jax.sharding import PartitionSpec as P

HEADS = 6
BLOCK = 16
CORES = 2
EXTRA = 16

masked_value = -1e30
epsilon = 1e-05
vmem_limit = 56 * 1024 * 1024
f32 = jnp.float32
bf16 = jnp.bfloat16


def round_up(value, step):
    return -(-value // step) * step


def chunk_sizes(patches_dev, group, count):
    groups = -(-patches_dev // group)
    count = min(count, groups)
    sizes = []
    left = patches_dev
    for index in range(count - 1):
        taken = (groups // count) * group
        sizes.append(taken)
        left -= taken
    sizes.append(left)
    return sizes


anywhere = pl.BlockSpec(memory_space=pl.ANY)


def run_all(pairs, sems):
    copies = [pltpu.make_async_copy(a, b, sems.at[i]) for i, (a, b) in enumerate(pairs)]
    for copy in copies:
        copy.start()
    return copies


def pack_kernel(tm_count, patches_dev, offset, size, x_ref, grad_ref, *rest):
    outs, sems = rest[:-1], rest[-1]
    width = x_ref.shape[2]
    me = lax.axis_index("tm")
    pairs = []
    for r in range(1, tm_count):
        place = pl.ds((me ^ r) * patches_dev + offset, size)
        pairs.append((x_ref.at[place], outs[r - 1].at[:, :, pl.ds(0, width)]))
        pairs.append(
            (grad_ref.at[place], outs[r - 1].at[:, :, pl.ds(width, grad_ref.shape[2])])
        )
    for copy in run_all(pairs, sems):
        copy.wait()


def pack(tm_count, patches_dev, offset, size, tokens, grads):
    _, frames, width = tokens.shape
    total = width + grads.shape[2]
    return pl.pallas_call(
        functools.partial(pack_kernel, tm_count, patches_dev, offset, size),
        out_shape=[jax.ShapeDtypeStruct((size, frames, total), bf16)] * (tm_count - 1),
        in_specs=[anywhere] * 2,
        out_specs=[pl.BlockSpec(memory_space=pltpu.VMEM)] * (tm_count - 1),
        scratch_shapes=[pltpu.SemaphoreType.DMA((2 * tm_count,))],
        compiler_params=pltpu.CompilerParams(vmem_limit_bytes=vmem_limit),
    )(tokens, grads)


def unpack_kernel(tm_count, patches_dev, offset, size, *refs):
    ins = refs[2 : tm_count + 1]
    mixed_ref, grad_ref, held, sems, out_sems = refs[tm_count + 1 :]
    joined, width = mixed_ref.shape[2], grad_ref.shape[2]
    me = lax.axis_index("tm")
    arriving = run_all([(ins[r - 1], held.at[r - 1]) for r in range(1, tm_count)], sems)
    leaving = []
    for r in range(1, tm_count):
        place = pl.ds((me ^ r) * patches_dev + offset, size)
        arriving[r - 1].wait()
        for at, ref in ((0, mixed_ref), (joined, grad_ref)):
            copy = pltpu.make_async_copy(
                held.at[r - 1, :, :, pl.ds(at, ref.shape[2])],
                ref.at[place],
                out_sems.at[len(leaving)],
            )
            copy.start()
            leaving.append(copy)
    for copy in leaving:
        copy.wait()


def unpack(tm_count, patches_dev, offset, size, mixed, grads, blocks):
    return pl.pallas_call(
        functools.partial(unpack_kernel, tm_count, patches_dev, offset, size),
        out_shape=[
            jax.ShapeDtypeStruct(mixed.shape, bf16),
            jax.ShapeDtypeStruct(grads.shape, bf16),
        ],
        in_specs=[anywhere] * (tm_count + 1),
        out_specs=[anywhere] * 2,
        input_output_aliases={0: 0, 1: 1},
        scratch_shapes=[
            pltpu.VMEM((tm_count - 1,) + blocks[0].shape, bf16),
            pltpu.SemaphoreType.DMA((tm_count,)),
            pltpu.SemaphoreType.DMA((2 * tm_count,)),
        ],
        compiler_params=pltpu.CompilerParams(vmem_limit_bytes=vmem_limit),
    )(mixed, grads, *blocks)


def frame_facts(frame, count_ref, starts_ref, kept_ref):
    clip = jnp.zeros_like(frame)
    for b in range(1, starts_ref.shape[1]):
        clip = clip + jnp.where(frame >= b * BLOCK, starts_ref[0, b], 0)
    kept = jnp.zeros_like(frame)
    for g in range(kept_ref.shape[1]):
        kept = jnp.where(frame == g, kept_ref[0, g], kept)
    usable = (frame < count_ref[0]) & (kept == 1)
    return clip, usable


def chunk_kernel(
    tm_count,
    dp_count,
    frames,
    group,
    groups,
    patches_dev,
    offset,
    first,
    last,
    count_ref,
    starts_ref,
    kept_ref,
    *rest,
):
    rest = list(rest)
    take = lambda n: [rest.pop(0) for _ in range(n)]
    pieces = take(dp_count)
    x_ref, grad_ref = take(2)
    sources = take(tm_count - 1)
    if not first:
        before = take(1)[0]
        take(2)
    outs = take(tm_count - 1)
    mixed_ref, tokens_ref = take(2)
    sums = take(2) if last else take(1)
    (xs, weight, extra, normed, standard, proj, pgrad, back, acc, ends, allow, sems) = rest
    size = sources[0].shape[0]
    width = weight.shape[0]
    columns = weight.shape[1]
    joined = columns // 3
    tokens = groups * group * frames * tm_count
    span = group * frames
    shard = width // dp_count
    me = lax.axis_index("tm")
    dp = lax.axis_index("dp")
    z, core = dp // CORES, dp % CORES
    nz = dp_count // CORES

    started = []

    def bring(src, dst):
        copy = pltpu.make_async_copy(src, dst, sems.at[len(started)])
        copy.start()
        started.append(copy)
        return copy

    mine = pl.ds(me * patches_dev + offset, size)
    kept = pl.ds(0, size)
    rows_in = [
        bring(x_ref.at[mine], xs.at[0, kept, :, pl.ds(0, width)]),
        bring(grad_ref.at[mine], xs.at[0, kept, :, pl.ds(width, joined)]),
    ]
    rows_in += [bring(sources[r - 1], xs.at[r, kept]) for r in range(1, tm_count)]
    weights_in = []
    for side in range(CORES):
        for k in range(nz):
            owner = lax.rem(z + nz - k, nz) * CORES + (core ^ side)
            piece = pieces[side * nz + k]
            place = pl.ds(pl.multiple_of(owner * shard, shard), shard)
            weights_in.append(bring(piece.at[pl.ds(0, shard)], weight.at[place]))
            weights_in.append(
                bring(piece.at[pl.ds(shard, EXTRA)], extra.at[side * nz + k])
            )
    if not first:
        acc_in = bring(before, acc)
    if xs.shape[1] > size:
        for r in range(tm_count):
            xs[r, size:] = jnp.zeros((xs.shape[1] - size,) + xs.shape[2:], bf16)

    row = lax.broadcasted_iota(jnp.int32, (tm_count * frames, tokens // groups), 0)
    lane = lax.broadcasted_iota(jnp.int32, (tm_count * frames, tokens // groups), 1)
    key_frame = (me ^ (row // frames)) * frames + row % frames
    query_frame = (me ^ (lane // span)) * frames + lane % frames
    key_clip, key_usable = frame_facts(key_frame, count_ref, starts_ref, kept_ref)
    query_clip, _ = frame_facts(query_frame, count_ref, starts_ref, kept_ref)
    ok = (key_clip == query_clip) & (key_usable | (key_frame == query_frame))
    allow[...] = jnp.where(ok, 1.0, 0.0)
    token = lax.broadcasted_iota(jnp.int32, (tokens // groups, 128), 0)
    token_frame = (me ^ (token // span)) * frames + token % frames
    token_valid = token_frame < count_ref[0]

    for copy in weights_in:
        copy.wait()
    gain = functools.reduce(
        lambda a, b: a + b, [extra[i, 0:1, :width].astype(f32) for i in range(dp_count)]
    )
    bias = functools.reduce(
        lambda a, b: a + b, [extra[i, 1:2, :width].astype(f32) for i in range(dp_count)]
    )
    for copy in rows_in:
        copy.wait()

    unit = tokens // groups

    def token_rows(j, cut):
        rows = pl.ds(j * group, group)
        return jnp.concatenate(
            [xs[r, rows, :, cut].astype(f32).reshape(span, -1) for r in range(tm_count)], axis=0
        )

    def put_rows(j, cut, values):
        rows = pl.ds(j * group, group)
        for r in range(tm_count):
            block = values[r * span : (r + 1) * span].reshape(group, frames, -1)
            back[r, rows, :, cut] = block.astype(bf16)

    @pl.loop(0, groups)
    def _(j):
        x = token_rows(j, slice(0, width))
        centred = x - jnp.mean(x, axis=-1, keepdims=True)
        inverse = lax.rsqrt(jnp.mean(centred * centred, axis=-1, keepdims=True) + epsilon)
        std = centred * inverse
        at = pl.ds(pl.multiple_of(j * unit, unit), unit)
        standard[at, :] = std
        ends[at, :] = jnp.broadcast_to(inverse, (unit, 128))
        normed[at, :] = (std * gain + bias).astype(bf16)

    for part in range(3):
        cut = slice(part * joined, (part + 1) * joined)
        proj[:, cut] = jnp.dot(
            normed[...], weight[:, cut], preferred_element_type=f32
        ).astype(bf16)

    pairs = joined // 128
    wide = joined // HEADS
    scale = wide ** (-0.5)
    low = lax.broadcasted_iota(jnp.int32, (unit, 128), 1) < wide
    patch_lane = (lax.broadcasted_iota(jnp.int32, (1, unit), 1) // frames) % group

    def stack(block):
        zero = jnp.zeros_like(block)
        return jnp.concatenate(
            [jnp.where(low, block, zero), jnp.where(low, zero, block)], axis=0
        )

    def compact(full):
        parts = full.reshape(2, tm_count, group, frames, unit)
        got = parts[:, :, 0]
        for p in range(1, group):
            got = jnp.where(patch_lane == p, parts[:, :, p], got)
        return got.reshape(2, tm_count * frames, unit)

    def expand(small):
        small = small.reshape(2, tm_count, 1, frames, unit)
        pieces = [jnp.where(patch_lane == p, small, 0.0) for p in range(group)]
        return jnp.concatenate(pieces, axis=2).reshape(2 * unit, unit).astype(bf16)

    nt = (((1,), (1,)), ((), ()))
    tn = (((0,), (0,)), ((), ()))

    @pl.loop(0, groups)
    def _(j):
        at = pl.ds(pl.multiple_of(j * unit, unit), unit)
        allowed = allow[...] > 0.5
        for pair in range(pairs):
            col = slice(pair * 128, (pair + 1) * 128)
            q2 = proj[at, pair * 128 : (pair + 1) * 128]
            k2 = proj[at, joined + pair * 128 : joined + (pair + 1) * 128]
            v2 = proj[at, 2 * joined + pair * 128 : 2 * joined + (pair + 1) * 128]
            up = token_rows(j, slice(width + pair * 128, width + (pair + 1) * 128))
            up = jnp.where(token_valid, up, 0.0).astype(bf16)
            kcat, vcat, qcat, ucat = stack(k2), stack(v2), stack(q2), stack(up)
            scores = compact(lax.dot_general(kcat, q2, nt, preferred_element_type=f32))
            scores = jnp.where(allowed, scores * scale, masked_value)
            shifted = jnp.exp(scores - jnp.max(scores, axis=1, keepdims=True))
            probs = shifted / jnp.sum(shifted, axis=1, keepdims=True)
            full = expand(probs)
            mixed = lax.dot_general(full, vcat, tn, preferred_element_type=f32)
            put_rows(j, col, jnp.where(token_valid, mixed, 0.0))
            across = jnp.concatenate([full[:unit], full[unit:]], axis=1)
            value_grad = jnp.dot(across, ucat, preferred_element_type=f32)
            wgrad = compact(lax.dot_general(vcat, up, nt, preferred_element_type=f32))
            inner = jnp.sum(wgrad * probs, axis=1, keepdims=True)
            sgrad = expand(probs * (wgrad - inner) * scale)
            query_grad = lax.dot_general(sgrad, kcat, tn, preferred_element_type=f32)
            sacross = jnp.concatenate([sgrad[:unit], sgrad[unit:]], axis=1)
            key_grad = jnp.dot(sacross, qcat, preferred_element_type=f32)
            pgrad[at, pair * 128 : (pair + 1) * 128] = query_grad.astype(bf16)
            pgrad[at, joined + pair * 128 : joined + (pair + 1) * 128] = key_grad.astype(bf16)
            pgrad[at, 2 * joined + pair * 128 : 2 * joined + (pair + 1) * 128] = (
                value_grad.astype(bf16)
            )

    if not first:
        acc_in.wait()
    for part in range(3):
        cut = slice(part * joined, (part + 1) * joined)
        share = lax.dot_general(normed[...], pgrad[:, cut], tn, preferred_element_type=f32)
        if first:
            acc[:width, cut] = share
        else:
            acc[:width, cut] += share

    if first:
        acc[width:, :] = jnp.zeros((acc.shape[0] - width, columns), f32)

    @pl.loop(0, groups)
    def _(j):
        at = pl.ds(pl.multiple_of(j * unit, unit), unit)
        ngrad = lax.dot_general(
            pgrad[at, :], weight[...], nt, preferred_element_type=f32
        )
        ngrad = ngrad.astype(bf16).astype(f32)
        std = standard[at, :]
        product = ngrad * std
        acc[width : width + 8, :width] += jnp.sum(product.reshape(unit // 8, 8, width), axis=0)
        acc[width + 8 : width + 16, :width] += jnp.sum(
            ngrad.reshape(unit // 8, 8, width), axis=0
        )
        scaled = ngrad * gain
        grad = ends[at, 0:1] * (
            scaled
            - jnp.mean(scaled, axis=-1, keepdims=True)
            - std * jnp.mean(product * gain, axis=-1, keepdims=True)
        )
        put_rows(j, slice(joined, columns), grad)

    gone = [bring(back.at[r, kept], outs[r - 1]) for r in range(1, tm_count)]
    gone.append(bring(back.at[0, kept, :, pl.ds(0, joined)], mixed_ref.at[mine]))
    gone.append(bring(back.at[0, kept, :, pl.ds(joined, width)], tokens_ref.at[mine]))
    if not last:
        gone.append(bring(acc, sums[0]))
    else:
        keep, send = sums
        extra_rows = jnp.concatenate(
            [
                jnp.sum(acc[width : width + 8, :], axis=0, keepdims=True),
                jnp.sum(acc[width + 8 : width + 16, :], axis=0, keepdims=True),
                jnp.zeros((EXTRA - 2, columns), f32),
            ],
            axis=0,
        ).astype(bf16)
        for k in range(nz):
            owner = lax.rem(z + k, nz) * CORES
            for ref, side in ((keep, core), (send, 1 - core)):
                place = pl.ds(pl.multiple_of((owner + side) * shard, shard), shard)
                ref[k, :shard, :] = acc[place, :].astype(bf16)
                ref[k, shard:, :] = extra_rows
    for copy in gone:
        copy.wait()


def chunk(
    tm_count, dp_count, group, patches_dev, offset, first, last, facts, pieces, sources, before
):
    tokens_in, grads_in, blocks = sources
    size, frames, total = blocks[0].shape
    shard, columns = pieces[0].shape[0] - EXTRA, pieces[0].shape[1]
    width = shard * dp_count
    groups = -(-size // group)
    tokens = groups * group * frames * tm_count
    nz = dp_count // CORES
    outs = [jax.ShapeDtypeStruct((size, frames, total), bf16)] * (tm_count - 1)
    outs += [
        jax.ShapeDtypeStruct(grads_in.shape, bf16),
        jax.ShapeDtypeStruct(tokens_in.shape, bf16),
    ]
    out_specs = [anywhere] * len(outs)
    if last:
        outs += [jax.ShapeDtypeStruct((nz, shard + EXTRA, columns), bf16)] * 2
        out_specs += [pl.BlockSpec(memory_space=pltpu.VMEM)] * 2
    else:
        outs += [jax.ShapeDtypeStruct((width + 16, columns), f32)]
        out_specs += [anywhere]
    args = list(facts) + list(pieces) + [tokens_in, grads_in] + list(blocks)
    aliases = {}
    if not first:
        args += list(before)
        aliases = {len(args) - 2: tm_count - 1, len(args) - 1: tm_count}
    rows = (tm_count, groups * group, frames, total)
    scratch = [
        pltpu.VMEM(rows, bf16),
        pltpu.VMEM((width, columns), bf16),
        pltpu.VMEM((dp_count, EXTRA, columns), bf16),
        pltpu.VMEM((tokens, width), bf16),
        pltpu.VMEM((tokens, width), f32),
        pltpu.VMEM((tokens, columns), bf16),
        pltpu.VMEM((tokens, columns), bf16),
        pltpu.VMEM(rows, bf16),
        pltpu.VMEM((width + 16, columns), f32),
        pltpu.VMEM((tokens, 128), f32),
        pltpu.VMEM((tm_count * frames, tokens // groups), f32),
        pltpu.SemaphoreType.DMA((2 * tm_count + 2 * dp_count + 8,)),
    ]
    return pl.pallas_call(
        functools.partial(
            chunk_kernel,
            tm_count,
            dp_count,
            frames,
            group,
            groups,
            patches_dev,
            offset,
            first,
            last,
        ),
        out_shape=outs,
        in_specs=[pl.BlockSpec(memory_space=pltpu.SMEM)] * 3 + [anywhere] * (len(args) - 3),
        out_specs=out_specs,
        scratch_shapes=scratch,
        input_output_aliases=aliases,
        compiler_params=pltpu.CompilerParams(vmem_limit_bytes=vmem_limit),
    )(*args)


def partner(count, r):
    return [(i, i ^ r) for i in range(count)]


def body(
    video_tokens,
    norm_gain,
    norm_bias,
    qkv_weight,
    frame_counts,
    clip_starts,
    frame_kept,
    attended_grad,
):
    tm_count, dp_count = lax.axis_size("tm"), lax.axis_size("dp")
    nz = dp_count // CORES
    _, frames, patches, width = video_tokens.shape
    joined = attended_grad.shape[3]
    shard, columns = qkv_weight.shape
    patches_dev = -(-patches // tm_count)
    group = max(2, 128 // (frames * tm_count))
    chunks = chunk_sizes(patches_dev, group, 2)
    dp = lax.axis_index("dp")

    def swap(array, r):
        return lax.ppermute(array, "tm", partner(tm_count, r))

    spare = ((0, tm_count * patches_dev - patches), (0, 0), (0, 0))
    tokens = jnp.pad(video_tokens[0].transpose(1, 0, 2), spare)
    upstream = jnp.pad(attended_grad[0].transpose(1, 0, 2), spare)
    offsets = [sum(chunks[:c]) for c in range(len(chunks))]
    gathered = []
    for offset, size in zip(offsets, chunks):
        blocks = pack(tm_count, patches_dev, offset, size, tokens, upstream)
        gathered.append([swap(part, r + 1) for r, part in enumerate(blocks)])

    lines = jnp.zeros((EXTRA, columns), bf16)
    lines = lax.dynamic_update_slice(lines, norm_gain[None], (0, dp * shard))
    lines = lax.dynamic_update_slice(lines, norm_bias[None], (1, dp * shard))
    own = jnp.concatenate([qkv_weight, lines], axis=0)
    along = [own] + [
        lax.ppermute(own, "dp", [(i, (i + CORES * k) % dp_count) for i in range(dp_count)])
        for k in range(1, nz)
    ]
    pieces = along + [lax.ppermute(a, "dp", partner(dp_count, 1)) for a in along]

    facts = (frame_counts, clip_starts, frame_kept)
    results, before = [], None
    for c, blocks in enumerate(gathered):
        first, last = c == 0, c == len(chunks) - 1
        got = chunk(
            tm_count,
            dp_count,
            group,
            patches_dev,
            offsets[c],
            first,
            last,
            facts,
            pieces,
            (tokens, upstream, blocks),
            before,
        )
        results.append([swap(part, r + 1) for r, part in enumerate(got[: tm_count - 1])])
        mixed, grads = got[tm_count - 1 : tm_count + 1]
        before = (got[tm_count + 1], mixed, grads)
    total, sent_half = got[-2:]

    other = lax.ppermute(sent_half, "dp", partner(dp_count, 1))
    blocks = [
        lax.optimization_barrier(
            (total[k].astype(f32) + other[k].astype(f32)).astype(bf16)
        )
        for k in range(nz)
    ]
    summed = blocks[0].astype(f32)
    for k in range(1, nz):
        summed = summed + lax.ppermute(
            blocks[k], "dp", [(i, (i + CORES * k) % dp_count) for i in range(dp_count)]
        ).astype(f32)
    r = 1
    while r < tm_count:
        mine = lax.optimization_barrier(summed.astype(bf16))
        summed = mine.astype(f32) + swap(mine, r).astype(f32)
        r *= 2

    for c, blocks in enumerate(results):
        mixed, grads = unpack(
            tm_count, patches_dev, offsets[c], chunks[c], mixed, grads, blocks
        )
    attended = mixed[:patches].transpose(1, 0, 2)[None]
    tokens_grad = grads[:patches].transpose(1, 0, 2)[None]
    weight_total = summed[:shard]
    gain_total = lax.dynamic_slice(summed[shard], (dp * shard,), (shard,))
    bias_total = lax.dynamic_slice(summed[shard + 1], (dp * shard,), (shard,))
    return (attended, tokens_grad, weight_total, gain_total, bias_total)


def solution(mesh):
    placed = (
        P("dp", "tm", None, None),
        P("dp"),
        P("dp"),
        P("dp", None),
        P("dp"),
        P("dp", None),
        P("dp", None),
        P("dp", "tm", None, None),
    )
    return jax.shard_map(
        body,
        mesh=mesh,
        in_specs=placed,
        out_specs=(
            P("dp", "tm", None, None),
            P("dp", "tm", None, None),
            P("dp", None),
            P("dp"),
            P("dp"),
        ),
        check_vma=False,
    )
```

time: 189 us -> 173 us (0.915)
  local copies, waits for them, and re-layouts: 16.6 us -> 6.81 us
  Pallas kernels: 68.4 us -> 62.4 us
  waiting for transfers between devices: 72.8 us -> 68.4 us
  starting transfers between devices: 26.4 us -> 30.3 us
    unnamed x58 -> x52, local copies, waits for them, and re-layouts: 13.6 us -> 3.82 us
    ppermute x14, waiting for transfers between devices: 39.8 us -> 30.8 us  [swap(): return lax.ppermute(array, 'tm', partner(tm_count, r))]
    ppermute x3, waiting for transfers between devices: 8.21 us -> 14.6 us  [body(): lax.ppermute(own, 'dp', [(i, (i + CORES * k) % dp_count) for i in range(d...]
    ppermute x14, starting transfers between devices: 16.2 us -> 21.3 us  [swap(): return lax.ppermute(array, 'tm', partner(tm_count, r))]
    pallas_call x2, Pallas kernels: 9.56 us -> 5.04 us  [pack(): pl.pallas_call(functools.partial(pack_kernel, tm_count, patches_dev, offs...]
    ppermute x3, waiting for transfers between devices: 21.9 us -> 19.5 us  [body(): lax.ppermute(blocks[k], 'dp', [(i, (i + CORES * k) % dp_count) for i in r...]
    pallas_call x1 -> x2, Pallas kernels: 5.98 us -> 4.36 us  [unpack(): pl.pallas_call(functools.partial(unpack_kernel, tm_count, patches_dev, of...]
  transfers between devices with their start and end apart: 25 -> 25, of which waited for: 10 -> 11; matrix products, arithmetic and copies ran while one was open for 6% -> 0% of each run, Pallas kernels for 21% -> 20%
where the time goes in v2:
time: 173 us; the launch traced here: 172 us
  waiting for transfers between devices  68.4 us (40%)
  Pallas kernels  62.4 us (36%)
  starting transfers between devices  30.3 us (18%)
  local copies, waits for them, and re-layouts  6.81 us (4%)
  other arithmetic  2.83 us (2%)
    pallas_call x2, Pallas kernels, chunk(): pl.pallas_call(functools.partial(chunk_kernel, tm_count, dp_count, frames...  53 us
    ppermute x14, waiting for transfers between devices, swap(): return lax.ppermute(array, 'tm', partner(tm_count, r))  30.8 us
    ppermute x14, starting transfers between devices, swap(): return lax.ppermute(array, 'tm', partner(tm_count, r))  21.3 us
    ppermute x3, waiting for transfers between devices, body(): lax.ppermute(blocks[k], 'dp', [(i, (i + CORES * k) % dp_count) for i in r...  19.5 us
    ppermute x3, waiting for transfers between devices, body(): lax.ppermute(own, 'dp', [(i, (i + CORES * k) % dp_count) for i in range(d...  14.6 us
    ppermute x3, starting transfers between devices, body(): lax.ppermute(own, 'dp', [(i, (i + CORES * k) % dp_count) for i in range(d...  5.49 us
    pallas_call x2, Pallas kernels, pack(): pl.pallas_call(functools.partial(pack_kernel, tm_count, patches_dev, offs...  5.04 us
    pallas_call x2, Pallas kernels, unpack(): pl.pallas_call(functools.partial(unpack_kernel, tm_count, patches_dev, of...  4.36 us
  transfers between devices with their start and end apart: 25, of which 11 were waited for; matrix products, arithmetic and copies ran while one was open for 0% of the time, Pallas kernels for 20%

profile of v2, /device:TPU:0, one launch (start us, length us, event | category | flops | bytes accessed | tf_op | source)
XLA Modules:
  0.0 172.4 jit_solution(7595149870677197901)
XLA Ops:
  3.9 4.7 %collective-permute-start.2 = (bf16[112,1152]{1,0:T(8,128)(2,1)S(1)}, bf16[112,1152]{1,0:T(8,128)(2,1)S(1)}, u32[]{:S(2)}, u32[]{:S(2)}) collective-permute-start(bf16[112,1152]{1,0:T(8,128)(2,1)S(1)} %pad_maximum_fusion.rest_0_), channel_id=1, source_target_pairs={{0,24},{4,28},{8,0},{12,4},{16,8},{20,12},{24,16},{28,20},{1,25},{... | collective-permute-start | bytes 774152 | tf_op jit(solution)/shard_map/ppermute | solution.py:477
  8.6 2.4 %shard_map.120 = (bf16[24,8,1152]{2,1,0:T(8,128)(2,1)}, bf16[24,8,1152]{2,1,0:T(8,128)(2,1)}, bf16[24,8,1152]{2,1,0:T(8,128)(2,1)}) custom-call(bf16[196,8,768]{2,1,0:T(8,128)(2,1)} %bitcast.26, bf16[196,8,384]{2,1,0:T(8,128)(2,1)} %bitcast.31), custom_call_target="tpu_custom_call" | custom-call | tf_op jit(solution)/shard_map/pallas_call | solution.py:67
  11.0 1.6 collective-permute-start.10
  15.2 2.5 %collective-permute-start.12 = (bf16[24,8,1152]{2,1,0:T(8,128)(2,1)}, bf16[24,8,1152]{2,1,0:T(8,128)(2,1)S(1)}, u32[]{:S(2)}, u32[]{:S(2)}) collective-permute-start(bf16[24,8,1152]{2,1,0:T(8,128)(2,1)} %get-tuple-element.33), channel_id=1, source_target_pairs={{0,3},{1,2},{2,1},{3,0},{4,7},{5,6},{6,5},{7,4},{8,11},{9,10},{10,... | collective-permute-start | bytes 1327112 | tf_op jit(solution)/shard_map/ppermute | solution.py:461
  17.7 14.3 %collective-permute-done.1.rest_2_ = bf16[112,1152]{1,0:T(8,128)(2,1)S(1)} collective-permute-done((bf16[112,1152]{1,0:T(8,128)(2,1)S(1)}, bf16[112,1152]{1,0:T(8,128)(2,1)S(1)}, u32[]{:S(2)}, u32[]{:S(2)}) %collective-permute-start.1) | collective-permute-done | bytes 258080 | tf_op jit(solution)/shard_map/ppermute | solution.py:477
  32.0 2.6 %shard_map.119 = (bf16[25,8,1152]{2,1,0:T(8,128)(2,1)}, bf16[25,8,1152]{2,1,0:T(8,128)(2,1)}, bf16[25,8,1152]{2,1,0:T(8,128)(2,1)}) custom-call(bf16[196,8,768]{2,1,0:T(8,128)(2,1)} %bitcast.27, bf16[196,8,384]{2,1,0:T(8,128)(2,1)} %bitcast.32), custom_call_target="tpu_custom_call" | custom-call | tf_op jit(solution)/shard_map/pallas_call | solution.py:67
  34.7 1.6 collective-permute-start.7
  41.2 24.8 %shard_map.121 = (bf16[24,8,1152]{2,1,0:T(8,128)(2,1)}, bf16[24,8,1152]{2,1,0:T(8,128)(2,1)}, bf16[24,8,1152]{2,1,0:T(8,128)(2,1)}, bf16[196,8,384]{2,1,0:T(8,12...) custom-call(s32[1]{0:T(128)S(6)} %copy.27.count_ref, s32[1,2]{1,0:T(1,128)} %starts_ref.3, s32[1,32]{1,0:T(1,128)} %kept_ref.3, ...), custom_call_target="tpu_custom_call" | custom-call | tf_op jit(solution)/shard_map/pallas_call | solution.py:414
  67.1 28.2 %shard_map.122 = (bf16[25,8,1152]{2,1,0:T(8,128)(2,1)}, bf16[25,8,1152]{2,1,0:T(8,128)(2,1)}, bf16[25,8,1152]{2,1,0:T(8,128)(2,1)}, bf16[196,8,384]{2,1,0:T(8,12...) custom-call(s32[1]{0:T(128)S(6)} %copy.27.count_ref, ...), custom_call_target="tpu_custom_call", output_to_operand_aliasing={{3}: (17, {}), {4}: (18, {})} | custom-call | tf_op jit(solution)/shard_map/pallas_call | solution.py:414
  95.6 2.7 %collective-permute-done.19 = bf16[4,112,1152]{2,1,0:T(8,128)(2,1)S(1)} collective-permute-done((bf16[4,112,1152]{2,1,0:T(8,128)(2,1)}, bf16[4,112,1152]{2,1,0:T(8,128)(2,1)S(1)}, u32[]{:S(2)}, u32[]{:S(2)}) %collective-permute-start.19) | collective-permute-done | bytes 1032224 | tf_op jit(solution)/shard_map/ppermute | solution.py:504
  98.4 1.6 fusion
  100.1 1.9 %collective-permute-start.20 = (bf16[112,1152]{1,0:T(8,128)(2,1)S(1)}, bf16[112,1152]{1,0:T(8,128)(2,1)S(1)}, u32[]{:S(2)}, u32[]{:S(2)}) collective-permute-start(bf16[112,1152]{1,0:T(8,128)(2,1)S(1)} %get-tuple-element.54), channel_id=1, source_target_pairs={{0,8},{4,12},{8,16},{12,20},{16,24},{20,28},{24,0},{28,4},{1,9},{5... | collective-permute-start | bytes 774152 | tf_op jit(solution)/shard_map/ppermute | solution.py:513
  103.5 6.0 %collective-permute-done.22 = bf16[112,1152]{1,0:T(8,128)(2,1)S(1)} collective-permute-done((bf16[112,1152]{1,0:T(8,128)(2,1)S(1)}, bf16[112,1152]{1,0:T(8,128)(2,1)S(1)}, u32[]{:S(2)}, u32[]{:S(2)}) %collective-permute-start.22) | collective-permute-done | bytes 258080 | tf_op jit(solution)/shard_map/ppermute | solution.py:513
  109.6 13.5 %collective-permute-done.21 = bf16[112,1152]{1,0:T(8,128)(2,1)S(1)} collective-permute-done((bf16[112,1152]{1,0:T(8,128)(2,1)S(1)}, bf16[112,1152]{1,0:T(8,128)(2,1)S(1)}, u32[]{:S(2)}, u32[]{:S(2)}) %collective-permute-start.21) | collective-permute-done | bytes 258080 | tf_op jit(solution)/shard_map/ppermute | solution.py:513
  123.2 1.6 collective-permute-start.23
  124.7 1.6 collective-permute-start.14
  128.2 1.6 collective-permute-start.17
  129.9 2.5 %collective-permute-done.23 = bf16[112,1152]{1,0:T(8,128)(2,1)S(1)} collective-permute-done((bf16[112,1152]{1,0:T(8,128)(2,1)S(1)}, bf16[112,1152]{1,0:T(8,128)(2,1)S(1)}, u32[]{:S(2)}, u32[]{:S(2)}) %collective-permute-start.23) | collective-permute-done | bytes 258080 | tf_op jit(solution)/shard_map/ppermute | solution.py:461
  132.4 2.5 %collective-permute-start.18 = (bf16[25,8,1152]{2,1,0:T(8,128)(2,1)S(1)}, bf16[25,8,1152]{2,1,0:T(8,128)(2,1)S(1)}, u32[]{:S(2)}, u32[]{:S(2)}) collective-permute-start(bf16[25,8,1152]{2,1,0:T(8,128)(2,1)S(1)} %copy-done.20), channel_id=1, source_target_pairs={{0,3},{1,2},{2,1},{3,0},{4,7},{5,6},{6,5},{7,4},{8,11},{9,10},{10,... | collective-permute-start | bytes 1382408 | tf_op jit(solution)/shard_map/ppermute | solution.py:461
  134.9 12.4 %collective-permute-done.14.refs_3_ = bf16[24,8,1152]{2,1,0:T(8,128)(2,1)S(1)} collective-permute-done((bf16[24,8,1152]{2,1,0:T(8,128)(2,1)S(1)}, bf16[24,8,1152]{2,1,0:T(8,128)(2,1)S(1)}, u32[]{:S(2)}, u32[]{:S(2)}) %collective-permute-start.14) | collective-permute-done | bytes 442400 | tf_op jit(solution)/shard_map/ppermute | solution.py:461
  147.3 1.6 collective-permute-start.24
  149.7 2.2 %shard_map.123 = (bf16[196,8,384]{2,1,0:T(8,128)(2,1)}, bf16[196,8,768]{2,1,0:T(8,128)(2,1)}) custom-call(bf16[196,8,384]{2,1,0:T(8,128)(2,1)} %get-tuple-element.37.refs_0_, bf16[196,8,768]{2,1,0:T(8,128)(2,1)} %get-tuple-element.38.refs_1_, bf16[24,8,1152]{2,1,0:T(8,128)(2,1)} %copy-done.16, ...), custom_call_target="tpu_custom_call", output_to_operand_aliasing={{0}: (0, {}), {1}: (1, {})} | custom-call | tf_op jit(solution)/shard_map/pallas_call | solution.py:100
  151.9 15.2 %collective-permute-done.17.refs_3_ = bf16[25,8,1152]{2,1,0:T(8,128)(2,1)S(1)} collective-permute-done((bf16[25,8,1152]{2,1,0:T(8,128)(2,1)S(1)}, bf16[25,8,1152]{2,1,0:T(8,128)(2,1)S(1)}, u32[]{:S(2)}, u32[]{:S(2)}) %collective-permute-start.17) | collective-permute-done | bytes 460832 | tf_op jit(solution)/shard_map/ppermute | solution.py:461
  168.0 2.2 %shard_map.124 = (bf16[196,8,384]{2,1,0:T(8,128)(2,1)}, bf16[196,8,768]{2,1,0:T(8,128)(2,1)}) custom-call(bf16[196,8,384]{2,1,0:T(8,128)(2,1)} %get-tuple-element.42.refs_0_, bf16[196,8,768]{2,1,0:T(8,128)(2,1)} %get-tuple-element.43.refs_1_, bf16[25,8,1152]{2,1,0:T(8,128)(2,1)} %copy-done.11, ...), custom_call_target="tpu_custom_call", output_to_operand_aliasing={{0}: (0, {}), {1}: (1, {})} | custom-call | tf_op jit(solution)/shard_map/pallas_call | solution.py:100
  (95 shorter events, 19.1 us)
Async XLA Ops:
  3.2 10.9 %collective-permute-start.3 = (bf16[112,1152]{1,0:T(8,128)(2,1)S(1)}, bf16[112,1152]{1,0:T(8,128)(2,1)S(1)}, u32[]{:S(2)}, u32[]{:S(2)}) collective-permute-start(bf16[112,1152]{1,0:T(8,128)(2,1)S(1)} %pad_maximum_fusion.rest_0_), channel_id=1, source_target_pairs={{0,4},{4,0},{8,12},{12,8},{16,20},{20,16},{24,28},{28,24},{1,5},{5... | collective-permute-start | bytes 774152 | tf_op jit(solution)/shard_map/ppermute | solution.py:480
  3.9 11.2 %collective-permute-start.2 = (bf16[112,1152]{1,0:T(8,128)(2,1)S(1)}, bf16[112,1152]{1,0:T(8,128)(2,1)S(1)}, u32[]{:S(2)}, u32[]{:S(2)}) collective-permute-start(bf16[112,1152]{1,0:T(8,128)(2,1)S(1)} %pad_maximum_fusion.rest_0_), channel_id=1, source_target_pairs={{0,24},{4,28},{8,0},{12,4},{16,8},{20,12},{24,16},{28,20},{1,25},{... | collective-permute-start | bytes 774152 | tf_op jit(solution)/shard_map/ppermute | solution.py:477
  11.0 25.2 %collective-permute-start.10 = (bf16[24,8,1152]{2,1,0:T(8,128)(2,1)}, bf16[24,8,1152]{2,1,0:T(8,128)(2,1)S(1)}, u32[]{:S(2)}, u32[]{:S(2)}) collective-permute-start(bf16[24,8,1152]{2,1,0:T(8,128)(2,1)} %get-tuple-element.31), channel_id=1, source_target_pairs={{0,1},{1,0},{2,3},{3,2},{4,5},{5,4},{6,7},{7,6},{8,9},{9,8},{10,11... | collective-permute-start | bytes 1327112 | tf_op jit(solution)/shard_map/ppermute | solution.py:461
  12.6 24.9 %collective-permute-start.11 = (bf16[24,8,1152]{2,1,0:T(8,128)(2,1)}, bf16[24,8,1152]{2,1,0:T(8,128)(2,1)S(1)}, u32[]{:S(2)}, u32[]{:S(2)}) collective-permute-start(bf16[24,8,1152]{2,1,0:T(8,128)(2,1)} %get-tuple-element.32), channel_id=1, source_target_pairs={{0,2},{1,3},{2,0},{3,1},{4,6},{5,7},{6,4},{7,5},{8,10},{9,11},{10,... | collective-permute-start | bytes 1327112 | tf_op jit(solution)/shard_map/ppermute | solution.py:461
  14.1 17.9 %collective-permute-start.1 = (bf16[112,1152]{1,0:T(8,128)(2,1)S(1)}, bf16[112,1152]{1,0:T(8,128)(2,1)S(1)}, u32[]{:S(2)}, u32[]{:S(2)}) collective-permute-start(bf16[112,1152]{1,0:T(8,128)(2,1)S(1)} %pad_maximum_fusion.rest_0_), channel_id=1, source_target_pairs={{0,16},{4,20},{8,24},{12,28},{16,0},{20,4},{24,8},{28,12},{1,17},{... | collective-permute-start | bytes 774152 | tf_op jit(solution)/shard_map/ppermute | solution.py:477
  14.1 20.6 %collective-permute-start = (bf16[112,1152]{1,0:T(8,128)(2,1)S(1)}, bf16[112,1152]{1,0:T(8,128)(2,1)S(1)}, u32[]{:S(2)}, u32[]{:S(2)}) collective-permute-start(bf16[112,1152]{1,0:T(8,128)(2,1)S(1)} %pad_maximum_fusion.rest_0_), channel_id=1, source_target_pairs={{0,8},{4,12},{8,16},{12,20},{16,24},{20,28},{24,0},{28,4},{1,9},{5... | collective-permute-start | bytes 774152 | tf_op jit(solution)/shard_map/ppermute | solution.py:477
  15.2 23.1 %collective-permute-start.12 = (bf16[24,8,1152]{2,1,0:T(8,128)(2,1)}, bf16[24,8,1152]{2,1,0:T(8,128)(2,1)S(1)}, u32[]{:S(2)}, u32[]{:S(2)}) collective-permute-start(bf16[24,8,1152]{2,1,0:T(8,128)(2,1)} %get-tuple-element.33), channel_id=1, source_target_pairs={{0,3},{1,2},{2,1},{3,0},{4,7},{5,6},{6,5},{7,4},{8,11},{9,10},{10,... | collective-permute-start | bytes 1327112 | tf_op jit(solution)/shard_map/ppermute | solution.py:461
  32.0 6.3 %collective-permute-start.6 = (bf16[112,1152]{1,0:T(8,128)(2,1)S(1)}, bf16[112,1152]{1,0:T(8,128)(2,1)S(1)}, u32[]{:S(2)}, u32[]{:S(2)}) collective-permute-start(bf16[112,1152]{1,0:T(8,128)(2,1)S(1)} %collective-permute-done.2.rest_3_), channel_id=1, source_target_pairs={{0,4},{4,0},{8,12},{12,8},{16,20},{20,16},{24,28},{28,24},{1,5},{5... | collective-permute-start | bytes 774152 | tf_op jit(solution)/shard_map/ppermute | solution.py:480
  34.7 31.3 %collective-permute-start.7 = (bf16[25,8,1152]{2,1,0:T(8,128)(2,1)}, bf16[25,8,1152]{2,1,0:T(8,128)(2,1)S(1)}, u32[]{:S(2)}, u32[]{:S(2)}) collective-permute-start(bf16[25,8,1152]{2,1,0:T(8,128)(2,1)} %get-tuple-element.28), channel_id=1, source_target_pairs={{0,1},{1,0},{2,3},{3,2},{4,5},{5,4},{6,7},{7,6},{8,9},{9,8},{10,11... | collective-permute-start | bytes 1382408 | tf_op jit(solution)/shard_map/ppermute | solution.py:461
  36.3 29.8 %collective-permute-start.8 = (bf16[25,8,1152]{2,1,0:T(8,128)(2,1)}, bf16[25,8,1152]{2,1,0:T(8,128)(2,1)S(1)}, u32[]{:S(2)}, u32[]{:S(2)}) collective-permute-start(bf16[25,8,1152]{2,1,0:T(8,128)(2,1)} %get-tuple-element.29), channel_id=1, source_target_pairs={{0,2},{1,3},{2,0},{3,1},{4,6},{5,7},{6,4},{7,5},{8,10},{9,11},{10,... | collective-permute-start | bytes 1382408 | tf_op jit(solution)/shard_map/ppermute | solution.py:461
  37.5 28.6 %collective-permute-start.9 = (bf16[25,8,1152]{2,1,0:T(8,128)(2,1)}, bf16[25,8,1152]{2,1,0:T(8,128)(2,1)S(1)}, u32[]{:S(2)}, u32[]{:S(2)}) collective-permute-start(bf16[25,8,1152]{2,1,0:T(8,128)(2,1)} %get-tuple-element.30), channel_id=1, source_target_pairs={{0,3},{1,2},{2,1},{3,0},{4,7},{5,6},{6,5},{7,4},{8,11},{9,10},{10,... | collective-permute-start | bytes 1382408 | tf_op jit(solution)/shard_map/ppermute | solution.py:461
  38.3 1.9 %collective-permute-start.4 = (bf16[112,1152]{1,0:T(8,128)(2,1)S(1)}, bf16[112,1152]{1,0:T(8,128)(2,1)S(1)}, u32[]{:S(2)}, u32[]{:S(2)}) collective-permute-start(bf16[112,1152]{1,0:T(8,128)(2,1)S(1)} %collective-permute-done.rest_1_), channel_id=1, source_target_pairs={{0,4},{4,0},{8,12},{12,8},{16,20},{20,16},{24,28},{28,24},{1,5},{5... | collective-permute-start | bytes 774152 | tf_op jit(solution)/shard_map/ppermute | solution.py:480
  95.4 2.9 %collective-permute-start.19 = (bf16[4,112,1152]{2,1,0:T(8,128)(2,1)}, bf16[4,112,1152]{2,1,0:T(8,128)(2,1)S(1)}, u32[]{:S(2)}, u32[]{:S(2)}) collective-permute-start(bf16[4,112,1152]{2,1,0:T(8,128)(2,1)} %get-tuple-element.50), channel_id=1, source_target_pairs={{0,4},{4,0},{8,12},{12,8},{16,20},{20,16},{24,28},{28,24},{1,5},{5... | collective-permute-start | bytes 3096584 | tf_op jit(solution)/shard_map/ppermute | solution.py:504
  100.0 9.6 %collective-permute-start.22 = (bf16[112,1152]{1,0:T(8,128)(2,1)S(1)}, bf16[112,1152]{1,0:T(8,128)(2,1)S(1)}, u32[]{:S(2)}, u32[]{:S(2)}) collective-permute-start(bf16[112,1152]{1,0:T(8,128)(2,1)S(1)} %get-tuple-element.52), channel_id=1, source_target_pairs={{0,24},{4,28},{8,0},{12,4},{16,8},{20,12},{24,16},{28,20},{1,25},{... | collective-permute-start | bytes 774152 | tf_op jit(solution)/shard_map/ppermute | solution.py:513
  100.0 23.0 %collective-permute-start.21 = (bf16[112,1152]{1,0:T(8,128)(2,1)S(1)}, bf16[112,1152]{1,0:T(8,128)(2,1)S(1)}, u32[]{:S(2)}, u32[]{:S(2)}) collective-permute-start(bf16[112,1152]{1,0:T(8,128)(2,1)S(1)} %get-tuple-element.53), channel_id=1, source_target_pairs={{0,16},{4,20},{8,24},{12,28},{16,0},{20,4},{24,8},{28,12},{1,17},{... | collective-permute-start | bytes 774152 | tf_op jit(solution)/shard_map/ppermute | solution.py:513
  100.1 22.9 %collective-permute-start.20 = (bf16[112,1152]{1,0:T(8,128)(2,1)S(1)}, bf16[112,1152]{1,0:T(8,128)(2,1)S(1)}, u32[]{:S(2)}, u32[]{:S(2)}) collective-permute-start(bf16[112,1152]{1,0:T(8,128)(2,1)S(1)} %get-tuple-element.54), channel_id=1, source_target_pairs={{0,8},{4,12},{8,16},{12,20},{16,24},{20,28},{24,0},{28,4},{1,9},{5... | collective-permute-start | bytes 774152 | tf_op jit(solution)/shard_map/ppermute | solution.py:513
  102.0 26.2 %collective-permute-start.13 = (bf16[24,8,1152]{2,1,0:T(8,128)(2,1)S(1)}, bf16[24,8,1152]{2,1,0:T(8,128)(2,1)S(1)}, u32[]{:S(2)}, u32[]{:S(2)}) collective-permute-start(bf16[24,8,1152]{2,1,0:T(8,128)(2,1)S(1)} %copy-done.25), channel_id=1, source_target_pairs={{0,1},{1,0},{2,3},{3,2},{4,5},{5,4},{6,7},{7,6},{8,9},{9,8},{10,11... | collective-permute-start | bytes 1327112 | tf_op jit(solution)/shard_map/ppermute | solution.py:461
  123.2 9.2 %collective-permute-start.23 = (bf16[112,1152]{1,0:T(8,128)(2,1)S(1)}, bf16[112,1152]{1,0:T(8,128)(2,1)S(1)}, u32[]{:S(2)}, u32[]{:S(2)}) collective-permute-start(bf16[112,1152]{1,0:T(8,128)(2,1)S(1)} %add_convert_fusion.1), channel_id=1, source_target_pairs={{0,1},{1,0},{2,3},{3,2},{4,5},{5,4},{6,7},{7,6},{8,9},{9,8},{10,11... | collective-permute-start | bytes 774152 | tf_op jit(solution)/shard_map/ppermute | solution.py:461
  124.7 22.6 %collective-permute-start.14 = (bf16[24,8,1152]{2,1,0:T(8,128)(2,1)S(1)}, bf16[24,8,1152]{2,1,0:T(8,128)(2,1)S(1)}, u32[]{:S(2)}, u32[]{:S(2)}) collective-permute-start(bf16[24,8,1152]{2,1,0:T(8,128)(2,1)S(1)} %copy-done.24), channel_id=1, source_target_pairs={{0,2},{1,3},{2,0},{3,1},{4,6},{5,7},{6,4},{7,5},{8,10},{9,11},{10,... | collective-permute-start | bytes 1327112 | tf_op jit(solution)/shard_map/ppermute | solution.py:461
  126.3 22.6 %collective-permute-start.15 = (bf16[24,8,1152]{2,1,0:T(8,128)(2,1)S(1)}, bf16[24,8,1152]{2,1,0:T(8,128)(2,1)S(1)}, u32[]{:S(2)}, u32[]{:S(2)}) collective-permute-start(bf16[24,8,1152]{2,1,0:T(8,128)(2,1)S(1)} %copy-done.23), channel_id=1, source_target_pairs={{0,3},{1,2},{2,1},{3,0},{4,7},{5,6},{6,5},{7,4},{8,11},{9,10},{10,... | collective-permute-start | bytes 1327112 | tf_op jit(solution)/shard_map/ppermute | solution.py:461
  126.7 25.1 %collective-permute-start.16 = (bf16[25,8,1152]{2,1,0:T(8,128)(2,1)S(1)}, bf16[25,8,1152]{2,1,0:T(8,128)(2,1)S(1)}, u32[]{:S(2)}, u32[]{:S(2)}) collective-permute-start(bf16[25,8,1152]{2,1,0:T(8,128)(2,1)S(1)} %copy-done.22), channel_id=1, source_target_pairs={{0,1},{1,0},{2,3},{3,2},{4,5},{5,4},{6,7},{7,6},{8,9},{9,8},{10,11... | collective-permute-start | bytes 1382408 | tf_op jit(solution)/shard_map/ppermute | solution.py:461
  128.2 38.8 %collective-permute-start.17 = (bf16[25,8,1152]{2,1,0:T(8,128)(2,1)S(1)}, bf16[25,8,1152]{2,1,0:T(8,128)(2,1)S(1)}, u32[]{:S(2)}, u32[]{:S(2)}) collective-permute-start(bf16[25,8,1152]{2,1,0:T(8,128)(2,1)S(1)} %copy-done.21), channel_id=1, source_target_pairs={{0,2},{1,3},{2,0},{3,1},{4,6},{5,7},{6,4},{7,5},{8,10},{9,11},{10,... | collective-permute-start | bytes 1382408 | tf_op jit(solution)/shard_map/ppermute | solution.py:461
  132.4 34.7 %collective-permute-start.18 = (bf16[25,8,1152]{2,1,0:T(8,128)(2,1)S(1)}, bf16[25,8,1152]{2,1,0:T(8,128)(2,1)S(1)}, u32[]{:S(2)}, u32[]{:S(2)}) collective-permute-start(bf16[25,8,1152]{2,1,0:T(8,128)(2,1)S(1)} %copy-done.20), channel_id=1, source_target_pairs={{0,3},{1,2},{2,1},{3,0},{4,7},{5,6},{6,5},{7,4},{8,11},{9,10},{10,... | collective-permute-start | bytes 1382408 | tf_op jit(solution)/shard_map/ppermute | solution.py:461
  147.3 23.6 %collective-permute-start.24 = (bf16[112,1152]{1,0:T(8,128)(2,1)S(1)}, bf16[112,1152]{1,0:T(8,128)(2,1)S(1)}, u32[]{:S(2)}, u32[]{:S(2)}) collective-permute-start(bf16[112,1152]{1,0:T(8,128)(2,1)S(1)} %add_convert_fusion), channel_id=1, source_target_pairs={{0,2},{1,3},{2,0},{3,1},{4,6},{5,7},{6,4},{7,5},{8,10},{9,11},{10,... | collective-permute-start | bytes 774152 | tf_op jit(solution)/shard_map/ppermute | solution.py:461
  (27 other events, 320.4 us)

commit v3 on v2

--- a/solution.py
+++ b/solution.py
@@ -47,7 +47,8 @@
 
 
 def pack_kernel(tm_count, patches_dev, offset, size, x_ref, grad_ref, *rest):
-    outs, sems = rest[:-1], rest[-1]
+    sems = rest[-1]
+    outs = rest[-tm_count:-1]
     width = x_ref.shape[2]
     me = lax.axis_index("tm")
     pairs = []
@@ -57,21 +58,40 @@
         pairs.append(
             (grad_ref.at[place], outs[r - 1].at[:, :, pl.ds(width, grad_ref.shape[2])])
         )
-    for copy in run_all(pairs, sems):
+    if len(rest) > tm_count:
+        weight_ref, lines_ref, own_ref = rest[:3]
+        shard, columns = weight_ref.shape
+        pairs.append((weight_ref, own_ref.at[pl.ds(0, shard)]))
+    copies = run_all(pairs, sems)
+    if len(rest) > tm_count:
+        owner = lax.broadcasted_iota(jnp.int32, lines_ref.shape, 1) // shard
+        lines = jnp.where(owner == lax.axis_index("dp"), lines_ref[...].astype(f32), 0.0)
+        own_ref[shard:, :] = jnp.concatenate(
+            [lines, jnp.zeros((EXTRA - lines.shape[0], columns), f32)], axis=0
+        ).astype(bf16)
+    for copy in copies:
         copy.wait()
 
 
-def pack(tm_count, patches_dev, offset, size, tokens, grads):
+def pack(tm_count, patches_dev, offset, size, tokens, grads, weight=None, lines=None):
     _, frames, width = tokens.shape
     total = width + grads.shape[2]
+    in_vmem = pl.BlockSpec(memory_space=pltpu.VMEM)
+    args, specs = [tokens, grads], [anywhere] * 2
+    outs = [jax.ShapeDtypeStruct((size, frames, total), bf16)] * (tm_count - 1)
+    if weight is not None:
+        args += [weight, lines]
+        specs += [anywhere, in_vmem]
+        shard, columns = weight.shape
+        outs = [jax.ShapeDtypeStruct((shard + EXTRA, columns), bf16)] + outs
     return pl.pallas_call(
         functools.partial(pack_kernel, tm_count, patches_dev, offset, size),
-        out_shape=[jax.ShapeDtypeStruct((size, frames, total), bf16)] * (tm_count - 1),
-        in_specs=[anywhere] * 2,
-        out_specs=[pl.BlockSpec(memory_space=pltpu.VMEM)] * (tm_count - 1),
+        out_shape=outs,
+        in_specs=specs,
+        out_specs=[in_vmem] * len(outs),
         scratch_shapes=[pltpu.SemaphoreType.DMA((2 * tm_count,))],
         compiler_params=pltpu.CompilerParams(vmem_limit_bytes=vmem_limit),
-    )(tokens, grads)
+    )(*args)
 
 
 def unpack_kernel(tm_count, patches_dev, offset, size, *refs):
@@ -141,18 +161,19 @@
     kept_ref,
     *rest,
 ):
+    nz = dp_count // CORES
     rest = list(rest)
     take = lambda n: [rest.pop(0) for _ in range(n)]
-    pieces = take(dp_count)
+    pieces = take(nz + 1)
     x_ref, grad_ref = take(2)
     sources = take(tm_count - 1)
     if not first:
-        before = take(1)[0]
+        before, before_ends = take(2)
         take(2)
     outs = take(tm_count - 1)
     mixed_ref, tokens_ref = take(2)
-    sums = take(2) if last else take(1)
-    (xs, weight, extra, normed, standard, proj, pgrad, back, acc, ends, allow, sems) = rest
+    sums = take(4) if last else take(2)
+    (xs, weight, extra, normed, standard, proj, pgrad, back, acc, ends, tails, allow, sems) = rest
     size = sources[0].shape[0]
     width = weight.shape[0]
     columns = weight.shape[1]
@@ -163,7 +184,6 @@
     me = lax.axis_index("tm")
     dp = lax.axis_index("dp")
     z, core = dp // CORES, dp % CORES
-    nz = dp_count // CORES
 
     started = []
 
@@ -184,14 +204,14 @@
     for side in range(CORES):
         for k in range(nz):
             owner = lax.rem(z + nz - k, nz) * CORES + (core ^ side)
-            piece = pieces[side * nz + k]
+            piece = pieces[k] if side == 0 else pieces[nz].at[k]
             place = pl.ds(pl.multiple_of(owner * shard, shard), shard)
             weights_in.append(bring(piece.at[pl.ds(0, shard)], weight.at[place]))
             weights_in.append(
                 bring(piece.at[pl.ds(shard, EXTRA)], extra.at[side * nz + k])
             )
     if not first:
-        acc_in = bring(before, acc)
+        acc_in = [bring(before, acc), bring(before_ends, tails)]
     if xs.shape[1] > size:
         for r in range(tm_count):
             xs[r, size:] = jnp.zeros((xs.shape[1] - size,) + xs.shape[2:], bf16)
@@ -281,61 +301,76 @@
     def _(j):
         at = pl.ds(pl.multiple_of(j * unit, unit), unit)
         allowed = allow[...] > 0.5
-        for pair in range(pairs):
-            col = slice(pair * 128, (pair + 1) * 128)
-            q2 = proj[at, pair * 128 : (pair + 1) * 128]
-            k2 = proj[at, joined + pair * 128 : joined + (pair + 1) * 128]
-            v2 = proj[at, 2 * joined + pair * 128 : 2 * joined + (pair + 1) * 128]
-            up = token_rows(j, slice(width + pair * 128, width + (pair + 1) * 128))
-            up = jnp.where(token_valid, up, 0.0).astype(bf16)
-            kcat, vcat, qcat, ucat = stack(k2), stack(v2), stack(q2), stack(up)
-            scores = compact(lax.dot_general(kcat, q2, nt, preferred_element_type=f32))
-            scores = jnp.where(allowed, scores * scale, masked_value)
-            shifted = jnp.exp(scores - jnp.max(scores, axis=1, keepdims=True))
-            probs = shifted / jnp.sum(shifted, axis=1, keepdims=True)
-            full = expand(probs)
-            mixed = lax.dot_general(full, vcat, tn, preferred_element_type=f32)
-            put_rows(j, col, jnp.where(token_valid, mixed, 0.0))
-            across = jnp.concatenate([full[:unit], full[unit:]], axis=1)
-            value_grad = jnp.dot(across, ucat, preferred_element_type=f32)
-            wgrad = compact(lax.dot_general(vcat, up, nt, preferred_element_type=f32))
-            inner = jnp.sum(wgrad * probs, axis=1, keepdims=True)
-            sgrad = expand(probs * (wgrad - inner) * scale)
-            query_grad = lax.dot_general(sgrad, kcat, tn, preferred_element_type=f32)
-            sacross = jnp.concatenate([sgrad[:unit], sgrad[unit:]], axis=1)
-            key_grad = jnp.dot(sacross, qcat, preferred_element_type=f32)
-            pgrad[at, pair * 128 : (pair + 1) * 128] = query_grad.astype(bf16)
-            pgrad[at, joined + pair * 128 : joined + (pair + 1) * 128] = key_grad.astype(bf16)
-            pgrad[at, 2 * joined + pair * 128 : 2 * joined + (pair + 1) * 128] = (
-                value_grad.astype(bf16)
-            )
+        every = range(pairs)
+        cols = [slice(pair * 128, (pair + 1) * 128) for pair in every]
+        cut = lambda part: [
+            proj[at, part * joined + pair * 128 : part * joined + (pair + 1) * 128]
+            for pair in every
+        ]
+        q2, k2, v2 = cut(0), cut(1), cut(2)
+        up = [
+            token_rows(j, slice(width + pair * 128, width + (pair + 1) * 128)) for pair in every
+        ]
+        up = [jnp.where(token_valid, u, 0.0).astype(bf16) for u in up]
+        kcat, vcat = [stack(k) for k in k2], [stack(v) for v in v2]
+        scores = [
+            compact(lax.dot_general(kcat[i], q2[i], nt, preferred_element_type=f32))
+            for i in every
+        ]
+        wgrad = [
+            compact(lax.dot_general(vcat[i], up[i], nt, preferred_element_type=f32))
+            for i in every
+        ]
+        probs = []
+        for i in every:
+            masked = jnp.where(allowed, scores[i] * scale, masked_value)
+            shifted = jnp.exp(masked - jnp.max(masked, axis=1, keepdims=True))
+            probs.append(shifted * (1.0 / jnp.sum(shifted, axis=1, keepdims=True)))
+        full = [expand(p) for p in probs]
+        sgrad = []
+        for i in every:
+            inner = jnp.sum(wgrad[i] * probs[i], axis=1, keepdims=True)
+            sgrad.append(expand(probs[i] * (wgrad[i] - inner) * scale))
+        for i in every:
+            mixed = lax.dot_general(full[i], vcat[i], tn, preferred_element_type=f32)
+            put_rows(j, cols[i], jnp.where(token_valid, mixed, 0.0))
+            across = jnp.concatenate([full[i][:unit], full[i][unit:]], axis=1)
+            value_grad = jnp.dot(across, stack(up[i]), preferred_element_type=f32)
+            query_grad = lax.dot_general(sgrad[i], kcat[i], tn, preferred_element_type=f32)
+            sacross = jnp.concatenate([sgrad[i][:unit], sgrad[i][unit:]], axis=1)
+            key_grad = jnp.dot(sacross, stack(q2[i]), preferred_element_type=f32)
+            for part, value in enumerate((query_grad, key_grad, value_grad)):
+                place = slice(part * joined + i * 128, part * joined + (i + 1) * 128)
+                pgrad[at, place] = value.astype(bf16)
 
     if not first:
-        acc_in.wait()
+        for copy in acc_in:
+            copy.wait()
+    else:
+        tails[...] = jnp.zeros_like(tails)
     for part in range(3):
         cut = slice(part * joined, (part + 1) * joined)
         share = lax.dot_general(normed[...], pgrad[:, cut], tn, preferred_element_type=f32)
         if first:
-            acc[:width, cut] = share
+            acc[:, cut] = share
         else:
-            acc[:width, cut] += share
-
-    if first:
-        acc[width:, :] = jnp.zeros((acc.shape[0] - width, columns), f32)
+            acc[:, cut] += share
+
+    gone = []
+    if not last:
+        gone.append(bring(acc, sums[0]))
+    normed[...] = lax.dot_general(
+        pgrad[...], weight[...], nt, preferred_element_type=f32
+    ).astype(bf16)
 
     @pl.loop(0, groups)
     def _(j):
         at = pl.ds(pl.multiple_of(j * unit, unit), unit)
-        ngrad = lax.dot_general(
-            pgrad[at, :], weight[...], nt, preferred_element_type=f32
-        )
-        ngrad = ngrad.astype(bf16).astype(f32)
+        ngrad = normed[at, :].astype(f32)
         std = standard[at, :]
         product = ngrad * std
-        acc[width : width + 8, :width] += jnp.sum(product.reshape(unit // 8, 8, width), axis=0)
-        acc[width + 8 : width + 16, :width] += jnp.sum(
-            ngrad.reshape(unit // 8, 8, width), axis=0
-        )
+        tails[0:8, :] += jnp.sum(product.reshape(unit // 8, 8, width), axis=0)
+        tails[8:16, :] += jnp.sum(ngrad.reshape(unit // 8, 8, width), axis=0)
         scaled = ngrad * gain
         grad = ends[at, 0:1] * (
             scaled
@@ -344,27 +379,31 @@
         )
         put_rows(j, slice(joined, columns), grad)
 
-    gone = [bring(back.at[r, kept], outs[r - 1]) for r in range(1, tm_count)]
+    gone += [bring(back.at[r, kept], outs[r - 1]) for r in range(1, tm_count)]
     gone.append(bring(back.at[0, kept, :, pl.ds(0, joined)], mixed_ref.at[mine]))
     gone.append(bring(back.at[0, kept, :, pl.ds(joined, width)], tokens_ref.at[mine]))
     if not last:
-        gone.append(bring(acc, sums[0]))
+        gone.append(bring(tails, sums[1]))
     else:
-        keep, send = sums
+        cut = sums[0].shape[1]
         extra_rows = jnp.concatenate(
             [
-                jnp.sum(acc[width : width + 8, :], axis=0, keepdims=True),
-                jnp.sum(acc[width + 8 : width + 16, :], axis=0, keepdims=True),
-                jnp.zeros((EXTRA - 2, columns), f32),
+                jnp.sum(tails[0:8, :], axis=0, keepdims=True),
+                jnp.sum(tails[8:16, :], axis=0, keepdims=True),
+                jnp.zeros((EXTRA - 2, width), f32),
             ],
             axis=0,
         ).astype(bf16)
         for k in range(nz):
             owner = lax.rem(z + k, nz) * CORES
-            for ref, side in ((keep, core), (send, 1 - core)):
-                place = pl.ds(pl.multiple_of((owner + side) * shard, shard), shard)
-                ref[k, :shard, :] = acc[place, :].astype(bf16)
-                ref[k, shard:, :] = extra_rows
+            for refs, side in ((sums[:2], core), (sums[2:], 1 - core)):
+                start = pl.multiple_of((owner + side) * shard, shard)
+                refs[0][k] = acc[pl.ds(start, cut), :].astype(bf16)
+                refs[1][k, : shard - cut, :] = acc[
+                    pl.ds(pl.multiple_of(start + cut, 16), shard - cut), :
+                ].astype(bf16)
+                refs[1][k, shard - cut :, :width] = extra_rows
+                refs[1][k, shard - cut :, width:] = jnp.zeros((EXTRA, columns - width), bf16)
     for copy in gone:
         copy.wait()
 
@@ -386,11 +425,15 @@
     ]
     out_specs = [anywhere] * len(outs)
     if last:
-        outs += [jax.ShapeDtypeStruct((nz, shard + EXTRA, columns), bf16)] * 2
-        out_specs += [pl.BlockSpec(memory_space=pltpu.VMEM)] * 2
+        cut = round_up(shard // 2, 16)
+        for _ in range(2):
+            outs.append(jax.ShapeDtypeStruct((nz, cut, columns), bf16))
+            outs.append(jax.ShapeDtypeStruct((nz, shard - cut + EXTRA, columns), bf16))
+        out_specs += [pl.BlockSpec(memory_space=pltpu.VMEM)] * 4
     else:
-        outs += [jax.ShapeDtypeStruct((width + 16, columns), f32)]
-        out_specs += [anywhere]
+        outs.append(jax.ShapeDtypeStruct((width, columns), f32))
+        outs.append(jax.ShapeDtypeStruct((16, width), f32))
+        out_specs += [anywhere] * 2
     args = list(facts) + list(pieces) + [tokens_in, grads_in] + list(blocks)
     aliases = {}
     if not first:
@@ -406,10 +449,11 @@
         pltpu.VMEM((tokens, columns), bf16),
         pltpu.VMEM((tokens, columns), bf16),
         pltpu.VMEM(rows, bf16),
-        pltpu.VMEM((width + 16, columns), f32),
+        pltpu.VMEM((width, columns), f32),
         pltpu.VMEM((tokens, 128), f32),
+        pltpu.VMEM((16, width), f32),
         pltpu.VMEM((tm_count * frames, tokens // groups), f32),
-        pltpu.SemaphoreType.DMA((2 * tm_count + 2 * dp_count + 8,)),
+        pltpu.SemaphoreType.DMA((2 * tm_count + 2 * dp_count + 12,)),
     ]
     return pl.pallas_call(
         functools.partial(
@@ -464,20 +508,24 @@
     tokens = jnp.pad(video_tokens[0].transpose(1, 0, 2), spare)
     upstream = jnp.pad(attended_grad[0].transpose(1, 0, 2), spare)
     offsets = [sum(chunks[:c]) for c in range(len(chunks))]
+    lines = jnp.tile(jnp.stack([norm_gain, norm_bias]), (1, -(-columns // shard)))[:, :columns]
+
+    def shift(array, k):
+        hops = [(i, (i + CORES * k) % dp_count) for i in range(dp_count)]
+        return lax.ppermute(array, "dp", hops)
+
     gathered = []
-    for offset, size in zip(offsets, chunks):
-        blocks = pack(tm_count, patches_dev, offset, size, tokens, upstream)
-        gathered.append([swap(part, r + 1) for r, part in enumerate(blocks)])
-
-    lines = jnp.zeros((EXTRA, columns), bf16)
-    lines = lax.dynamic_update_slice(lines, norm_gain[None], (0, dp * shard))
-    lines = lax.dynamic_update_slice(lines, norm_bias[None], (1, dp * shard))
-    own = jnp.concatenate([qkv_weight, lines], axis=0)
-    along = [own] + [
-        lax.ppermute(own, "dp", [(i, (i + CORES * k) % dp_count) for i in range(dp_count)])
-        for k in range(1, nz)
-    ]
-    pieces = along + [lax.ppermute(a, "dp", partner(dp_count, 1)) for a in along]
+    for c, size in enumerate(chunks):
+        more = (qkv_weight, lines) if c == 0 else ()
+        blocks = pack(tm_count, patches_dev, offsets[c], size, tokens, upstream, *more)
+        if c == 0:
+            along = [blocks[0]] + [shift(blocks[0], k) for k in range(1, nz)]
+            blocks = blocks[1:]
+        blocks = [swap(part, r + 1) for r, part in enumerate(blocks)]
+        if c == 0:
+            along, blocks = lax.optimization_barrier((along, blocks))
+            pieces = along + [lax.ppermute(jnp.stack(along), "dp", partner(dp_count, 1))]
+        gathered.append(blocks)
 
     facts = (frame_counts, clip_starts, frame_kept)
     results, before = [], None
@@ -498,26 +546,30 @@
         )
         results.append([swap(part, r + 1) for r, part in enumerate(got[: tm_count - 1])])
         mixed, grads = got[tm_count - 1 : tm_count + 1]
-        before = (got[tm_count + 1], mixed, grads)
-    total, sent_half = got[-2:]
-
-    other = lax.ppermute(sent_half, "dp", partner(dp_count, 1))
-    blocks = [
-        lax.optimization_barrier(
-            (total[k].astype(f32) + other[k].astype(f32)).astype(bf16)
-        )
-        for k in range(nz)
-    ]
-    summed = blocks[0].astype(f32)
-    for k in range(1, nz):
-        summed = summed + lax.ppermute(
-            blocks[k], "dp", [(i, (i + CORES * k) % dp_count) for i in range(dp_count)]
-        ).astype(f32)
-    r = 1
-    while r < tm_count:
-        mine = lax.optimization_barrier(summed.astype(bf16))
-        summed = mine.astype(f32) + swap(mine, r).astype(f32)
-        r *= 2
+        before = (got[tm_count + 1], got[tm_count + 2], mixed, grads)
+    keep, send = got[-4:-2], got[-2:]
+
+    send, results[0] = lax.optimization_barrier((send, results[0]))
+    others = [lax.ppermute(part, "dp", partner(dp_count, 1)) for part in send]
+    halves = []
+    for mine, other in zip(keep, others):
+        blocks = [
+            lax.optimization_barrier((mine[k].astype(f32) + other[k].astype(f32)).astype(bf16))
+            for k in range(nz)
+        ]
+        half = blocks[0].astype(f32)
+        for k in range(1, nz):
+            half = half + shift(blocks[k], k).astype(f32)
+        halves.append(half)
+    halves[0], results[-1] = lax.optimization_barrier((halves[0], results[-1]))
+    summed = []
+    for half in halves:
+        r = 1
+        while r < tm_count:
+            mine = lax.optimization_barrier(half.astype(bf16))
+            half = mine.astype(f32) + swap(mine, r).astype(f32)
+            r *= 2
+        summed.append(half)
 
     for c, blocks in enumerate(results):
         mixed, grads = unpack(
@@ -525,9 +577,10 @@
         )
     attended = mixed[:patches].transpose(1, 0, 2)[None]
     tokens_grad = grads[:patches].transpose(1, 0, 2)[None]
-    weight_total = summed[:shard]
-    gain_total = lax.dynamic_slice(summed[shard], (dp * shard,), (shard,))
-    bias_total = lax.dynamic_slice(summed[shard + 1], (dp * shard,), (shard,))
+    rest = shard - summed[0].shape[0]
+    weight_total = jnp.concatenate([summed[0], summed[1][:rest]], axis=0)
+    gain_total = lax.dynamic_slice(summed[1][rest], (dp * shard,), (shard,))
+    bias_total = lax.dynamic_slice(summed[1][rest + 1], (dp * shard,), (shard,))
     return (attended, tokens_grad, weight_total, gain_total, bias_total)
 
 

time: 173 us -> 125 us (0.72)
  waiting for transfers between devices: 68.4 us -> 26.2 us
  Pallas kernels: 62.4 us -> 46.7 us
  starting transfers between devices: 30.3 us -> 43.3 us
  local copies, waits for them, and re-layouts: 6.81 us -> 3.25 us
    ppermute x14 -> x16, waiting for transfers between devices: 30.8 us -> 9.47 us  [swap(): return lax.ppermute(array, 'tm', partner(tm_count, r))]
    ppermute x11 -> x12, waiting for transfers between devices: 37.5 us -> 16.8 us  [the longest x9 16.8 us: shift(): return lax.ppermute(array, 'dp', hops)]
    pallas_call x2, Pallas kernels: 53 us -> 36.5 us  [chunk(): pl.pallas_call(functools.partial(chunk_kernel, tm_count, dp_count, frames...]
    ppermute x11 -> x12, starting transfers between devices: 8.96 us -> 22 us  [the longest x9 21.3 us: shift(): return lax.ppermute(array, 'dp', hops)]
    another operation x0 -> x2, other arithmetic: none -> 2.09 us  [the longest x1 1.41 us: body(): jnp.stack(along)]
    unnamed x52 -> x38, local copies, waits for them, and re-layouts: 3.82 us -> 1.95 us
    ppermute x14 -> x16, starting transfers between devices: 21.3 us -> 21.4 us  [swap(): return lax.ppermute(array, 'tm', partner(tm_count, r))]
  transfers between devices with their start and end apart: 25 -> 28, of which waited for: 11 -> 9; matrix products, arithmetic and copies ran while one was open for 0% -> 0% of each run, Pallas kernels for 20% -> 35%
where the time goes in v3:
time: 125 us
  Pallas kernels  46.7 us (37%)
  starting transfers between devices  43.3 us (35%)
  waiting for transfers between devices  26.2 us (21%)
  other arithmetic  3.41 us (3%)
  local copies, waits for them, and re-layouts  3.25 us (3%)
  between operations  1.65 us (1%)
    pallas_call x2, Pallas kernels, chunk(): pl.pallas_call(functools.partial(chunk_kernel, tm_count, dp_count, frames...  36.5 us
    ppermute x16, starting transfers between devices, swap(): return lax.ppermute(array, 'tm', partner(tm_count, r))  21.4 us
    ppermute x9, starting transfers between devices, shift(): return lax.ppermute(array, 'dp', hops)  21.3 us
    ppermute x9, waiting for transfers between devices, shift(): return lax.ppermute(array, 'dp', hops)  16.8 us
    ppermute x16, waiting for transfers between devices, swap(): return lax.ppermute(array, 'tm', partner(tm_count, r))  9.47 us
    pallas_call x2, Pallas kernels, pack(): pl.pallas_call(functools.partial(pack_kernel, tm_count, patches_dev, offs...  5.75 us
    pallas_call x2, Pallas kernels, unpack(): pl.pallas_call(functools.partial(unpack_kernel, tm_count, patches_dev, of...  4.46 us
  transfers between devices with their start and end apart: 28, of which 9 were waited for; matrix products, arithmetic and copies ran while one was open for 0% of the time, Pallas kernels for 35%

profile of v3, /device:TPU:0, one launch (start us, length us, event | category | flops | bytes accessed | tf_op | source)
XLA Modules:
  0.0 124.6 jit_solution(4345254287489613750)
XLA Ops:
  2.0 3.3 %shard_map.119 = (bf16[112,1152]{1,0:T(8,128)(2,1)}, bf16[24,8,1152]{2,1,0:T(8,128)(2,1)}, bf16[24,8,1152]{2,1,0:T(8,128)(2,1)}, bf16[24,8,1152]{2,1,0:T(8,128)(2,1)}) custom-call(bf16[196,8,768]{2,1,0:T(8,128)(2,1)} %bitcast.38, bf16[196,8,384]{2,1,0:T(8,128)(2,1)} %bitcast.43, bf16[96,1152]{1,0:T(8,128)(2,1)} %rest_0_.1, bf16[2,1152]{1,0:T(2,128)(2,1)} %tile.10.rest_1_), custom_call_target="tpu_custom_call" | custom-call | tf_op jit(solution)/shard_map/pallas_call | solution.py:87
  5.3 3.1 %collective-permute-start = (bf16[112,1152]{1,0:T(8,128)(2,1)}, bf16[112,1152]{1,0:T(8,128)(2,1)S(1)}, u32[]{:S(2)}, u32[]{:S(2)}) collective-permute-start(bf16[112,1152]{1,0:T(8,128)(2,1)} %get-tuple-element.52.rest_0_), channel_id=1, source_target_pairs={{0,8},{4,12},{8,16},{12,20},{16,24},{20,28},{24,0},{28,4},{1,9},{5... | collective-permute-start | bytes 774152 | tf_op jit(solution)/shard_map/ppermute | solution.py:515
  11.8 2.6 %collective-permute-start.1 = (bf16[112,1152]{1,0:T(8,128)(2,1)}, bf16[112,1152]{1,0:T(8,128)(2,1)S(1)}, u32[]{:S(2)}, u32[]{:S(2)}) collective-permute-start(bf16[112,1152]{1,0:T(8,128)(2,1)} %get-tuple-element.52.rest_0_), channel_id=1, source_target_pairs={{0,16},{4,20},{8,24},{12,28},{16,0},{20,4},{24,8},{28,12},{1,17},{... | collective-permute-start | bytes 774152 | tf_op jit(solution)/shard_map/ppermute | solution.py:515
  14.4 3.3 %collective-permute-done.rest_1_ = bf16[112,1152]{1,0:T(8,128)(2,1)S(1)} collective-permute-done((bf16[112,1152]{1,0:T(8,128)(2,1)}, bf16[112,1152]{1,0:T(8,128)(2,1)S(1)}, u32[]{:S(2)}, u32[]{:S(2)}) %collective-permute-start) | collective-permute-done | bytes 258080 | tf_op jit(solution)/shard_map/ppermute | solution.py:515
  19.1 8.8 %collective-permute-done.1.rest_2_ = bf16[112,1152]{1,0:T(8,128)(2,1)S(1)} collective-permute-done((bf16[112,1152]{1,0:T(8,128)(2,1)}, bf16[112,1152]{1,0:T(8,128)(2,1)S(1)}, u32[]{:S(2)}, u32[]{:S(2)}) %collective-permute-start.1) | collective-permute-done | bytes 258080 | tf_op jit(solution)/shard_map/ppermute | solution.py:515
  28.0 4.5 %collective-permute-done.2.rest_3_ = bf16[112,1152]{1,0:T(8,128)(2,1)S(1)} collective-permute-done((bf16[112,1152]{1,0:T(8,128)(2,1)}, bf16[112,1152]{1,0:T(8,128)(2,1)S(1)}, u32[]{:S(2)}, u32[]{:S(2)}) %collective-permute-start.2) | collective-permute-done | bytes 258080 | tf_op jit(solution)/shard_map/ppermute | solution.py:515
  34.0 2.5 %shard_map.120 = (bf16[25,8,1152]{2,1,0:T(8,128)(2,1)}, bf16[25,8,1152]{2,1,0:T(8,128)(2,1)}, bf16[25,8,1152]{2,1,0:T(8,128)(2,1)}) custom-call(bf16[196,8,768]{2,1,0:T(8,128)(2,1)} %bitcast.39, bf16[196,8,384]{2,1,0:T(8,128)(2,1)} %bitcast.44), custom_call_target="tpu_custom_call" | custom-call | tf_op jit(solution)/shard_map/pallas_call | solution.py:87
  36.5 1.6 %collective-permute-start.7 = (bf16[25,8,1152]{2,1,0:T(8,128)(2,1)}, bf16[25,8,1152]{2,1,0:T(8,128)(2,1)S(1)}, u32[]{:S(2)}, u32[]{:S(2)}) collective-permute-start(bf16[25,8,1152]{2,1,0:T(8,128)(2,1)} %get-tuple-element.56), channel_id=1, source_target_pairs={{0,1},{1,0},{2,3},{3,2},{4,5},{5,4},{6,7},{7,6},{8,9},{9,8},{10,11... | collective-permute-start | bytes 1382408 | tf_op jit(solution)/shard_map/ppermute | solution.py:505
  41.8 16.4 %shard_map.121 = (bf16[24,8,1152]{2,1,0:T(8,128)(2,1)}, bf16[24,8,1152]{2,1,0:T(8,128)(2,1)}, bf16[24,8,1152]{2,1,0:T(8,128)(2,1)}, bf16[196,8,384]{2,1,0:T(8,12...) custom-call(s32[1]{0:T(128)S(6)} %copy.25.count_ref, s32[1,2]{1,0:T(1,128)} %starts_ref.3, ...), custom_call_target="tpu_custom_call" | custom-call | tf_op jit(solution)/shard_map/pallas_call | solution.py:458
  58.2 1.6 %collective-permute-start.10 = (bf16[24,8,1152]{2,1,0:T(8,128)(2,1)}, bf16[24,8,1152]{2,1,0:T(8,128)(2,1)S(1)}, u32[]{:S(2)}, u32[]{:S(2)}) collective-permute-start(bf16[24,8,1152]{2,1,0:T(8,128)(2,1)} %get-tuple-element.70), channel_id=1, source_target_pairs={{0,1},{1,0},{2,3},{3,2},{4,5},{5,4},{6,7},{7,6},{8,9},{9,8},{10,11... | collective-permute-start | bytes 1327112 | tf_op jit(solution)/shard_map/ppermute | solution.py:505
  62.6 20.1 %shard_map.122 = (bf16[25,8,1152]{2,1,0:T(8,128)(2,1)}, bf16[25,8,1152]{2,1,0:T(8,128)(2,1)}, bf16[25,8,1152]{2,1,0:T(8,128)(2,1)}, bf16[196,8,384]{2,1,0:T(8,12...) custom-call(s32[1]{0:T(128)S(6)} %copy.25.count_ref, ...), custom_call_target="tpu_custom_call", output_to_operand_aliasing={{3}: (15, {}), {4}: (16, {})} | custom-call | tf_op jit(solution)/shard_map/pallas_call | solution.py:458
  86.4 2.3 %shard_map.123 = (bf16[196,8,384]{2,1,0:T(8,128)(2,1)}, bf16[196,8,768]{2,1,0:T(8,128)(2,1)}) custom-call(bf16[196,8,384]{2,1,0:T(8,128)(2,1)} %get-tuple-element.66.refs_0_, bf16[196,8,768]{2,1,0:T(8,128)(2,1)} %get-tuple-element.67.refs_1_, bf16[24,8,1152]{2,1,0:T(8,128)(2,1)} %copy-done.11, ...), custom_call_target="tpu_custom_call", output_to_operand_aliasing={{0}: (0, {}), {1}: (1, {})} | custom-call | tf_op jit(solution)/shard_map/pallas_call | solution.py:120
  88.8 2.4 %collective-permute-start.14 = (bf16[48,1152]{1,0:T(8,128)(2,1)S(1)}, bf16[48,1152]{1,0:T(8,128)(2,1)S(1)}, u32[]{:S(2)}, u32[]{:S(2)}) collective-permute-start(bf16[48,1152]{1,0:T(8,128)(2,1)S(1)} %get-tuple-element.98), channel_id=1, source_target_pairs={{0,8},{4,12},{8,16},{12,20},{16,24},{20,28},{24,0},{28,4},{1,9},{5... | collective-permute-start | bytes 331784 | tf_op jit(solution)/shard_map/ppermute | solution.py:515
  91.2 1.5 %collective-permute-start.15 = (bf16[48,1152]{1,0:T(8,128)(2,1)S(1)}, bf16[48,1152]{1,0:T(8,128)(2,1)S(1)}, u32[]{:S(2)}, u32[]{:S(2)}) collective-permute-start(bf16[48,1152]{1,0:T(8,128)(2,1)S(1)} %get-tuple-element.97), channel_id=1, source_target_pairs={{0,16},{4,20},{8,24},{12,28},{16,0},{20,4},{24,8},{28,12},{1,17},{... | collective-permute-start | bytes 331784 | tf_op jit(solution)/shard_map/ppermute | solution.py:515
  92.8 2.8 %collective-permute-start.16 = (bf16[48,1152]{1,0:T(8,128)(2,1)S(1)}, bf16[48,1152]{1,0:T(8,128)(2,1)S(1)}, u32[]{:S(2)}, u32[]{:S(2)}) collective-permute-start(bf16[48,1152]{1,0:T(8,128)(2,1)S(1)} %get-tuple-element.96), channel_id=1, source_target_pairs={{0,24},{4,28},{8,0},{12,4},{16,8},{20,12},{24,16},{28,20},{1,25},{... | collective-permute-start | bytes 331784 | tf_op jit(solution)/shard_map/ppermute | solution.py:515
  96.1 2.5 %collective-permute-start.19 = (bf16[25,8,1152]{2,1,0:T(8,128)(2,1)S(1)}, bf16[25,8,1152]{2,1,0:T(8,128)(2,1)S(1)}, u32[]{:S(2)}, u32[]{:S(2)}) collective-permute-start(bf16[25,8,1152]{2,1,0:T(8,128)(2,1)S(1)} %copy-done.18), channel_id=1, source_target_pairs={{0,3},{1,2},{2,1},{3,0},{4,7},{5,6},{6,5},{7,4},{8,11},{9,10},{10,... | collective-permute-start | bytes 1382408 | tf_op jit(solution)/shard_map/ppermute | solution.py:505
  98.6 2.6 %collective-permute-start.23 = (bf16[64,1152]{1,0:T(8,128)(2,1)S(1)}, bf16[64,1152]{1,0:T(8,128)(2,1)S(1)}, u32[]{:S(2)}, u32[]{:S(2)}) collective-permute-start(bf16[64,1152]{1,0:T(8,128)(2,1)S(1)} %get-tuple-element.94), channel_id=1, source_target_pairs={{0,8},{4,12},{8,16},{12,20},{16,24},{20,28},{24,0},{28,4},{1,9},{5... | collective-permute-start | bytes 442376 | tf_op jit(solution)/shard_map/ppermute | solution.py:515
  101.2 1.9 %collective-permute-start.24 = (bf16[64,1152]{1,0:T(8,128)(2,1)S(1)}, bf16[64,1152]{1,0:T(8,128)(2,1)S(1)}, u32[]{:S(2)}, u32[]{:S(2)}) collective-permute-start(bf16[64,1152]{1,0:T(8,128)(2,1)S(1)} %get-tuple-element.93), channel_id=1, source_target_pairs={{0,16},{4,20},{8,24},{12,28},{16,0},{20,4},{24,8},{28,12},{1,17},{... | collective-permute-start | bytes 442376 | tf_op jit(solution)/shard_map/ppermute | solution.py:515
  103.1 2.9 %collective-permute-start.25 = (bf16[64,1152]{1,0:T(8,128)(2,1)S(1)}, bf16[64,1152]{1,0:T(8,128)(2,1)S(1)}, u32[]{:S(2)}, u32[]{:S(2)}) collective-permute-start(bf16[64,1152]{1,0:T(8,128)(2,1)S(1)} %get-tuple-element.92), channel_id=1, source_target_pairs={{0,24},{4,28},{8,0},{12,4},{16,8},{20,12},{24,16},{28,20},{1,25},{... | collective-permute-start | bytes 442376 | tf_op jit(solution)/shard_map/ppermute | solution.py:515
  106.1 2.6 %collective-permute-done.19.refs_4_ = bf16[25,8,1152]{2,1,0:T(8,128)(2,1)S(1)} collective-permute-done((bf16[25,8,1152]{2,1,0:T(8,128)(2,1)S(1)}, bf16[25,8,1152]{2,1,0:T(8,128)(2,1)S(1)}, u32[]{:S(2)}, u32[]{:S(2)}) %collective-permute-start.19) | collective-permute-done | bytes 460832 | tf_op jit(solution)/shard_map/ppermute | solution.py:505
  110.2 2.2 %shard_map.124 = (bf16[196,8,384]{2,1,0:T(8,128)(2,1)}, bf16[196,8,768]{2,1,0:T(8,128)(2,1)}) custom-call(bf16[196,8,384]{2,1,0:T(8,128)(2,1)} %get-tuple-element.76.refs_0_, bf16[196,8,768]{2,1,0:T(8,128)(2,1)} %get-tuple-element.77.refs_1_, bf16[25,8,1152]{2,1,0:T(8,128)(2,1)} %copy-done.8, ...), custom_call_target="tpu_custom_call", output_to_operand_aliasing={{0}: (0, {}), {1}: (1, {})} | custom-call | tf_op jit(solution)/shard_map/pallas_call | solution.py:120
  113.5 1.6 %collective-permute-start.21 = (bf16[48,1152]{1,0:T(8,128)(2,1)S(1)}, bf16[48,1152]{1,0:T(8,128)(2,1)S(1)}, u32[]{:S(2)}, u32[]{:S(2)}) collective-permute-start(bf16[48,1152]{1,0:T(8,128)(2,1)S(1)} %add_convert_fusion.6), channel_id=1, source_target_pairs={{0,2},{1,3},{2,0},{3,1},{4,6},{5,7},{6,4},{7,5},{8,10},{9,11},{10,... | collective-permute-start | bytes 331784 | tf_op jit(solution)/shard_map/ppermute | solution.py:505
  115.1 2.8 %collective-permute-done.26 = bf16[64,1152]{1,0:T(8,128)(2,1)S(1)} collective-permute-done((bf16[64,1152]{1,0:T(8,128)(2,1)S(1)}, bf16[64,1152]{1,0:T(8,128)(2,1)S(1)}, u32[]{:S(2)}, u32[]{:S(2)}) %collective-permute-start.26) | collective-permute-done | bytes 147488 | tf_op jit(solution)/shard_map/ppermute | solution.py:505
  119.4 3.7 %collective-permute-done.27 = bf16[64,1152]{1,0:T(8,128)(2,1)S(1)} collective-permute-done((bf16[64,1152]{1,0:T(8,128)(2,1)S(1)}, bf16[64,1152]{1,0:T(8,128)(2,1)S(1)}, u32[]{:S(2)}, u32[]{:S(2)}) %collective-permute-start.27) | collective-permute-done | bytes 147488 | tf_op jit(solution)/shard_map/ppermute | solution.py:505
  (92 shorter events, 23.5 us)
Async XLA Ops:
  5.3 12.5 %collective-permute-start = (bf16[112,1152]{1,0:T(8,128)(2,1)}, bf16[112,1152]{1,0:T(8,128)(2,1)S(1)}, u32[]{:S(2)}, u32[]{:S(2)}) collective-permute-start(bf16[112,1152]{1,0:T(8,128)(2,1)} %get-tuple-element.52.rest_0_), channel_id=1, source_target_pairs={{0,8},{4,12},{8,16},{12,20},{16,24},{20,28},{24,0},{28,4},{1,9},{5... | collective-permute-start | bytes 774152 | tf_op jit(solution)/shard_map/ppermute | solution.py:515
  8.4 24.1 %collective-permute-start.3 = (bf16[24,8,1152]{2,1,0:T(8,128)(2,1)}, bf16[24,8,1152]{2,1,0:T(8,128)(2,1)S(1)}, u32[]{:S(2)}, u32[]{:S(2)}) collective-permute-start(bf16[24,8,1152]{2,1,0:T(8,128)(2,1)} %get-tuple-element.49), channel_id=1, source_target_pairs={{0,1},{1,0},{2,3},{3,2},{4,5},{5,4},{6,7},{7,6},{8,9},{9,8},{10,11... | collective-permute-start | bytes 1327112 | tf_op jit(solution)/shard_map/ppermute | solution.py:505
  9.8 22.6 %collective-permute-start.4 = (bf16[24,8,1152]{2,1,0:T(8,128)(2,1)}, bf16[24,8,1152]{2,1,0:T(8,128)(2,1)S(1)}, u32[]{:S(2)}, u32[]{:S(2)}) collective-permute-start(bf16[24,8,1152]{2,1,0:T(8,128)(2,1)} %get-tuple-element.50), channel_id=1, source_target_pairs={{0,2},{1,3},{2,0},{3,1},{4,6},{5,7},{6,4},{7,5},{8,10},{9,11},{10,... | collective-permute-start | bytes 1327112 | tf_op jit(solution)/shard_map/ppermute | solution.py:505
  11.4 21.1 %collective-permute-start.5 = (bf16[24,8,1152]{2,1,0:T(8,128)(2,1)}, bf16[24,8,1152]{2,1,0:T(8,128)(2,1)S(1)}, u32[]{:S(2)}, u32[]{:S(2)}) collective-permute-start(bf16[24,8,1152]{2,1,0:T(8,128)(2,1)} %get-tuple-element.51), channel_id=1, source_target_pairs={{0,3},{1,2},{2,1},{3,0},{4,7},{5,6},{6,5},{7,4},{8,11},{9,10},{10,... | collective-permute-start | bytes 1327112 | tf_op jit(solution)/shard_map/ppermute | solution.py:505
  11.8 16.1 %collective-permute-start.1 = (bf16[112,1152]{1,0:T(8,128)(2,1)}, bf16[112,1152]{1,0:T(8,128)(2,1)S(1)}, u32[]{:S(2)}, u32[]{:S(2)}) collective-permute-start(bf16[112,1152]{1,0:T(8,128)(2,1)} %get-tuple-element.52.rest_0_), channel_id=1, source_target_pairs={{0,16},{4,20},{8,24},{12,28},{16,0},{20,4},{24,8},{28,12},{1,17},{... | collective-permute-start | bytes 774152 | tf_op jit(solution)/shard_map/ppermute | solution.py:515
  17.7 14.7 %collective-permute-start.2 = (bf16[112,1152]{1,0:T(8,128)(2,1)}, bf16[112,1152]{1,0:T(8,128)(2,1)S(1)}, u32[]{:S(2)}, u32[]{:S(2)}) collective-permute-start(bf16[112,1152]{1,0:T(8,128)(2,1)} %get-tuple-element.52.rest_0_), channel_id=1, source_target_pairs={{0,24},{4,28},{8,0},{12,4},{16,8},{20,12},{24,16},{28,20},{1,25},{... | collective-permute-start | bytes 774152 | tf_op jit(solution)/shard_map/ppermute | solution.py:515
  33.9 6.8 %collective-permute-start.6 = (bf16[4,112,1152]{2,1,0:T(8,128)(2,1)S(1)}, bf16[4,112,1152]{2,1,0:T(8,128)(2,1)S(1)}, u32[]{:S(2)}, u32[]{:S(2)}) collective-permute-start(bf16[4,112,1152]{2,1,0:T(8,128)(2,1)S(1)} %pad_maximum_fusion), channel_id=1, source_target_pairs={{0,4},{4,0},{8,12},{12,8},{16,20},{20,16},{24,28},{28,24},{1,5},{5... | collective-permute-start | bytes 3096584 | tf_op jit(solution)/shard_map/ppermute | solution.py:527
  36.5 24.7 %collective-permute-start.7 = (bf16[25,8,1152]{2,1,0:T(8,128)(2,1)}, bf16[25,8,1152]{2,1,0:T(8,128)(2,1)S(1)}, u32[]{:S(2)}, u32[]{:S(2)}) collective-permute-start(bf16[25,8,1152]{2,1,0:T(8,128)(2,1)} %get-tuple-element.56), channel_id=1, source_target_pairs={{0,1},{1,0},{2,3},{3,2},{4,5},{5,4},{6,7},{7,6},{8,9},{9,8},{10,11... | collective-permute-start | bytes 1382408 | tf_op jit(solution)/shard_map/ppermute | solution.py:505
  38.1 23.6 %collective-permute-start.8 = (bf16[25,8,1152]{2,1,0:T(8,128)(2,1)}, bf16[25,8,1152]{2,1,0:T(8,128)(2,1)S(1)}, u32[]{:S(2)}, u32[]{:S(2)}) collective-permute-start(bf16[25,8,1152]{2,1,0:T(8,128)(2,1)} %get-tuple-element.57), channel_id=1, source_target_pairs={{0,2},{1,3},{2,0},{3,1},{4,6},{5,7},{6,4},{7,5},{8,10},{9,11},{10,... | collective-permute-start | bytes 1382408 | tf_op jit(solution)/shard_map/ppermute | solution.py:505
  39.6 22.1 %collective-permute-start.9 = (bf16[25,8,1152]{2,1,0:T(8,128)(2,1)}, bf16[25,8,1152]{2,1,0:T(8,128)(2,1)S(1)}, u32[]{:S(2)}, u32[]{:S(2)}) collective-permute-start(bf16[25,8,1152]{2,1,0:T(8,128)(2,1)} %get-tuple-element.58), channel_id=1, source_target_pairs={{0,3},{1,2},{2,1},{3,0},{4,7},{5,6},{6,5},{7,4},{8,11},{9,10},{10,... | collective-permute-start | bytes 1382408 | tf_op jit(solution)/shard_map/ppermute | solution.py:505
  58.2 24.6 %collective-permute-start.10 = (bf16[24,8,1152]{2,1,0:T(8,128)(2,1)}, bf16[24,8,1152]{2,1,0:T(8,128)(2,1)S(1)}, u32[]{:S(2)}, u32[]{:S(2)}) collective-permute-start(bf16[24,8,1152]{2,1,0:T(8,128)(2,1)} %get-tuple-element.70), channel_id=1, source_target_pairs={{0,1},{1,0},{2,3},{3,2},{4,5},{5,4},{6,7},{7,6},{8,9},{9,8},{10,11... | collective-permute-start | bytes 1327112 | tf_op jit(solution)/shard_map/ppermute | solution.py:505
  59.7 23.0 %collective-permute-start.11 = (bf16[24,8,1152]{2,1,0:T(8,128)(2,1)}, bf16[24,8,1152]{2,1,0:T(8,128)(2,1)S(1)}, u32[]{:S(2)}, u32[]{:S(2)}) collective-permute-start(bf16[24,8,1152]{2,1,0:T(8,128)(2,1)} %get-tuple-element.71), channel_id=1, source_target_pairs={{0,2},{1,3},{2,0},{3,1},{4,6},{5,7},{6,4},{7,5},{8,10},{9,11},{10,... | collective-permute-start | bytes 1327112 | tf_op jit(solution)/shard_map/ppermute | solution.py:505
  61.2 21.5 %collective-permute-start.12 = (bf16[24,8,1152]{2,1,0:T(8,128)(2,1)}, bf16[24,8,1152]{2,1,0:T(8,128)(2,1)S(1)}, u32[]{:S(2)}, u32[]{:S(2)}) collective-permute-start(bf16[24,8,1152]{2,1,0:T(8,128)(2,1)} %get-tuple-element.72), channel_id=1, source_target_pairs={{0,3},{1,2},{2,1},{3,0},{4,7},{5,6},{6,5},{7,4},{8,11},{9,10},{10,... | collective-permute-start | bytes 1327112 | tf_op jit(solution)/shard_map/ppermute | solution.py:505
  82.8 5.9 %collective-permute-start.13 = (bf16[4,48,1152]{2,1,0:T(8,128)(2,1)}, bf16[4,48,1152]{2,1,0:T(8,128)(2,1)S(1)}, u32[]{:S(2)}, u32[]{:S(2)}) collective-permute-start(bf16[4,48,1152]{2,1,0:T(8,128)(2,1)} %get-tuple-element.79), channel_id=1, source_target_pairs={{0,4},{4,0},{8,12},{12,8},{16,20},{20,16},{24,28},{28,24},{1,5},{5... | collective-permute-start | bytes 1327112 | tf_op jit(solution)/shard_map/ppermute | solution.py:553
  82.9 9.9 %collective-permute-start.22 = (bf16[4,64,1152]{2,1,0:T(8,128)(2,1)}, bf16[4,64,1152]{2,1,0:T(8,128)(2,1)S(1)}, u32[]{:S(2)}, u32[]{:S(2)}) collective-permute-start(bf16[4,64,1152]{2,1,0:T(8,128)(2,1)} %get-tuple-element.90), channel_id=1, source_target_pairs={{0,4},{4,0},{8,12},{12,8},{16,20},{20,16},{24,28},{28,24},{1,5},{5... | collective-permute-start | bytes 1769480 | tf_op jit(solution)/shard_map/ppermute | solution.py:553
  83.4 12.8 %collective-permute-start.17 = (bf16[25,8,1152]{2,1,0:T(8,128)(2,1)}, bf16[25,8,1152]{2,1,0:T(8,128)(2,1)S(1)}, u32[]{:S(2)}, u32[]{:S(2)}) collective-permute-start(bf16[25,8,1152]{2,1,0:T(8,128)(2,1)} %get-tuple-element.80), channel_id=1, source_target_pairs={{0,1},{1,0},{2,3},{3,2},{4,5},{5,4},{6,7},{7,6},{8,9},{9,8},{10,11... | collective-permute-start | bytes 1382408 | tf_op jit(solution)/shard_map/ppermute | solution.py:505
  84.9 21.3 %collective-permute-start.18 = (bf16[25,8,1152]{2,1,0:T(8,128)(2,1)}, bf16[25,8,1152]{2,1,0:T(8,128)(2,1)S(1)}, u32[]{:S(2)}, u32[]{:S(2)}) collective-permute-start(bf16[25,8,1152]{2,1,0:T(8,128)(2,1)} %get-tuple-element.81), channel_id=1, source_target_pairs={{0,2},{1,3},{2,0},{3,1},{4,6},{5,7},{6,4},{7,5},{8,10},{9,11},{10,... | collective-permute-start | bytes 1382408 | tf_op jit(solution)/shard_map/ppermute | solution.py:505
  88.8 9.8 %collective-permute-start.14 = (bf16[48,1152]{1,0:T(8,128)(2,1)S(1)}, bf16[48,1152]{1,0:T(8,128)(2,1)S(1)}, u32[]{:S(2)}, u32[]{:S(2)}) collective-permute-start(bf16[48,1152]{1,0:T(8,128)(2,1)S(1)} %get-tuple-element.98), channel_id=1, source_target_pairs={{0,8},{4,12},{8,16},{12,20},{16,24},{20,28},{24,0},{28,4},{1,9},{5... | collective-permute-start | bytes 331784 | tf_op jit(solution)/shard_map/ppermute | solution.py:515
  91.2 10.0 %collective-permute-start.15 = (bf16[48,1152]{1,0:T(8,128)(2,1)S(1)}, bf16[48,1152]{1,0:T(8,128)(2,1)S(1)}, u32[]{:S(2)}, u32[]{:S(2)}) collective-permute-start(bf16[48,1152]{1,0:T(8,128)(2,1)S(1)} %get-tuple-element.97), channel_id=1, source_target_pairs={{0,16},{4,20},{8,24},{12,28},{16,0},{20,4},{24,8},{28,12},{1,17},{... | collective-permute-start | bytes 331784 | tf_op jit(solution)/shard_map/ppermute | solution.py:515
  92.8 10.3 %collective-permute-start.16 = (bf16[48,1152]{1,0:T(8,128)(2,1)S(1)}, bf16[48,1152]{1,0:T(8,128)(2,1)S(1)}, u32[]{:S(2)}, u32[]{:S(2)}) collective-permute-start(bf16[48,1152]{1,0:T(8,128)(2,1)S(1)} %get-tuple-element.96), channel_id=1, source_target_pairs={{0,24},{4,28},{8,0},{12,4},{16,8},{20,12},{24,16},{28,20},{1,25},{... | collective-permute-start | bytes 331784 | tf_op jit(solution)/shard_map/ppermute | solution.py:515
  96.1 12.6 %collective-permute-start.19 = (bf16[25,8,1152]{2,1,0:T(8,128)(2,1)S(1)}, bf16[25,8,1152]{2,1,0:T(8,128)(2,1)S(1)}, u32[]{:S(2)}, u32[]{:S(2)}) collective-permute-start(bf16[25,8,1152]{2,1,0:T(8,128)(2,1)S(1)} %copy-done.18), channel_id=1, source_target_pairs={{0,3},{1,2},{2,1},{3,0},{4,7},{5,6},{6,5},{7,4},{8,11},{9,10},{10,... | collective-permute-start | bytes 1382408 | tf_op jit(solution)/shard_map/ppermute | solution.py:505
  98.6 13.9 %collective-permute-start.23 = (bf16[64,1152]{1,0:T(8,128)(2,1)S(1)}, bf16[64,1152]{1,0:T(8,128)(2,1)S(1)}, u32[]{:S(2)}, u32[]{:S(2)}) collective-permute-start(bf16[64,1152]{1,0:T(8,128)(2,1)S(1)} %get-tuple-element.94), channel_id=1, source_target_pairs={{0,8},{4,12},{8,16},{12,20},{16,24},{20,28},{24,0},{28,4},{1,9},{5... | collective-permute-start | bytes 442376 | tf_op jit(solution)/shard_map/ppermute | solution.py:515
  101.2 11.2 %collective-permute-start.24 = (bf16[64,1152]{1,0:T(8,128)(2,1)S(1)}, bf16[64,1152]{1,0:T(8,128)(2,1)S(1)}, u32[]{:S(2)}, u32[]{:S(2)}) collective-permute-start(bf16[64,1152]{1,0:T(8,128)(2,1)S(1)} %get-tuple-element.93), channel_id=1, source_target_pairs={{0,16},{4,20},{8,24},{12,28},{16,0},{20,4},{24,8},{28,12},{1,17},{... | collective-permute-start | bytes 442376 | tf_op jit(solution)/shard_map/ppermute | solution.py:515
  103.1 9.4 %collective-permute-start.25 = (bf16[64,1152]{1,0:T(8,128)(2,1)S(1)}, bf16[64,1152]{1,0:T(8,128)(2,1)S(1)}, u32[]{:S(2)}, u32[]{:S(2)}) collective-permute-start(bf16[64,1152]{1,0:T(8,128)(2,1)S(1)} %get-tuple-element.92), channel_id=1, source_target_pairs={{0,24},{4,28},{8,0},{12,4},{16,8},{20,12},{24,16},{28,20},{1,25},{... | collective-permute-start | bytes 442376 | tf_op jit(solution)/shard_map/ppermute | solution.py:515
  (23 other events, 117.6 us)

commit v4 on v3

--- a/solution.py
+++ b/solution.py
@@ -10,7 +10,7 @@
 HEADS = 6
 BLOCK = 16
 CORES = 2
-EXTRA = 16
+EXTRA = 8
 
 masked_value = -1e30
 epsilon = 1e-05
@@ -19,21 +19,22 @@
 bf16 = jnp.bfloat16
 
 
+def halving_order(count):
+    order, bit = [0], count // 2
+    while bit:
+        order = order + [bit + k for k in order]
+        bit //= 2
+    return order
+
+
 def round_up(value, step):
     return -(-value // step) * step
 
 
-def chunk_sizes(patches_dev, group, count):
-    groups = -(-patches_dev // group)
-    count = min(count, groups)
-    sizes = []
-    left = patches_dev
-    for index in range(count - 1):
-        taken = (groups // count) * group
-        sizes.append(taken)
-        left -= taken
-    sizes.append(left)
-    return sizes
+def chunk_sizes(patches_dev, group):
+    whole = patches_dev // group
+    second = (whole // 2) * group
+    return [patches_dev - second, second]
 
 
 anywhere = pl.BlockSpec(memory_space=pl.ANY)
@@ -59,29 +60,31 @@
             (grad_ref.at[place], outs[r - 1].at[:, :, pl.ds(width, grad_ref.shape[2])])
         )
     if len(rest) > tm_count:
-        weight_ref, lines_ref, own_ref = rest[:3]
+        weight_ref, gain_ref, bias_ref, own_ref = rest[:4]
         shard, columns = weight_ref.shape
         pairs.append((weight_ref, own_ref.at[pl.ds(0, shard)]))
     copies = run_all(pairs, sems)
     if len(rest) > tm_count:
-        owner = lax.broadcasted_iota(jnp.int32, lines_ref.shape, 1) // shard
-        lines = jnp.where(owner == lax.axis_index("dp"), lines_ref[...].astype(f32), 0.0)
-        own_ref[shard:, :] = jnp.concatenate(
-            [lines, jnp.zeros((EXTRA - lines.shape[0], columns), f32)], axis=0
-        ).astype(bf16)
+        row = lax.broadcasted_iota(jnp.int32, (EXTRA, columns), 0)
+        owner = lax.broadcasted_iota(jnp.int32, (EXTRA, columns), 1) // shard
+        spread = lambda ref: jnp.concatenate(
+            [ref[...].astype(f32).reshape(1, shard)] * (columns // shard), axis=1
+        )
+        lines = jnp.where(row == 0, spread(gain_ref), jnp.where(row == 1, spread(bias_ref), 0.0))
+        own_ref[shard:, :] = jnp.where(owner == lax.axis_index("dp"), lines, 0.0).astype(bf16)
     for copy in copies:
         copy.wait()
 
 
-def pack(tm_count, patches_dev, offset, size, tokens, grads, weight=None, lines=None):
+def pack(tm_count, patches_dev, offset, size, tokens, grads, weight=None, gain=None, bias=None):
     _, frames, width = tokens.shape
     total = width + grads.shape[2]
     in_vmem = pl.BlockSpec(memory_space=pltpu.VMEM)
     args, specs = [tokens, grads], [anywhere] * 2
     outs = [jax.ShapeDtypeStruct((size, frames, total), bf16)] * (tm_count - 1)
     if weight is not None:
-        args += [weight, lines]
-        specs += [anywhere, in_vmem]
+        args += [weight, gain, bias]
+        specs += [anywhere, in_vmem, in_vmem]
         shard, columns = weight.shape
         outs = [jax.ShapeDtypeStruct((shard + EXTRA, columns), bf16)] + outs
     return pl.pallas_call(
@@ -200,16 +203,14 @@
         bring(grad_ref.at[mine], xs.at[0, kept, :, pl.ds(width, joined)]),
     ]
     rows_in += [bring(sources[r - 1], xs.at[r, kept]) for r in range(1, tm_count)]
-    weights_in = []
+    weights_in, lines_in = [], []
     for side in range(CORES):
         for k in range(nz):
             owner = lax.rem(z + nz - k, nz) * CORES + (core ^ side)
             piece = pieces[k] if side == 0 else pieces[nz].at[k]
             place = pl.ds(pl.multiple_of(owner * shard, shard), shard)
             weights_in.append(bring(piece.at[pl.ds(0, shard)], weight.at[place]))
-            weights_in.append(
-                bring(piece.at[pl.ds(shard, EXTRA)], extra.at[side * nz + k])
-            )
+            lines_in.append(bring(piece.at[pl.ds(shard, EXTRA)], extra.at[side * nz + k]))
     if not first:
         acc_in = [bring(before, acc), bring(before_ends, tails)]
     if xs.shape[1] > size:
@@ -228,7 +229,7 @@
     token_frame = (me ^ (token // span)) * frames + token % frames
     token_valid = token_frame < count_ref[0]
 
-    for copy in weights_in:
+    for copy in lines_in:
         copy.wait()
     gain = functools.reduce(
         lambda a, b: a + b, [extra[i, 0:1, :width].astype(f32) for i in range(dp_count)]
@@ -264,6 +265,8 @@
         ends[at, :] = jnp.broadcast_to(inverse, (unit, 128))
         normed[at, :] = (std * gain + bias).astype(bf16)
 
+    for copy in weights_in:
+        copy.wait()
     for part in range(3):
         cut = slice(part * joined, (part + 1) * joined)
         proj[:, cut] = jnp.dot(
@@ -394,8 +397,8 @@
             ],
             axis=0,
         ).astype(bf16)
-        for k in range(nz):
-            owner = lax.rem(z + k, nz) * CORES
+        for k, far in enumerate(halving_order(nz)):
+            owner = (z ^ far) * CORES
             for refs, side in ((sums[:2], core), (sums[2:], 1 - core)):
                 start = pl.multiple_of((owner + side) * shard, shard)
                 refs[0][k] = acc[pl.ds(start, cut), :].astype(bf16)
@@ -498,7 +501,7 @@
     shard, columns = qkv_weight.shape
     patches_dev = -(-patches // tm_count)
     group = max(2, 128 // (frames * tm_count))
-    chunks = chunk_sizes(patches_dev, group, 2)
+    chunks = chunk_sizes(patches_dev, group)
     dp = lax.axis_index("dp")
 
     def swap(array, r):
@@ -508,28 +511,27 @@
     tokens = jnp.pad(video_tokens[0].transpose(1, 0, 2), spare)
     upstream = jnp.pad(attended_grad[0].transpose(1, 0, 2), spare)
     offsets = [sum(chunks[:c]) for c in range(len(chunks))]
-    lines = jnp.tile(jnp.stack([norm_gain, norm_bias]), (1, -(-columns // shard)))[:, :columns]
 
     def shift(array, k):
         hops = [(i, (i + CORES * k) % dp_count) for i in range(dp_count)]
         return lax.ppermute(array, "dp", hops)
 
-    gathered = []
-    for c, size in enumerate(chunks):
-        more = (qkv_weight, lines) if c == 0 else ()
-        blocks = pack(tm_count, patches_dev, offsets[c], size, tokens, upstream, *more)
-        if c == 0:
-            along = [blocks[0]] + [shift(blocks[0], k) for k in range(1, nz)]
-            blocks = blocks[1:]
-        blocks = [swap(part, r + 1) for r, part in enumerate(blocks)]
-        if c == 0:
-            along, blocks = lax.optimization_barrier((along, blocks))
-            pieces = along + [lax.ppermute(jnp.stack(along), "dp", partner(dp_count, 1))]
-        gathered.append(blocks)
+    blocks = [
+        pack(tm_count, patches_dev, offset, size, tokens, upstream, *more)
+        for offset, size, more in zip(offsets, chunks, ((qkv_weight, norm_gain, norm_bias), ()))
+    ]
+    own, early, late = blocks[0][0], list(blocks[0][1:]), blocks[1]
+    along = [own] + [shift(own, k) for k in range(1, nz)]
+    early[-1], along[1] = lax.optimization_barrier((early[-1], along[1]))
+    early = [swap(part, r + 1) for r, part in enumerate(early)]
+    along, early, late = lax.optimization_barrier((along, early, late))
+    pieces = along + [lax.ppermute(jnp.stack(along), "dp", partner(dp_count, 1))]
+    gathered = [early, [swap(part, r + 1) for r, part in enumerate(late)]]
 
     facts = (frame_counts, clip_starts, frame_kept)
     results, before = [], None
-    for c, blocks in enumerate(gathered):
+    for c in range(len(chunks)):
+        blocks = gathered[c]
         first, last = c == 0, c == len(chunks) - 1
         got = chunk(
             tm_count,
@@ -544,23 +546,28 @@
             (tokens, upstream, blocks),
             before,
         )
-        results.append([swap(part, r + 1) for r, part in enumerate(got[: tm_count - 1])])
+        leaving = got[: tm_count - 1]
+        if first:
+            leaving, gathered[1] = lax.optimization_barrier((leaving, gathered[1]))
+        results.append([swap(part, r + 1) for r, part in enumerate(leaving)])
         mixed, grads = got[tm_count - 1 : tm_count + 1]
         before = (got[tm_count + 1], got[tm_count + 2], mixed, grads)
     keep, send = got[-4:-2], got[-2:]
 
     send, results[0] = lax.optimization_barrier((send, results[0]))
     others = [lax.ppermute(part, "dp", partner(dp_count, 1)) for part in send]
+    others, results[0] = lax.optimization_barrier((others, results[0]))
     halves = []
     for mine, other in zip(keep, others):
-        blocks = [
-            lax.optimization_barrier((mine[k].astype(f32) + other[k].astype(f32)).astype(bf16))
-            for k in range(nz)
-        ]
-        half = blocks[0].astype(f32)
-        for k in range(1, nz):
-            half = half + shift(blocks[k], k).astype(f32)
-        halves.append(half)
+        left, bit = nz, 1
+        half = mine.astype(f32) + other.astype(f32)
+        while bit < nz:
+            left //= 2
+            gone = lax.optimization_barrier(half[left:].astype(bf16))
+            got = lax.ppermute(gone, "dp", partner(dp_count, CORES * bit))
+            half = half[:left] + got.astype(f32)
+            bit *= 2
+        halves.append(half[0])
     halves[0], results[-1] = lax.optimization_barrier((halves[0], results[-1]))
     summed = []
     for half in halves:

time: 125 us -> 119 us (0.952)
  starting transfers between devices: 43.3 us -> 35.3 us
  waiting for transfers between devices: 26.2 us -> 31.3 us
  local copies, waits for them, and re-layouts: 3.25 us -> 1.71 us
    ppermute x9 -> x3, starting transfers between devices: 21.3 us -> 5.14 us  [shift(): return lax.ppermute(array, 'dp', hops)]
    ppermute x0 -> x4, waiting for transfers between devices: none -> 9.27 us  [body(): got = lax.ppermute(gone, 'dp', partner(dp_count, CORES * bit))]
    ppermute x0 -> x4, starting transfers between devices: none -> 8.73 us  [body(): got = lax.ppermute(gone, 'dp', partner(dp_count, CORES * bit))]
    ppermute x9 -> x3, waiting for transfers between devices: 16.8 us -> 12.7 us  [shift(): return lax.ppermute(array, 'dp', hops)]
    add x1 -> x4, other arithmetic: 0.06 us -> 1.33 us  [the longest x2 1.25 us: body(): half = mine.astype(f32) + other.astype(f32)]
    another operation x1, other arithmetic: 1.41 us -> 0.15 us  [body(): jnp.stack(along)]
  transfers between devices with their start and end apart: 28 -> 26, of which waited for: 9 -> 12; matrix products, arithmetic and copies ran while one was open for 0% -> 1% of each run, Pallas kernels for 35% -> 36%
where the time goes in v4:
time: 119 us
  Pallas kernels  46.1 us (39%)
  starting transfers between devices  35.3 us (30%)
  waiting for transfers between devices  31.3 us (26%)
  other arithmetic  2.44 us (2%)
  local copies, waits for them, and re-layouts  1.71 us (1%)
  between operations  1.68 us (1%)
    pallas_call x2, Pallas kernels, chunk(): pl.pallas_call(functools.partial(chunk_kernel, tm_count, dp_count, frames...  36 us
    ppermute x16, starting transfers between devices, swap(): return lax.ppermute(array, 'tm', partner(tm_count, r))  20.9 us
    ppermute x3, waiting for transfers between devices, shift(): return lax.ppermute(array, 'dp', hops)  12.7 us
    ppermute x16, waiting for transfers between devices, swap(): return lax.ppermute(array, 'tm', partner(tm_count, r))  9.31 us
    ppermute x4, waiting for transfers between devices, body(): got = lax.ppermute(gone, 'dp', partner(dp_count, CORES * bit))  9.27 us
    ppermute x4, starting transfers between devices, body(): got = lax.ppermute(gone, 'dp', partner(dp_count, CORES * bit))  8.73 us
    pallas_call x2, Pallas kernels, pack(): pl.pallas_call(functools.partial(pack_kernel, tm_count, patches_dev, offs...  5.75 us
    ppermute x3, starting transfers between devices, shift(): return lax.ppermute(array, 'dp', hops)  5.14 us
  transfers between devices with their start and end apart: 26, of which 12 were waited for; matrix products, arithmetic and copies ran while one was open for 1% of the time, Pallas kernels for 36%

profile of v4, /device:TPU:0, one launch (start us, length us, event | category | flops | bytes accessed | tf_op | source)
XLA Modules:
  0.0 118.5 jit_solution(9590322465662852966)
XLA Ops:
  0.6 3.3 %shard_map.119 = (bf16[104,1152]{1,0:T(8,128)(2,1)}, bf16[25,8,1152]{2,1,0:T(8,128)(2,1)}, bf16[25,8,1152]{2,1,0:T(8,128)(2,1)}, bf16[25,8,1152]{2,1,0:T(8,128)(2,1)}) custom-call(bf16[196,8,768]{2,1,0:T(8,128)(2,1)} %bitcast.24, bf16[196,8,384]{2,1,0:T(8,128)(2,1)} %bitcast.29, bf16[96,1152]{1,0:T(8,128)(2,1)} %rest_0_.1, bf16[96]{0:T(256)(128)(2,1)} %rest_1_.1, ...), custom_call_target="tpu_custom_call" | custom-call | tf_op jit(solution)/shard_map/pallas_call | solution.py:90
  3.9 3.1 %collective-permute-start = (bf16[104,1152]{1,0:T(8,128)(2,1)}, bf16[104,1152]{1,0:T(8,128)(2,1)S(1)}, u32[]{:S(2)}, u32[]{:S(2)}) collective-permute-start(bf16[104,1152]{1,0:T(8,128)(2,1)} %get-tuple-element.73.rest_0_), channel_id=1, source_target_pairs={{0,8},{4,12},{8,16},{12,20},{16,24},{20,28},{24,0},{28,4},{1,9},{5... | collective-permute-start | bytes 718856 | tf_op jit(solution)/shard_map/ppermute | solution.py:517
  7.0 1.5 %collective-permute-start.3 = (bf16[25,8,1152]{2,1,0:T(8,128)(2,1)}, bf16[25,8,1152]{2,1,0:T(8,128)(2,1)S(1)}, u32[]{:S(2)}, u32[]{:S(2)}) collective-permute-start(bf16[25,8,1152]{2,1,0:T(8,128)(2,1)} %get-tuple-element.67), channel_id=1, source_target_pairs={{0,1},{1,0},{2,3},{3,2},{4,5},{5,4},{6,7},{7,6},{8,9},{9,8},{10,11... | collective-permute-start | bytes 1382408 | tf_op jit(solution)/shard_map/ppermute | solution.py:508
  8.5 1.5 %collective-permute-start.4 = (bf16[25,8,1152]{2,1,0:T(8,128)(2,1)}, bf16[25,8,1152]{2,1,0:T(8,128)(2,1)S(1)}, u32[]{:S(2)}, u32[]{:S(2)}) collective-permute-start(bf16[25,8,1152]{2,1,0:T(8,128)(2,1)} %get-tuple-element.68), channel_id=1, source_target_pairs={{0,2},{1,3},{2,0},{3,1},{4,6},{5,7},{6,4},{7,5},{8,10},{9,11},{10,... | collective-permute-start | bytes 1382408 | tf_op jit(solution)/shard_map/ppermute | solution.py:508
  10.0 5.1 %collective-permute-done.rest_1_ = bf16[104,1152]{1,0:T(8,128)(2,1)S(1)} collective-permute-done((bf16[104,1152]{1,0:T(8,128)(2,1)}, bf16[104,1152]{1,0:T(8,128)(2,1)S(1)}, u32[]{:S(2)}, u32[]{:S(2)}) %collective-permute-start) | collective-permute-done | bytes 239648 | tf_op jit(solution)/shard_map/ppermute | solution.py:517
  15.1 2.4 %collective-permute-start.5 = (bf16[25,8,1152]{2,1,0:T(8,128)(2,1)}, bf16[25,8,1152]{2,1,0:T(8,128)(2,1)S(1)}, u32[]{:S(2)}, u32[]{:S(2)}) collective-permute-start(bf16[25,8,1152]{2,1,0:T(8,128)(2,1)} %get-tuple-element.69), channel_id=1, source_target_pairs={{0,3},{1,2},{2,1},{3,0},{4,7},{5,6},{6,5},{7,4},{8,11},{9,10},{10,... | collective-permute-start | bytes 1382408 | tf_op jit(solution)/shard_map/ppermute | solution.py:508
  19.6 2.5 %shard_map.120 = (bf16[24,8,1152]{2,1,0:T(8,128)(2,1)}, bf16[24,8,1152]{2,1,0:T(8,128)(2,1)}, bf16[24,8,1152]{2,1,0:T(8,128)(2,1)}) custom-call(bf16[196,8,768]{2,1,0:T(8,128)(2,1)} %bitcast.25, bf16[196,8,384]{2,1,0:T(8,128)(2,1)} %bitcast.30), custom_call_target="tpu_custom_call" | custom-call | tf_op jit(solution)/shard_map/pallas_call | solution.py:90
  22.1 7.5 %collective-permute-done.1.rest_2_ = bf16[104,1152]{1,0:T(8,128)(2,1)S(1)} collective-permute-done((bf16[104,1152]{1,0:T(8,128)(2,1)}, bf16[104,1152]{1,0:T(8,128)(2,1)S(1)}, u32[]{:S(2)}, u32[]{:S(2)}) %collective-permute-start.1) | collective-permute-done | bytes 239648 | tf_op jit(solution)/shard_map/ppermute | solution.py:517
  35.8 18.4 %shard_map.121 = (bf16[25,8,1152]{2,1,0:T(8,128)(2,1)}, bf16[25,8,1152]{2,1,0:T(8,128)(2,1)}, bf16[25,8,1152]{2,1,0:T(8,128)(2,1)}, bf16[196,8,384]{2,1,0:T(8,12...) custom-call(s32[1]{0:T(128)S(6)} %copy.25.count_ref, s32[1,2]{1,0:T(1,128)} %starts_ref.3, ...), custom_call_target="tpu_custom_call" | custom-call | tf_op jit(solution)/shard_map/pallas_call | solution.py:461
  57.8 17.6 %shard_map.122 = (bf16[24,8,1152]{2,1,0:T(8,128)(2,1)}, bf16[24,8,1152]{2,1,0:T(8,128)(2,1)}, bf16[24,8,1152]{2,1,0:T(8,128)(2,1)}, bf16[196,8,384]{2,1,0:T(8,12...) custom-call(s32[1]{0:T(128)S(6)} %copy.25.count_ref, ...), custom_call_target="tpu_custom_call", output_to_operand_aliasing={{3}: (15, {}), {4}: (16, {})} | custom-call | tf_op jit(solution)/shard_map/pallas_call | solution.py:461
  75.9 1.5 %collective-permute-done.12.refs_4_ = bf16[25,8,1152]{2,1,0:T(8,128)(2,1)S(1)} collective-permute-done((bf16[25,8,1152]{2,1,0:T(8,128)(2,1)}, bf16[25,8,1152]{2,1,0:T(8,128)(2,1)S(1)}, u32[]{:S(2)}, u32[]{:S(2)}) %collective-permute-start.12) | collective-permute-done | bytes 460832 | tf_op jit(solution)/shard_map/ppermute | solution.py:508
  78.8 1.5 %collective-permute-start.18 = (bf16[24,8,1152]{2,1,0:T(8,128)(2,1)}, bf16[24,8,1152]{2,1,0:T(8,128)(2,1)S(1)}, u32[]{:S(2)}, u32[]{:S(2)}) collective-permute-start(bf16[24,8,1152]{2,1,0:T(8,128)(2,1)} %get-tuple-element.113), channel_id=1, source_target_pairs={{0,2},{1,3},{2,0},{3,1},{4,6},{5,7},{6,4},{7,5},{8,10},{9,11},{10,... | collective-permute-start | bytes 1327112 | tf_op jit(solution)/shard_map/ppermute | solution.py:508
  82.6 4.2 %collective-permute-start.15 = (bf16[2,48,1152]{2,1,0:T(8,128)(2,1)S(1)}, bf16[2,48,1152]{2,1,0:T(8,128)(2,1)S(1)}, u32[]{:S(2)}, u32[]{:S(2)}) collective-permute-start(bf16[2,48,1152]{2,1,0:T(8,128)(2,1)S(1)} %slice.74), channel_id=1, source_target_pairs={{0,8},{4,12},{8,0},{12,4},{16,24},{20,28},{24,16},{28,20},{1,9},{5... | collective-permute-start | bytes 663560 | tf_op jit(solution)/shard_map/ppermute | solution.py:567
  87.1 2.2 %shard_map.123 = (bf16[196,8,384]{2,1,0:T(8,128)(2,1)}, bf16[196,8,768]{2,1,0:T(8,128)(2,1)}) custom-call(bf16[196,8,384]{2,1,0:T(8,128)(2,1)} %get-tuple-element.93.refs_0_, bf16[196,8,768]{2,1,0:T(8,128)(2,1)} %get-tuple-element.94.refs_1_, bf16[25,8,1152]{2,1,0:T(8,128)(2,1)} %copy-done.9, ...), custom_call_target="tpu_custom_call", output_to_operand_aliasing={{0}: (0, {}), {1}: (1, {})} | custom-call | tf_op jit(solution)/shard_map/pallas_call | solution.py:123
  89.3 3.9 %collective-permute-done.15 = bf16[2,48,1152]{2,1,0:T(8,128)(2,1)S(1)} collective-permute-done((bf16[2,48,1152]{2,1,0:T(8,128)(2,1)S(1)}, bf16[2,48,1152]{2,1,0:T(8,128)(2,1)S(1)}, u32[]{:S(2)}, u32[]{:S(2)}) %collective-permute-start.15) | collective-permute-done | bytes 221216 | tf_op jit(solution)/shard_map/ppermute | solution.py:567
  93.2 2.5 %collective-permute-start.16 = (bf16[1,48,1152]{2,1,0:T(8,128)(2,1)S(1)}, bf16[1,48,1152]{2,1,0:T(8,128)(2,1)S(1)}, u32[]{:S(2)}, u32[]{:S(2)}) collective-permute-start(bf16[1,48,1152]{2,1,0:T(8,128)(2,1)S(1)} %slice.76), channel_id=1, source_target_pairs={{0,16},{4,20},{8,24},{12,28},{16,0},{20,4},{24,8},{28,12},{1,17},{... | collective-permute-start | bytes 331784 | tf_op jit(solution)/shard_map/ppermute | solution.py:567
  95.8 3.2 %collective-permute-done.22 = bf16[2,56,1152]{2,1,0:T(8,128)(2,1)S(1)} collective-permute-done((bf16[2,56,1152]{2,1,0:T(8,128)(2,1)S(1)}, bf16[2,56,1152]{2,1,0:T(8,128)(2,1)S(1)}, u32[]{:S(2)}, u32[]{:S(2)}) %collective-permute-start.22) | collective-permute-done | bytes 258080 | tf_op jit(solution)/shard_map/ppermute | solution.py:567
  99.1 1.9 %collective-permute-start.23 = (bf16[1,56,1152]{2,1,0:T(8,128)(2,1)S(1)}, bf16[1,56,1152]{2,1,0:T(8,128)(2,1)S(1)}, u32[]{:S(2)}, u32[]{:S(2)}) collective-permute-start(bf16[1,56,1152]{2,1,0:T(8,128)(2,1)S(1)} %slice.75), channel_id=1, source_target_pairs={{0,16},{4,20},{8,24},{12,28},{16,0},{20,4},{24,8},{28,12},{1,17},{... | collective-permute-start | bytes 387080 | tf_op jit(solution)/shard_map/ppermute | solution.py:567
  101.1 1.6 %collective-permute-start.20 = (bf16[48,1152]{1,0:T(8,128)(2,1)S(1)}, bf16[48,1152]{1,0:T(8,128)(2,1)S(1)}, u32[]{:S(2)}, u32[]{:S(2)}) collective-permute-start(bf16[48,1152]{1,0:T(8,128)(2,1)S(1)} %fusion.1), channel_id=1, source_target_pairs={{0,1},{1,0},{2,3},{3,2},{4,5},{5,4},{6,7},{7,6},{8,9},{9,8},{10,11... | collective-permute-start | bytes 331784 | tf_op jit(solution)/shard_map/ppermute | solution.py:508
  102.6 2.2 %shard_map.124 = (bf16[196,8,384]{2,1,0:T(8,128)(2,1)}, bf16[196,8,768]{2,1,0:T(8,128)(2,1)}) custom-call(bf16[196,8,384]{2,1,0:T(8,128)(2,1)} %get-tuple-element.108.refs_0_, bf16[196,8,768]{2,1,0:T(8,128)(2,1)} %get-tuple-element.109.refs_1_, bf16[24,8,1152]{2,1,0:T(8,128)(2,1)} %copy-done.12, ...), custom_call_target="tpu_custom_call", output_to_operand_aliasing={{0}: (0, {}), {1}: (1, {})} | custom-call | tf_op jit(solution)/shard_map/pallas_call | solution.py:123
  104.8 2.2 %collective-permute-done.23 = bf16[1,56,1152]{2,1,0:T(8,128)(2,1)S(1)} collective-permute-done((bf16[1,56,1152]{2,1,0:T(8,128)(2,1)S(1)}, bf16[1,56,1152]{2,1,0:T(8,128)(2,1)S(1)}, u32[]{:S(2)}, u32[]{:S(2)}) %collective-permute-start.23) | collective-permute-done | bytes 129056 | tf_op jit(solution)/shard_map/ppermute | solution.py:567
  107.0 1.6 %collective-permute-start.24 = (bf16[56,1152]{1,0:T(8,128)(2,1)S(1)}, bf16[56,1152]{1,0:T(8,128)(2,1)S(1)}, u32[]{:S(2)}, u32[]{:S(2)}) collective-permute-start(bf16[56,1152]{1,0:T(8,128)(2,1)S(1)} %fusion.2), channel_id=1, source_target_pairs={{0,1},{1,0},{2,3},{3,2},{4,5},{5,4},{6,7},{7,6},{8,9},{9,8},{10,11... | collective-permute-start | bytes 387080 | tf_op jit(solution)/shard_map/ppermute | solution.py:508
  109.2 2.8 %collective-permute-done.24 = bf16[56,1152]{1,0:T(8,128)(2,1)S(1)} collective-permute-done((bf16[56,1152]{1,0:T(8,128)(2,1)S(1)}, bf16[56,1152]{1,0:T(8,128)(2,1)S(1)}, u32[]{:S(2)}, u32[]{:S(2)}) %collective-permute-start.24) | collective-permute-done | bytes 129056 | tf_op jit(solution)/shard_map/ppermute | solution.py:508
  114.1 3.0 %collective-permute-done.25 = bf16[56,1152]{1,0:T(8,128)(2,1)S(1)} collective-permute-done((bf16[56,1152]{1,0:T(8,128)(2,1)S(1)}, bf16[56,1152]{1,0:T(8,128)(2,1)S(1)}, u32[]{:S(2)}, u32[]{:S(2)}) %collective-permute-start.25) | collective-permute-done | bytes 129056 | tf_op jit(solution)/shard_map/ppermute | solution.py:508
  (89 shorter events, 19.7 us)
Async XLA Ops:
  3.9 11.1 %collective-permute-start = (bf16[104,1152]{1,0:T(8,128)(2,1)}, bf16[104,1152]{1,0:T(8,128)(2,1)S(1)}, u32[]{:S(2)}, u32[]{:S(2)}) collective-permute-start(bf16[104,1152]{1,0:T(8,128)(2,1)} %get-tuple-element.73.rest_0_), channel_id=1, source_target_pairs={{0,8},{4,12},{8,16},{12,20},{16,24},{20,28},{24,0},{28,4},{1,9},{5... | collective-permute-start | bytes 718856 | tf_op jit(solution)/shard_map/ppermute | solution.py:517
  7.0 22.7 %collective-permute-start.3 = (bf16[25,8,1152]{2,1,0:T(8,128)(2,1)}, bf16[25,8,1152]{2,1,0:T(8,128)(2,1)S(1)}, u32[]{:S(2)}, u32[]{:S(2)}) collective-permute-start(bf16[25,8,1152]{2,1,0:T(8,128)(2,1)} %get-tuple-element.67), channel_id=1, source_target_pairs={{0,1},{1,0},{2,3},{3,2},{4,5},{5,4},{6,7},{7,6},{8,9},{9,8},{10,11... | collective-permute-start | bytes 1382408 | tf_op jit(solution)/shard_map/ppermute | solution.py:508
  8.5 21.8 %collective-permute-start.4 = (bf16[25,8,1152]{2,1,0:T(8,128)(2,1)}, bf16[25,8,1152]{2,1,0:T(8,128)(2,1)S(1)}, u32[]{:S(2)}, u32[]{:S(2)}) collective-permute-start(bf16[25,8,1152]{2,1,0:T(8,128)(2,1)} %get-tuple-element.68), channel_id=1, source_target_pairs={{0,2},{1,3},{2,0},{3,1},{4,6},{5,7},{6,4},{7,5},{8,10},{9,11},{10,... | collective-permute-start | bytes 1382408 | tf_op jit(solution)/shard_map/ppermute | solution.py:508
  15.1 15.3 %collective-permute-start.5 = (bf16[25,8,1152]{2,1,0:T(8,128)(2,1)}, bf16[25,8,1152]{2,1,0:T(8,128)(2,1)S(1)}, u32[]{:S(2)}, u32[]{:S(2)}) collective-permute-start(bf16[25,8,1152]{2,1,0:T(8,128)(2,1)} %get-tuple-element.69), channel_id=1, source_target_pairs={{0,3},{1,2},{2,1},{3,0},{4,7},{5,6},{6,5},{7,4},{8,11},{9,10},{10,... | collective-permute-start | bytes 1382408 | tf_op jit(solution)/shard_map/ppermute | solution.py:508
  17.5 12.0 %collective-permute-start.1 = (bf16[104,1152]{1,0:T(8,128)(2,1)}, bf16[104,1152]{1,0:T(8,128)(2,1)S(1)}, u32[]{:S(2)}, u32[]{:S(2)}) collective-permute-start(bf16[104,1152]{1,0:T(8,128)(2,1)} %get-tuple-element.73.rest_0_), channel_id=1, source_target_pairs={{0,16},{4,20},{8,24},{12,28},{16,0},{20,4},{24,8},{28,12},{1,17},{... | collective-permute-start | bytes 718856 | tf_op jit(solution)/shard_map/ppermute | solution.py:517
  18.3 11.5 %collective-permute-start.2 = (bf16[104,1152]{1,0:T(8,128)(2,1)}, bf16[104,1152]{1,0:T(8,128)(2,1)S(1)}, u32[]{:S(2)}, u32[]{:S(2)}) collective-permute-start(bf16[104,1152]{1,0:T(8,128)(2,1)} %get-tuple-element.73.rest_0_), channel_id=1, source_target_pairs={{0,24},{4,28},{8,0},{12,4},{16,8},{20,12},{24,16},{28,20},{1,25},{... | collective-permute-start | bytes 718856 | tf_op jit(solution)/shard_map/ppermute | solution.py:517
  30.5 4.3 %collective-permute-start.6 = (bf16[4,104,1152]{2,1,0:T(8,128)(2,1)S(1)}, bf16[4,104,1152]{2,1,0:T(8,128)(2,1)S(1)}, u32[]{:S(2)}, u32[]{:S(2)}) collective-permute-start(bf16[4,104,1152]{2,1,0:T(8,128)(2,1)S(1)} %pad_maximum_fusion), channel_id=1, source_target_pairs={{0,4},{4,0},{8,12},{12,8},{16,20},{20,16},{24,28},{28,24},{1,5},{5... | collective-permute-start | bytes 2875400 | tf_op jit(solution)/shard_map/ppermute | solution.py:528
  30.6 23.6 %collective-permute-start.7 = (bf16[24,8,1152]{2,1,0:T(8,128)(2,1)}, bf16[24,8,1152]{2,1,0:T(8,128)(2,1)S(1)}, u32[]{:S(2)}, u32[]{:S(2)}) collective-permute-start(bf16[24,8,1152]{2,1,0:T(8,128)(2,1)} %get-tuple-element.83), channel_id=1, source_target_pairs={{0,1},{1,0},{2,3},{3,2},{4,5},{5,4},{6,7},{7,6},{8,9},{9,8},{10,11... | collective-permute-start | bytes 1327112 | tf_op jit(solution)/shard_map/ppermute | solution.py:508
  31.9 22.3 %collective-permute-start.8 = (bf16[24,8,1152]{2,1,0:T(8,128)(2,1)}, bf16[24,8,1152]{2,1,0:T(8,128)(2,1)S(1)}, u32[]{:S(2)}, u32[]{:S(2)}) collective-permute-start(bf16[24,8,1152]{2,1,0:T(8,128)(2,1)} %get-tuple-element.84), channel_id=1, source_target_pairs={{0,2},{1,3},{2,0},{3,1},{4,6},{5,7},{6,4},{7,5},{8,10},{9,11},{10,... | collective-permute-start | bytes 1327112 | tf_op jit(solution)/shard_map/ppermute | solution.py:508
  32.7 21.5 %collective-permute-start.9 = (bf16[24,8,1152]{2,1,0:T(8,128)(2,1)}, bf16[24,8,1152]{2,1,0:T(8,128)(2,1)S(1)}, u32[]{:S(2)}, u32[]{:S(2)}) collective-permute-start(bf16[24,8,1152]{2,1,0:T(8,128)(2,1)} %get-tuple-element.85), channel_id=1, source_target_pairs={{0,3},{1,2},{2,1},{3,0},{4,7},{5,6},{6,5},{7,4},{8,11},{9,10},{10,... | collective-permute-start | bytes 1327112 | tf_op jit(solution)/shard_map/ppermute | solution.py:508
  54.3 21.2 %collective-permute-start.10 = (bf16[25,8,1152]{2,1,0:T(8,128)(2,1)}, bf16[25,8,1152]{2,1,0:T(8,128)(2,1)S(1)}, u32[]{:S(2)}, u32[]{:S(2)}) collective-permute-start(bf16[25,8,1152]{2,1,0:T(8,128)(2,1)} %get-tuple-element.97), channel_id=1, source_target_pairs={{0,1},{1,0},{2,3},{3,2},{4,5},{5,4},{6,7},{7,6},{8,9},{9,8},{10,11... | collective-permute-start | bytes 1382408 | tf_op jit(solution)/shard_map/ppermute | solution.py:508
  55.6 20.4 %collective-permute-start.11 = (bf16[25,8,1152]{2,1,0:T(8,128)(2,1)}, bf16[25,8,1152]{2,1,0:T(8,128)(2,1)S(1)}, u32[]{:S(2)}, u32[]{:S(2)}) collective-permute-start(bf16[25,8,1152]{2,1,0:T(8,128)(2,1)} %get-tuple-element.98), channel_id=1, source_target_pairs={{0,2},{1,3},{2,0},{3,1},{4,6},{5,7},{6,4},{7,5},{8,10},{9,11},{10,... | collective-permute-start | bytes 1382408 | tf_op jit(solution)/shard_map/ppermute | solution.py:508
  56.4 21.1 %collective-permute-start.12 = (bf16[25,8,1152]{2,1,0:T(8,128)(2,1)}, bf16[25,8,1152]{2,1,0:T(8,128)(2,1)S(1)}, u32[]{:S(2)}, u32[]{:S(2)}) collective-permute-start(bf16[25,8,1152]{2,1,0:T(8,128)(2,1)} %get-tuple-element.99), channel_id=1, source_target_pairs={{0,3},{1,2},{2,1},{3,0},{4,7},{5,6},{6,5},{7,4},{8,11},{9,10},{10,... | collective-permute-start | bytes 1382408 | tf_op jit(solution)/shard_map/ppermute | solution.py:508
  78.0 23.0 %collective-permute-start.17 = (bf16[24,8,1152]{2,1,0:T(8,128)(2,1)}, bf16[24,8,1152]{2,1,0:T(8,128)(2,1)S(1)}, u32[]{:S(2)}, u32[]{:S(2)}) collective-permute-start(bf16[24,8,1152]{2,1,0:T(8,128)(2,1)} %get-tuple-element.112), channel_id=1, source_target_pairs={{0,1},{1,0},{2,3},{3,2},{4,5},{5,4},{6,7},{7,6},{8,9},{9,8},{10,11... | collective-permute-start | bytes 1327112 | tf_op jit(solution)/shard_map/ppermute | solution.py:508
  78.8 22.2 %collective-permute-start.18 = (bf16[24,8,1152]{2,1,0:T(8,128)(2,1)}, bf16[24,8,1152]{2,1,0:T(8,128)(2,1)S(1)}, u32[]{:S(2)}, u32[]{:S(2)}) collective-permute-start(bf16[24,8,1152]{2,1,0:T(8,128)(2,1)} %get-tuple-element.113), channel_id=1, source_target_pairs={{0,2},{1,3},{2,0},{3,1},{4,6},{5,7},{6,4},{7,5},{8,10},{9,11},{10,... | collective-permute-start | bytes 1327112 | tf_op jit(solution)/shard_map/ppermute | solution.py:508
  80.3 20.7 %collective-permute-start.19 = (bf16[24,8,1152]{2,1,0:T(8,128)(2,1)}, bf16[24,8,1152]{2,1,0:T(8,128)(2,1)S(1)}, u32[]{:S(2)}, u32[]{:S(2)}) collective-permute-start(bf16[24,8,1152]{2,1,0:T(8,128)(2,1)} %get-tuple-element.114), channel_id=1, source_target_pairs={{0,3},{1,2},{2,1},{3,0},{4,7},{5,6},{6,5},{7,4},{8,11},{9,10},{10,... | collective-permute-start | bytes 1327112 | tf_op jit(solution)/shard_map/ppermute | solution.py:508
  82.6 10.6 %collective-permute-start.15 = (bf16[2,48,1152]{2,1,0:T(8,128)(2,1)S(1)}, bf16[2,48,1152]{2,1,0:T(8,128)(2,1)S(1)}, u32[]{:S(2)}, u32[]{:S(2)}) collective-permute-start(bf16[2,48,1152]{2,1,0:T(8,128)(2,1)S(1)} %slice.74), channel_id=1, source_target_pairs={{0,8},{4,12},{8,0},{12,4},{16,24},{20,28},{24,16},{28,20},{1,9},{5... | collective-permute-start | bytes 663560 | tf_op jit(solution)/shard_map/ppermute | solution.py:567
  87.0 12.0 %collective-permute-start.22 = (bf16[2,56,1152]{2,1,0:T(8,128)(2,1)S(1)}, bf16[2,56,1152]{2,1,0:T(8,128)(2,1)S(1)}, u32[]{:S(2)}, u32[]{:S(2)}) collective-permute-start(bf16[2,56,1152]{2,1,0:T(8,128)(2,1)S(1)} %slice.73), channel_id=1, source_target_pairs={{0,8},{4,12},{8,0},{12,4},{16,24},{20,28},{24,16},{28,20},{1,9},{5... | collective-permute-start | bytes 774152 | tf_op jit(solution)/shard_map/ppermute | solution.py:567
  93.2 7.7 %collective-permute-start.16 = (bf16[1,48,1152]{2,1,0:T(8,128)(2,1)S(1)}, bf16[1,48,1152]{2,1,0:T(8,128)(2,1)S(1)}, u32[]{:S(2)}, u32[]{:S(2)}) collective-permute-start(bf16[1,48,1152]{2,1,0:T(8,128)(2,1)S(1)} %slice.76), channel_id=1, source_target_pairs={{0,16},{4,20},{8,24},{12,28},{16,0},{20,4},{24,8},{28,12},{1,17},{... | collective-permute-start | bytes 331784 | tf_op jit(solution)/shard_map/ppermute | solution.py:567
  99.1 7.9 %collective-permute-start.23 = (bf16[1,56,1152]{2,1,0:T(8,128)(2,1)S(1)}, bf16[1,56,1152]{2,1,0:T(8,128)(2,1)S(1)}, u32[]{:S(2)}, u32[]{:S(2)}) collective-permute-start(bf16[1,56,1152]{2,1,0:T(8,128)(2,1)S(1)} %slice.75), channel_id=1, source_target_pairs={{0,16},{4,20},{8,24},{12,28},{16,0},{20,4},{24,8},{28,12},{1,17},{... | collective-permute-start | bytes 387080 | tf_op jit(solution)/shard_map/ppermute | solution.py:567
  101.1 7.5 %collective-permute-start.20 = (bf16[48,1152]{1,0:T(8,128)(2,1)S(1)}, bf16[48,1152]{1,0:T(8,128)(2,1)S(1)}, u32[]{:S(2)}, u32[]{:S(2)}) collective-permute-start(bf16[48,1152]{1,0:T(8,128)(2,1)S(1)} %fusion.1), channel_id=1, source_target_pairs={{0,1},{1,0},{2,3},{3,2},{4,5},{5,4},{6,7},{7,6},{8,9},{9,8},{10,11... | collective-permute-start | bytes 331784 | tf_op jit(solution)/shard_map/ppermute | solution.py:508
  107.0 5.0 %collective-permute-start.24 = (bf16[56,1152]{1,0:T(8,128)(2,1)S(1)}, bf16[56,1152]{1,0:T(8,128)(2,1)S(1)}, u32[]{:S(2)}, u32[]{:S(2)}) collective-permute-start(bf16[56,1152]{1,0:T(8,128)(2,1)S(1)} %fusion.2), channel_id=1, source_target_pairs={{0,1},{1,0},{2,3},{3,2},{4,5},{5,4},{6,7},{7,6},{8,9},{9,8},{10,11... | collective-permute-start | bytes 387080 | tf_op jit(solution)/shard_map/ppermute | solution.py:508
  108.6 5.4 %collective-permute-start.21 = (bf16[48,1152]{1,0:T(8,128)(2,1)S(1)}, bf16[48,1152]{1,0:T(8,128)(2,1)S(1)}, u32[]{:S(2)}, u32[]{:S(2)}) collective-permute-start(bf16[48,1152]{1,0:T(8,128)(2,1)S(1)} %add_convert_fusion.1), channel_id=1, source_target_pairs={{0,2},{1,3},{2,0},{3,1},{4,6},{5,7},{6,4},{7,5},{8,10},{9,11},{10,... | collective-permute-start | bytes 331784 | tf_op jit(solution)/shard_map/ppermute | solution.py:508
  112.1 5.0 %collective-permute-start.25 = (bf16[56,1152]{1,0:T(8,128)(2,1)S(1)}, bf16[56,1152]{1,0:T(8,128)(2,1)S(1)}, u32[]{:S(2)}, u32[]{:S(2)}) collective-permute-start(bf16[56,1152]{1,0:T(8,128)(2,1)S(1)} %add_convert_fusion), channel_id=1, source_target_pairs={{0,2},{1,3},{2,0},{3,1},{4,6},{5,7},{6,4},{7,5},{8,10},{9,11},{10,... | collective-permute-start | bytes 387080 | tf_op jit(solution)/shard_map/ppermute | solution.py:508
  (20 other events, 134.4 us)

commit v5 on v4

--- a/solution.py
+++ b/solution.py
@@ -206,7 +206,7 @@
     weights_in, lines_in = [], []
     for side in range(CORES):
         for k in range(nz):
-            owner = lax.rem(z + nz - k, nz) * CORES + (core ^ side)
+            owner = (z ^ k) * CORES + (core ^ side)
             piece = pieces[k] if side == 0 else pieces[nz].at[k]
             place = pl.ds(pl.multiple_of(owner * shard, shard), shard)
             weights_in.append(bring(piece.at[pl.ds(0, shard)], weight.at[place]))
@@ -267,8 +267,8 @@
 
     for copy in weights_in:
         copy.wait()
-    for part in range(3):
-        cut = slice(part * joined, (part + 1) * joined)
+    cuts = [slice(at, min(at + 512, columns)) for at in range(0, columns, 512)]
+    for cut in cuts:
         proj[:, cut] = jnp.dot(
             normed[...], weight[:, cut], preferred_element_type=f32
         ).astype(bf16)
@@ -351,8 +351,7 @@
             copy.wait()
     else:
         tails[...] = jnp.zeros_like(tails)
-    for part in range(3):
-        cut = slice(part * joined, (part + 1) * joined)
+    for cut in cuts:
         share = lax.dot_general(normed[...], pgrad[:, cut], tn, preferred_element_type=f32)
         if first:
             acc[:, cut] = share
@@ -366,8 +365,7 @@
         pgrad[...], weight[...], nt, preferred_element_type=f32
     ).astype(bf16)
 
-    @pl.loop(0, groups)
-    def _(j):
+    def finish(j):
         at = pl.ds(pl.multiple_of(j * unit, unit), unit)
         ngrad = normed[at, :].astype(f32)
         std = standard[at, :]
@@ -382,9 +380,16 @@
         )
         put_rows(j, slice(joined, columns), grad)
 
-    gone += [bring(back.at[r, kept], outs[r - 1]) for r in range(1, tm_count)]
-    gone.append(bring(back.at[0, kept, :, pl.ds(0, joined)], mixed_ref.at[mine]))
-    gone.append(bring(back.at[0, kept, :, pl.ds(joined, width)], tokens_ref.at[mine]))
+    middle = (groups + 1) // 2
+    for low_group, high_group in ((0, middle), (middle, groups)):
+        pl.loop(low_group, high_group)(finish)
+        start = low_group * group
+        count = min(high_group * group, size) - start
+        here, there = pl.ds(start, count), pl.ds(me * patches_dev + offset + start, count)
+        for r in range(1, tm_count):
+            gone.append(bring(back.at[r, here], outs[r - 1].at[here]))
+        gone.append(bring(back.at[0, here, :, pl.ds(0, joined)], mixed_ref.at[there]))
+        gone.append(bring(back.at[0, here, :, pl.ds(joined, width)], tokens_ref.at[there]))
     if not last:
         gone.append(bring(tails, sums[1]))
     else:
@@ -456,7 +461,7 @@
         pltpu.VMEM((tokens, 128), f32),
         pltpu.VMEM((16, width), f32),
         pltpu.VMEM((tm_count * frames, tokens // groups), f32),
-        pltpu.SemaphoreType.DMA((2 * tm_count + 2 * dp_count + 12,)),
+        pltpu.SemaphoreType.DMA((3 * tm_count + 2 * dp_count + 14,)),
     ]
     return pl.pallas_call(
         functools.partial(
@@ -512,20 +517,22 @@
     upstream = jnp.pad(attended_grad[0].transpose(1, 0, 2), spare)
     offsets = [sum(chunks[:c]) for c in range(len(chunks))]
 
-    def shift(array, k):
-        hops = [(i, (i + CORES * k) % dp_count) for i in range(dp_count)]
-        return lax.ppermute(array, "dp", hops)
+    def across(array, k):
+        return lax.ppermute(array, "dp", partner(dp_count, k))
 
     blocks = [
         pack(tm_count, patches_dev, offset, size, tokens, upstream, *more)
         for offset, size, more in zip(offsets, chunks, ((qkv_weight, norm_gain, norm_bias), ()))
     ]
     own, early, late = blocks[0][0], list(blocks[0][1:]), blocks[1]
-    along = [own] + [shift(own, k) for k in range(1, nz)]
-    early[-1], along[1] = lax.optimization_barrier((early[-1], along[1]))
+    along, bit = {0: own}, nz // 2
+    while bit:
+        along.update({k + bit: across(along[k], CORES * bit) for k in sorted(along)})
+        bit //= 2
+    along = [along[k] for k in range(nz)]
     early = [swap(part, r + 1) for r, part in enumerate(early)]
     along, early, late = lax.optimization_barrier((along, early, late))
-    pieces = along + [lax.ppermute(jnp.stack(along), "dp", partner(dp_count, 1))]
+    pieces = along + [across(jnp.stack(along), 1)]
     gathered = [early, [swap(part, r + 1) for r, part in enumerate(late)]]
 
     facts = (frame_counts, clip_starts, frame_kept)
@@ -555,7 +562,7 @@
     keep, send = got[-4:-2], got[-2:]
 
     send, results[0] = lax.optimization_barrier((send, results[0]))
-    others = [lax.ppermute(part, "dp", partner(dp_count, 1)) for part in send]
+    others = [across(part, 1) for part in send]
     others, results[0] = lax.optimization_barrier((others, results[0]))
     halves = []
     for mine, other in zip(keep, others):
@@ -564,17 +571,23 @@
         while bit < nz:
             left //= 2
             gone = lax.optimization_barrier(half[left:].astype(bf16))
-            got = lax.ppermute(gone, "dp", partner(dp_count, CORES * bit))
+            got = across(gone, CORES * bit)
             half = half[:left] + got.astype(f32)
             bit *= 2
         halves.append(half[0])
     halves[0], results[-1] = lax.optimization_barrier((halves[0], results[-1]))
     summed = []
-    for half in halves:
+    for side, half in enumerate(halves):
         r = 1
         while r < tm_count:
             mine = lax.optimization_barrier(half.astype(bf16))
-            half = mine.astype(f32) + swap(mine, r).astype(f32)
+            got = swap(mine, r)
+            if side == 0 and r == 1:
+                got, results[-1] = lax.optimization_barrier((got, results[-1]))
+            half = mine.astype(f32) + got.astype(f32)
+            if side == 1 and 2 * r < tm_count:
+                half += swap(mine, 2 * r).astype(f32) + swap(mine, 3 * r).astype(f32)
+                r *= 2
             r *= 2
         summed.append(half)
 

time: 119 us -> 115 us (0.966)
  starting transfers between devices: 35.3 us -> 29 us
  waiting for transfers between devices: 31.3 us -> 35.7 us
  Pallas kernels: 46.1 us -> 44.2 us
    ppermute x16 -> x17, waiting for transfers between devices: 9.31 us -> 14.5 us  [swap(): return lax.ppermute(array, 'tm', partner(tm_count, r))]
    ppermute x10, starting transfers between devices: 14.5 us -> 9.63 us  [across(): return lax.ppermute(array, 'dp', partner(dp_count, k))]
    pallas_call x2, Pallas kernels: 36 us -> 34.1 us  [chunk(): pl.pallas_call(functools.partial(chunk_kernel, tm_count, dp_count, frames...]
    ppermute x16 -> x17, starting transfers between devices: 20.9 us -> 19.4 us  [swap(): return lax.ppermute(array, 'tm', partner(tm_count, r))]
  transfers between devices with their start and end apart: 26 -> 27, of which waited for: 12 -> 12; matrix products, arithmetic and copies ran while one was open for 1% -> 2% of each run, Pallas kernels for 36% -> 36%
where the time goes in v5:
time: 115 us
  Pallas kernels  44.2 us (38%)
  waiting for transfers between devices  35.7 us (31%)
  starting transfers between devices  29 us (25%)
  other arithmetic  2.45 us (2%)
  local copies, waits for them, and re-layouts  1.72 us (1%)
  between operations  1.68 us (1%)
    pallas_call x2, Pallas kernels, chunk(): pl.pallas_call(functools.partial(chunk_kernel, tm_count, dp_count, frames...  34.1 us
    ppermute x10, waiting for transfers between devices, across(): return lax.ppermute(array, 'dp', partner(dp_count, k))  21.2 us
    ppermute x17, starting transfers between devices, swap(): return lax.ppermute(array, 'tm', partner(tm_count, r))  19.4 us
    ppermute x17, waiting for transfers between devices, swap(): return lax.ppermute(array, 'tm', partner(tm_count, r))  14.5 us
    ppermute x10, starting transfers between devices, across(): return lax.ppermute(array, 'dp', partner(dp_count, k))  9.63 us
    pallas_call x2, Pallas kernels, pack(): pl.pallas_call(functools.partial(pack_kernel, tm_count, patches_dev, offs...  5.74 us
    pallas_call x2, Pallas kernels, unpack(): pl.pallas_call(functools.partial(unpack_kernel, tm_count, patches_dev, of...  4.37 us
  transfers between devices with their start and end apart: 27, of which 12 were waited for; matrix products, arithmetic and copies ran while one was open for 2% of the time, Pallas kernels for 36%

profile of v5, /device:TPU:0, one launch (start us, length us, event | category | flops | bytes accessed | tf_op | source)
XLA Modules:
  0.0 114.8 jit_solution(8803386331138876028)
XLA Ops:
  0.6 3.3 %shard_map.119 = (bf16[104,1152]{1,0:T(8,128)(2,1)}, bf16[25,8,1152]{2,1,0:T(8,128)(2,1)}, bf16[25,8,1152]{2,1,0:T(8,128)(2,1)}, bf16[25,8,1152]{2,1,0:T(8,128)(2,1)}) custom-call(bf16[196,8,768]{2,1,0:T(8,128)(2,1)} %bitcast.24, bf16[196,8,384]{2,1,0:T(8,128)(2,1)} %bitcast.29, bf16[96,1152]{1,0:T(8,128)(2,1)} %rest_0_.1, bf16[96]{0:T(256)(128)(2,1)} %rest_1_.1, ...), custom_call_target="tpu_custom_call" | custom-call | tf_op jit(solution)/shard_map/pallas_call | solution.py:90
  3.9 4.1 %collective-permute-start.1 = (bf16[104,1152]{1,0:T(8,128)(2,1)}, bf16[104,1152]{1,0:T(8,128)(2,1)S(1)}, u32[]{:S(2)}, u32[]{:S(2)}) collective-permute-start(bf16[104,1152]{1,0:T(8,128)(2,1)} %get-tuple-element.73.rest_0_), channel_id=1, source_target_pairs={{0,16},{4,20},{8,24},{12,28},{16,0},{20,4},{24,8},{28,12},{1,17},{... | collective-permute-start | bytes 718856 | tf_op jit(solution)/shard_map/ppermute | solution.py:521
  8.0 1.5 %collective-permute-start.3 = (bf16[25,8,1152]{2,1,0:T(8,128)(2,1)}, bf16[25,8,1152]{2,1,0:T(8,128)(2,1)S(1)}, u32[]{:S(2)}, u32[]{:S(2)}) collective-permute-start(bf16[25,8,1152]{2,1,0:T(8,128)(2,1)} %get-tuple-element.67), channel_id=1, source_target_pairs={{0,1},{1,0},{2,3},{3,2},{4,5},{5,4},{6,7},{7,6},{8,9},{9,8},{10,11... | collective-permute-start | bytes 1382408 | tf_op jit(solution)/shard_map/ppermute | solution.py:513
  9.5 1.5 %collective-permute-start.4 = (bf16[25,8,1152]{2,1,0:T(8,128)(2,1)}, bf16[25,8,1152]{2,1,0:T(8,128)(2,1)S(1)}, u32[]{:S(2)}, u32[]{:S(2)}) collective-permute-start(bf16[25,8,1152]{2,1,0:T(8,128)(2,1)} %get-tuple-element.68), channel_id=1, source_target_pairs={{0,2},{1,3},{2,0},{3,1},{4,6},{5,7},{6,4},{7,5},{8,10},{9,11},{10,... | collective-permute-start | bytes 1382408 | tf_op jit(solution)/shard_map/ppermute | solution.py:513
  11.5 1.6 %collective-permute-start = (bf16[104,1152]{1,0:T(8,128)(2,1)}, bf16[104,1152]{1,0:T(8,128)(2,1)S(1)}, u32[]{:S(2)}, u32[]{:S(2)}) collective-permute-start(bf16[104,1152]{1,0:T(8,128)(2,1)} %get-tuple-element.73.rest_0_), channel_id=1, source_target_pairs={{0,8},{4,12},{8,0},{12,4},{16,24},{20,28},{24,16},{28,20},{1,9},{5... | collective-permute-start | bytes 718856 | tf_op jit(solution)/shard_map/ppermute | solution.py:521
  13.1 6.2 %collective-permute-done.1.rest_2_ = bf16[104,1152]{1,0:T(8,128)(2,1)S(1)} collective-permute-done((bf16[104,1152]{1,0:T(8,128)(2,1)}, bf16[104,1152]{1,0:T(8,128)(2,1)S(1)}, u32[]{:S(2)}, u32[]{:S(2)}) %collective-permute-start.1) | collective-permute-done | bytes 239648 | tf_op jit(solution)/shard_map/ppermute | solution.py:521
  20.1 2.4 %shard_map.120 = (bf16[24,8,1152]{2,1,0:T(8,128)(2,1)}, bf16[24,8,1152]{2,1,0:T(8,128)(2,1)}, bf16[24,8,1152]{2,1,0:T(8,128)(2,1)}) custom-call(bf16[196,8,768]{2,1,0:T(8,128)(2,1)} %bitcast.25, bf16[196,8,384]{2,1,0:T(8,128)(2,1)} %bitcast.30), custom_call_target="tpu_custom_call" | custom-call | tf_op jit(solution)/shard_map/pallas_call | solution.py:90
  23.1 8.2 %collective-permute-done.4.rest_8_ = bf16[25,8,1152]{2,1,0:T(8,128)(2,1)S(1)} collective-permute-done((bf16[25,8,1152]{2,1,0:T(8,128)(2,1)}, bf16[25,8,1152]{2,1,0:T(8,128)(2,1)S(1)}, u32[]{:S(2)}, u32[]{:S(2)}) %collective-permute-start.4) | collective-permute-done | bytes 460832 | tf_op jit(solution)/shard_map/ppermute | solution.py:513
  33.8 1.4 %collective-permute-start.9 = (bf16[24,8,1152]{2,1,0:T(8,128)(2,1)}, bf16[24,8,1152]{2,1,0:T(8,128)(2,1)S(1)}, u32[]{:S(2)}, u32[]{:S(2)}) collective-permute-start(bf16[24,8,1152]{2,1,0:T(8,128)(2,1)} %get-tuple-element.85), channel_id=1, source_target_pairs={{0,3},{1,2},{2,1},{3,0},{4,7},{5,6},{6,5},{7,4},{8,11},{9,10},{10,... | collective-permute-start | bytes 1327112 | tf_op jit(solution)/shard_map/ppermute | solution.py:513
  36.9 17.4 %shard_map.121 = (bf16[25,8,1152]{2,1,0:T(8,128)(2,1)}, bf16[25,8,1152]{2,1,0:T(8,128)(2,1)}, bf16[25,8,1152]{2,1,0:T(8,128)(2,1)}, bf16[196,8,384]{2,1,0:T(8,12...) custom-call(s32[1]{0:T(128)S(6)} %copy.25.count_ref, s32[1,2]{1,0:T(1,128)} %starts_ref.3, ...), custom_call_target="tpu_custom_call" | custom-call | tf_op jit(solution)/shard_map/pallas_call | solution.py:466
  55.7 1.5 %collective-permute-start.11 = (bf16[25,8,1152]{2,1,0:T(8,128)(2,1)}, bf16[25,8,1152]{2,1,0:T(8,128)(2,1)S(1)}, u32[]{:S(2)}, u32[]{:S(2)}) collective-permute-start(bf16[25,8,1152]{2,1,0:T(8,128)(2,1)} %get-tuple-element.98), channel_id=1, source_target_pairs={{0,2},{1,3},{2,0},{3,1},{4,6},{5,7},{6,4},{7,5},{8,10},{9,11},{10,... | collective-permute-start | bytes 1382408 | tf_op jit(solution)/shard_map/ppermute | solution.py:513
  58.4 16.7 %shard_map.122 = (bf16[24,8,1152]{2,1,0:T(8,128)(2,1)}, bf16[24,8,1152]{2,1,0:T(8,128)(2,1)}, bf16[24,8,1152]{2,1,0:T(8,128)(2,1)}, bf16[196,8,384]{2,1,0:T(8,12...) custom-call(s32[1]{0:T(128)S(6)} %copy.25.count_ref, ...), custom_call_target="tpu_custom_call", output_to_operand_aliasing={{3}: (15, {}), {4}: (16, {})} | custom-call | tf_op jit(solution)/shard_map/pallas_call | solution.py:466
  75.2 2.3 %collective-permute-done.12.refs_4_ = bf16[25,8,1152]{2,1,0:T(8,128)(2,1)S(1)} collective-permute-done((bf16[25,8,1152]{2,1,0:T(8,128)(2,1)}, bf16[25,8,1152]{2,1,0:T(8,128)(2,1)S(1)}, u32[]{:S(2)}, u32[]{:S(2)}) %collective-permute-start.12) | collective-permute-done | bytes 460832 | tf_op jit(solution)/shard_map/ppermute | solution.py:513
  78.0 1.4 %collective-permute-start.17 = (bf16[24,8,1152]{2,1,0:T(8,128)(2,1)}, bf16[24,8,1152]{2,1,0:T(8,128)(2,1)S(1)}, u32[]{:S(2)}, u32[]{:S(2)}) collective-permute-start(bf16[24,8,1152]{2,1,0:T(8,128)(2,1)} %get-tuple-element.112), channel_id=1, source_target_pairs={{0,1},{1,0},{2,3},{3,2},{4,5},{5,4},{6,7},{7,6},{8,9},{9,8},{10,11... | collective-permute-start | bytes 1327112 | tf_op jit(solution)/shard_map/ppermute | solution.py:513
  82.7 1.6 %collective-permute-start.15 = (bf16[2,48,1152]{2,1,0:T(8,128)(2,1)S(1)}, bf16[2,48,1152]{2,1,0:T(8,128)(2,1)S(1)}, u32[]{:S(2)}, u32[]{:S(2)}) collective-permute-start(bf16[2,48,1152]{2,1,0:T(8,128)(2,1)S(1)} %slice.74), channel_id=1, source_target_pairs={{0,8},{4,12},{8,0},{12,4},{16,24},{20,28},{24,16},{28,20},{1,9},{5... | collective-permute-start | bytes 663560 | tf_op jit(solution)/shard_map/ppermute | solution.py:521
  85.0 2.2 %shard_map.123 = (bf16[196,8,384]{2,1,0:T(8,128)(2,1)}, bf16[196,8,768]{2,1,0:T(8,128)(2,1)}) custom-call(bf16[196,8,384]{2,1,0:T(8,128)(2,1)} %get-tuple-element.93.refs_0_, bf16[196,8,768]{2,1,0:T(8,128)(2,1)} %get-tuple-element.94.refs_1_, bf16[25,8,1152]{2,1,0:T(8,128)(2,1)} %copy-done.9, ...), custom_call_target="tpu_custom_call", output_to_operand_aliasing={{0}: (0, {}), {1}: (1, {})} | custom-call | tf_op jit(solution)/shard_map/pallas_call | solution.py:123
  87.2 3.9 %collective-permute-done.15 = bf16[2,48,1152]{2,1,0:T(8,128)(2,1)S(1)} collective-permute-done((bf16[2,48,1152]{2,1,0:T(8,128)(2,1)S(1)}, bf16[2,48,1152]{2,1,0:T(8,128)(2,1)S(1)}, u32[]{:S(2)}, u32[]{:S(2)}) %collective-permute-start.15) | collective-permute-done | bytes 221216 | tf_op jit(solution)/shard_map/ppermute | solution.py:521
  91.6 5.4 %collective-permute-done.22 = bf16[2,56,1152]{2,1,0:T(8,128)(2,1)S(1)} collective-permute-done((bf16[2,56,1152]{2,1,0:T(8,128)(2,1)S(1)}, bf16[2,56,1152]{2,1,0:T(8,128)(2,1)S(1)}, u32[]{:S(2)}, u32[]{:S(2)}) %collective-permute-start.22) | collective-permute-done | bytes 258080 | tf_op jit(solution)/shard_map/ppermute | solution.py:521
  97.2 2.4 %collective-permute-done.16 = bf16[1,48,1152]{2,1,0:T(8,128)(2,1)S(1)} collective-permute-done((bf16[1,48,1152]{2,1,0:T(8,128)(2,1)S(1)}, bf16[1,48,1152]{2,1,0:T(8,128)(2,1)S(1)}, u32[]{:S(2)}, u32[]{:S(2)}) %collective-permute-start.16) | collective-permute-done | bytes 110624 | tf_op jit(solution)/shard_map/ppermute | solution.py:521
  99.6 1.4 %collective-permute-done.18.refs_3_ = bf16[24,8,1152]{2,1,0:T(8,128)(2,1)S(1)} collective-permute-done((bf16[24,8,1152]{2,1,0:T(8,128)(2,1)}, bf16[24,8,1152]{2,1,0:T(8,128)(2,1)S(1)}, u32[]{:S(2)}, u32[]{:S(2)}) %collective-permute-start.18) | collective-permute-done | bytes 442400 | tf_op jit(solution)/shard_map/ppermute | solution.py:513
  101.7 2.7 %collective-permute-done.23 = bf16[1,56,1152]{2,1,0:T(8,128)(2,1)S(1)} collective-permute-done((bf16[1,56,1152]{2,1,0:T(8,128)(2,1)S(1)}, bf16[1,56,1152]{2,1,0:T(8,128)(2,1)S(1)}, u32[]{:S(2)}, u32[]{:S(2)}) %collective-permute-start.23) | collective-permute-done | bytes 129056 | tf_op jit(solution)/shard_map/ppermute | solution.py:521
  104.4 1.5 %collective-permute-start.24 = (bf16[56,1152]{1,0:T(8,128)(2,1)S(1)}, bf16[56,1152]{1,0:T(8,128)(2,1)S(1)}, u32[]{:S(2)}, u32[]{:S(2)}) collective-permute-start(bf16[56,1152]{1,0:T(8,128)(2,1)S(1)} %fusion.2), channel_id=1, source_target_pairs={{0,1},{1,0},{2,3},{3,2},{4,5},{5,4},{6,7},{7,6},{8,9},{9,8},{10,11... | collective-permute-start | bytes 387080 | tf_op jit(solution)/shard_map/ppermute | solution.py:513
  109.2 2.2 %shard_map.124 = (bf16[196,8,384]{2,1,0:T(8,128)(2,1)}, bf16[196,8,768]{2,1,0:T(8,128)(2,1)}) custom-call(bf16[196,8,384]{2,1,0:T(8,128)(2,1)} %get-tuple-element.108.refs_0_, bf16[196,8,768]{2,1,0:T(8,128)(2,1)} %get-tuple-element.109.refs_1_, bf16[24,8,1152]{2,1,0:T(8,128)(2,1)} %copy-done.12, ...), custom_call_target="tpu_custom_call", output_to_operand_aliasing={{0}: (0, {}), {1}: (1, {})} | custom-call | tf_op jit(solution)/shard_map/pallas_call | solution.py:123
  111.4 1.5 %collective-permute-done.26 = bf16[56,1152]{1,0:T(8,128)(2,1)S(1)} collective-permute-done((bf16[56,1152]{1,0:T(8,128)(2,1)S(1)}, bf16[56,1152]{1,0:T(8,128)(2,1)S(1)}, u32[]{:S(2)}, u32[]{:S(2)}) %collective-permute-start.26) | collective-permute-done | bytes 129056 | tf_op jit(solution)/shard_map/ppermute | solution.py:513
  (90 shorter events, 18.6 us)
Async XLA Ops:
  3.9 15.4 %collective-permute-start.1 = (bf16[104,1152]{1,0:T(8,128)(2,1)}, bf16[104,1152]{1,0:T(8,128)(2,1)S(1)}, u32[]{:S(2)}, u32[]{:S(2)}) collective-permute-start(bf16[104,1152]{1,0:T(8,128)(2,1)} %get-tuple-element.73.rest_0_), channel_id=1, source_target_pairs={{0,16},{4,20},{8,24},{12,28},{16,0},{20,4},{24,8},{28,12},{1,17},{... | collective-permute-start | bytes 718856 | tf_op jit(solution)/shard_map/ppermute | solution.py:521
  8.0 15.1 %collective-permute-start.3 = (bf16[25,8,1152]{2,1,0:T(8,128)(2,1)}, bf16[25,8,1152]{2,1,0:T(8,128)(2,1)S(1)}, u32[]{:S(2)}, u32[]{:S(2)}) collective-permute-start(bf16[25,8,1152]{2,1,0:T(8,128)(2,1)} %get-tuple-element.67), channel_id=1, source_target_pairs={{0,1},{1,0},{2,3},{3,2},{4,5},{5,4},{6,7},{7,6},{8,9},{9,8},{10,11... | collective-permute-start | bytes 1382408 | tf_op jit(solution)/shard_map/ppermute | solution.py:513
  9.5 21.8 %collective-permute-start.4 = (bf16[25,8,1152]{2,1,0:T(8,128)(2,1)}, bf16[25,8,1152]{2,1,0:T(8,128)(2,1)S(1)}, u32[]{:S(2)}, u32[]{:S(2)}) collective-permute-start(bf16[25,8,1152]{2,1,0:T(8,128)(2,1)} %get-tuple-element.68), channel_id=1, source_target_pairs={{0,2},{1,3},{2,0},{3,1},{4,6},{5,7},{6,4},{7,5},{8,10},{9,11},{10,... | collective-permute-start | bytes 1382408 | tf_op jit(solution)/shard_map/ppermute | solution.py:513
  11.1 20.3 %collective-permute-start.5 = (bf16[25,8,1152]{2,1,0:T(8,128)(2,1)}, bf16[25,8,1152]{2,1,0:T(8,128)(2,1)S(1)}, u32[]{:S(2)}, u32[]{:S(2)}) collective-permute-start(bf16[25,8,1152]{2,1,0:T(8,128)(2,1)} %get-tuple-element.69), channel_id=1, source_target_pairs={{0,3},{1,2},{2,1},{3,0},{4,7},{5,6},{6,5},{7,4},{8,11},{9,10},{10,... | collective-permute-start | bytes 1382408 | tf_op jit(solution)/shard_map/ppermute | solution.py:513
  11.5 11.6 %collective-permute-start = (bf16[104,1152]{1,0:T(8,128)(2,1)}, bf16[104,1152]{1,0:T(8,128)(2,1)S(1)}, u32[]{:S(2)}, u32[]{:S(2)}) collective-permute-start(bf16[104,1152]{1,0:T(8,128)(2,1)} %get-tuple-element.73.rest_0_), channel_id=1, source_target_pairs={{0,8},{4,12},{8,0},{12,4},{16,24},{20,28},{24,16},{28,20},{1,9},{5... | collective-permute-start | bytes 718856 | tf_op jit(solution)/shard_map/ppermute | solution.py:521
  19.3 12.1 %collective-permute-start.2 = (bf16[104,1152]{1,0:T(8,128)(2,1)S(1)}, bf16[104,1152]{1,0:T(8,128)(2,1)S(1)}, u32[]{:S(2)}, u32[]{:S(2)}) collective-permute-start(bf16[104,1152]{1,0:T(8,128)(2,1)S(1)} %collective-permute-done.1.rest_2_), channel_id=1, source_target_pairs={{0,8},{4,12},{8,0},{12,4},{16,24},{20,28},{24,16},{28,20},{1,9},{5... | collective-permute-start | bytes 718856 | tf_op jit(solution)/shard_map/ppermute | solution.py:521
  31.6 22.6 %collective-permute-start.7 = (bf16[24,8,1152]{2,1,0:T(8,128)(2,1)}, bf16[24,8,1152]{2,1,0:T(8,128)(2,1)S(1)}, u32[]{:S(2)}, u32[]{:S(2)}) collective-permute-start(bf16[24,8,1152]{2,1,0:T(8,128)(2,1)} %get-tuple-element.83), channel_id=1, source_target_pairs={{0,1},{1,0},{2,3},{3,2},{4,5},{5,4},{6,7},{7,6},{8,9},{9,8},{10,11... | collective-permute-start | bytes 1327112 | tf_op jit(solution)/shard_map/ppermute | solution.py:513
  32.9 21.3 %collective-permute-start.8 = (bf16[24,8,1152]{2,1,0:T(8,128)(2,1)}, bf16[24,8,1152]{2,1,0:T(8,128)(2,1)S(1)}, u32[]{:S(2)}, u32[]{:S(2)}) collective-permute-start(bf16[24,8,1152]{2,1,0:T(8,128)(2,1)} %get-tuple-element.84), channel_id=1, source_target_pairs={{0,2},{1,3},{2,0},{3,1},{4,6},{5,7},{6,4},{7,5},{8,10},{9,11},{10,... | collective-permute-start | bytes 1327112 | tf_op jit(solution)/shard_map/ppermute | solution.py:513
  33.8 21.1 %collective-permute-start.9 = (bf16[24,8,1152]{2,1,0:T(8,128)(2,1)}, bf16[24,8,1152]{2,1,0:T(8,128)(2,1)S(1)}, u32[]{:S(2)}, u32[]{:S(2)}) collective-permute-start(bf16[24,8,1152]{2,1,0:T(8,128)(2,1)} %get-tuple-element.85), channel_id=1, source_target_pairs={{0,3},{1,2},{2,1},{3,0},{4,7},{5,6},{6,5},{7,4},{8,11},{9,10},{10,... | collective-permute-start | bytes 1327112 | tf_op jit(solution)/shard_map/ppermute | solution.py:513
  54.9 20.3 %collective-permute-start.10 = (bf16[25,8,1152]{2,1,0:T(8,128)(2,1)}, bf16[25,8,1152]{2,1,0:T(8,128)(2,1)S(1)}, u32[]{:S(2)}, u32[]{:S(2)}) collective-permute-start(bf16[25,8,1152]{2,1,0:T(8,128)(2,1)} %get-tuple-element.97), channel_id=1, source_target_pairs={{0,1},{1,0},{2,3},{3,2},{4,5},{5,4},{6,7},{7,6},{8,9},{9,8},{10,11... | collective-permute-start | bytes 1382408 | tf_op jit(solution)/shard_map/ppermute | solution.py:513
  55.7 19.4 %collective-permute-start.11 = (bf16[25,8,1152]{2,1,0:T(8,128)(2,1)}, bf16[25,8,1152]{2,1,0:T(8,128)(2,1)S(1)}, u32[]{:S(2)}, u32[]{:S(2)}) collective-permute-start(bf16[25,8,1152]{2,1,0:T(8,128)(2,1)} %get-tuple-element.98), channel_id=1, source_target_pairs={{0,2},{1,3},{2,0},{3,1},{4,6},{5,7},{6,4},{7,5},{8,10},{9,11},{10,... | collective-permute-start | bytes 1382408 | tf_op jit(solution)/shard_map/ppermute | solution.py:513
  57.3 20.3 %collective-permute-start.12 = (bf16[25,8,1152]{2,1,0:T(8,128)(2,1)}, bf16[25,8,1152]{2,1,0:T(8,128)(2,1)S(1)}, u32[]{:S(2)}, u32[]{:S(2)}) collective-permute-start(bf16[25,8,1152]{2,1,0:T(8,128)(2,1)} %get-tuple-element.99), channel_id=1, source_target_pairs={{0,3},{1,2},{2,1},{3,0},{4,7},{5,6},{6,5},{7,4},{8,11},{9,10},{10,... | collective-permute-start | bytes 1382408 | tf_op jit(solution)/shard_map/ppermute | solution.py:513
  78.0 21.6 %collective-permute-start.17 = (bf16[24,8,1152]{2,1,0:T(8,128)(2,1)}, bf16[24,8,1152]{2,1,0:T(8,128)(2,1)S(1)}, u32[]{:S(2)}, u32[]{:S(2)}) collective-permute-start(bf16[24,8,1152]{2,1,0:T(8,128)(2,1)} %get-tuple-element.112), channel_id=1, source_target_pairs={{0,1},{1,0},{2,3},{3,2},{4,5},{5,4},{6,7},{7,6},{8,9},{9,8},{10,11... | collective-permute-start | bytes 1327112 | tf_op jit(solution)/shard_map/ppermute | solution.py:513
  79.4 21.6 %collective-permute-start.18 = (bf16[24,8,1152]{2,1,0:T(8,128)(2,1)}, bf16[24,8,1152]{2,1,0:T(8,128)(2,1)S(1)}, u32[]{:S(2)}, u32[]{:S(2)}) collective-permute-start(bf16[24,8,1152]{2,1,0:T(8,128)(2,1)} %get-tuple-element.113), channel_id=1, source_target_pairs={{0,2},{1,3},{2,0},{3,1},{4,6},{5,7},{6,4},{7,5},{8,10},{9,11},{10,... | collective-permute-start | bytes 1327112 | tf_op jit(solution)/shard_map/ppermute | solution.py:513
  80.4 20.6 %collective-permute-start.19 = (bf16[24,8,1152]{2,1,0:T(8,128)(2,1)}, bf16[24,8,1152]{2,1,0:T(8,128)(2,1)S(1)}, u32[]{:S(2)}, u32[]{:S(2)}) collective-permute-start(bf16[24,8,1152]{2,1,0:T(8,128)(2,1)} %get-tuple-element.114), channel_id=1, source_target_pairs={{0,3},{1,2},{2,1},{3,0},{4,7},{5,6},{6,5},{7,4},{8,11},{9,10},{10,... | collective-permute-start | bytes 1327112 | tf_op jit(solution)/shard_map/ppermute | solution.py:513
  82.7 8.4 %collective-permute-start.15 = (bf16[2,48,1152]{2,1,0:T(8,128)(2,1)S(1)}, bf16[2,48,1152]{2,1,0:T(8,128)(2,1)S(1)}, u32[]{:S(2)}, u32[]{:S(2)}) collective-permute-start(bf16[2,48,1152]{2,1,0:T(8,128)(2,1)S(1)} %slice.74), channel_id=1, source_target_pairs={{0,8},{4,12},{8,0},{12,4},{16,24},{20,28},{24,16},{28,20},{1,9},{5... | collective-permute-start | bytes 663560 | tf_op jit(solution)/shard_map/ppermute | solution.py:521
  84.5 12.5 %collective-permute-start.22 = (bf16[2,56,1152]{2,1,0:T(8,128)(2,1)S(1)}, bf16[2,56,1152]{2,1,0:T(8,128)(2,1)S(1)}, u32[]{:S(2)}, u32[]{:S(2)}) collective-permute-start(bf16[2,56,1152]{2,1,0:T(8,128)(2,1)S(1)} %slice.73), channel_id=1, source_target_pairs={{0,8},{4,12},{8,0},{12,4},{16,24},{20,28},{24,16},{28,20},{1,9},{5... | collective-permute-start | bytes 774152 | tf_op jit(solution)/shard_map/ppermute | solution.py:521
  91.2 8.4 %collective-permute-start.16 = (bf16[1,48,1152]{2,1,0:T(8,128)(2,1)S(1)}, bf16[1,48,1152]{2,1,0:T(8,128)(2,1)S(1)}, u32[]{:S(2)}, u32[]{:S(2)}) collective-permute-start(bf16[1,48,1152]{2,1,0:T(8,128)(2,1)S(1)} %slice.76), channel_id=1, source_target_pairs={{0,16},{4,20},{8,24},{12,28},{16,0},{20,4},{24,8},{28,12},{1,17},{... | collective-permute-start | bytes 331784 | tf_op jit(solution)/shard_map/ppermute | solution.py:521
  97.1 7.3 %collective-permute-start.23 = (bf16[1,56,1152]{2,1,0:T(8,128)(2,1)S(1)}, bf16[1,56,1152]{2,1,0:T(8,128)(2,1)S(1)}, u32[]{:S(2)}, u32[]{:S(2)}) collective-permute-start(bf16[1,56,1152]{2,1,0:T(8,128)(2,1)S(1)} %slice.75), channel_id=1, source_target_pairs={{0,16},{4,20},{8,24},{12,28},{16,0},{20,4},{24,8},{28,12},{1,17},{... | collective-permute-start | bytes 387080 | tf_op jit(solution)/shard_map/ppermute | solution.py:521
  101.0 7.0 %collective-permute-start.20 = (bf16[48,1152]{1,0:T(8,128)(2,1)S(1)}, bf16[48,1152]{1,0:T(8,128)(2,1)S(1)}, u32[]{:S(2)}, u32[]{:S(2)}) collective-permute-start(bf16[48,1152]{1,0:T(8,128)(2,1)S(1)} %fusion.1), channel_id=1, source_target_pairs={{0,1},{1,0},{2,3},{3,2},{4,5},{5,4},{6,7},{7,6},{8,9},{9,8},{10,11... | collective-permute-start | bytes 331784 | tf_op jit(solution)/shard_map/ppermute | solution.py:513
  104.4 6.9 %collective-permute-start.24 = (bf16[56,1152]{1,0:T(8,128)(2,1)S(1)}, bf16[56,1152]{1,0:T(8,128)(2,1)S(1)}, u32[]{:S(2)}, u32[]{:S(2)}) collective-permute-start(bf16[56,1152]{1,0:T(8,128)(2,1)S(1)} %fusion.2), channel_id=1, source_target_pairs={{0,1},{1,0},{2,3},{3,2},{4,5},{5,4},{6,7},{7,6},{8,9},{9,8},{10,11... | collective-permute-start | bytes 387080 | tf_op jit(solution)/shard_map/ppermute | solution.py:513
  106.0 5.4 %collective-permute-start.25 = (bf16[56,1152]{1,0:T(8,128)(2,1)S(1)}, bf16[56,1152]{1,0:T(8,128)(2,1)S(1)}, u32[]{:S(2)}, u32[]{:S(2)}) collective-permute-start(bf16[56,1152]{1,0:T(8,128)(2,1)S(1)} %fusion.2), channel_id=1, source_target_pairs={{0,2},{1,3},{2,0},{3,1},{4,6},{5,7},{6,4},{7,5},{8,10},{9,11},{10,... | collective-permute-start | bytes 387080 | tf_op jit(solution)/shard_map/ppermute | solution.py:513
  106.9 5.9 %collective-permute-start.26 = (bf16[56,1152]{1,0:T(8,128)(2,1)S(1)}, bf16[56,1152]{1,0:T(8,128)(2,1)S(1)}, u32[]{:S(2)}, u32[]{:S(2)}) collective-permute-start(bf16[56,1152]{1,0:T(8,128)(2,1)S(1)} %fusion.2), channel_id=1, source_target_pairs={{0,3},{1,2},{2,1},{3,0},{4,7},{5,6},{6,5},{7,4},{8,11},{9,10},{10,... | collective-permute-start | bytes 387080 | tf_op jit(solution)/shard_map/ppermute | solution.py:513
  108.0 6.0 %collective-permute-start.21 = (bf16[48,1152]{1,0:T(8,128)(2,1)S(1)}, bf16[48,1152]{1,0:T(8,128)(2,1)S(1)}, u32[]{:S(2)}, u32[]{:S(2)}) collective-permute-start(bf16[48,1152]{1,0:T(8,128)(2,1)S(1)} %add_convert_fusion), channel_id=1, source_target_pairs={{0,2},{1,3},{2,0},{3,1},{4,6},{5,7},{6,4},{7,5},{8,10},{9,11},{10,... | collective-permute-start | bytes 331784 | tf_op jit(solution)/shard_map/ppermute | solution.py:513
  (21 other events, 164.6 us)

commit v6 on v5

--- a/solution.py
+++ b/solution.py
@@ -11,6 +11,7 @@
 BLOCK = 16
 CORES = 2
 EXTRA = 8
+CARRIED = 16
 
 masked_value = -1e30
 epsilon = 1e-05
@@ -157,6 +158,7 @@
     groups,
     patches_dev,
     offset,
+    carry,
     first,
     last,
     count_ref,
@@ -171,9 +173,11 @@
     x_ref, grad_ref = take(2)
     sources = take(tm_count - 1)
     if not first:
+        carried = take(tm_count - 1) if carry else []
         before, before_ends = take(2)
         take(2)
     outs = take(tm_count - 1)
+    rests = take(tm_count - 1) if first and carry else []
     mixed_ref, tokens_ref = take(2)
     sums = take(4) if last else take(2)
     (xs, weight, extra, normed, standard, proj, pgrad, back, acc, ends, tails, allow, sems) = rest
@@ -239,6 +243,9 @@
     )
     for copy in rows_in:
         copy.wait()
+    gone = []
+    if not first:
+        gone += [bring(ref, outs[r].at[pl.ds(0, carry)]) for r, ref in enumerate(carried)]
 
     unit = tokens // groups
 
@@ -254,7 +261,7 @@
             block = values[r * span : (r + 1) * span].reshape(group, frames, -1)
             back[r, rows, :, cut] = block.astype(bf16)
 
-    @pl.loop(0, groups)
+    @pl.loop(0, groups, unroll=2)
     def _(j):
         x = token_rows(j, slice(0, width))
         centred = x - jnp.mean(x, axis=-1, keepdims=True)
@@ -300,7 +307,7 @@
     nt = (((1,), (1,)), ((), ()))
     tn = (((0,), (0,)), ((), ()))
 
-    @pl.loop(0, groups)
+    @pl.loop(0, groups, unroll=2)
     def _(j):
         at = pl.ds(pl.multiple_of(j * unit, unit), unit)
         allowed = allow[...] > 0.5
@@ -358,9 +365,18 @@
         else:
             acc[:, cut] += share
 
-    gone = []
     if not last:
         gone.append(bring(acc, sums[0]))
+    else:
+        cut = sums[0].shape[1]
+        for k, far in enumerate(halving_order(nz)):
+            owner = (z ^ far) * CORES
+            for refs, side in ((sums[:2], core), (sums[2:], 1 - core)):
+                start = pl.multiple_of((owner + side) * shard, shard)
+                refs[0][k] = acc[pl.ds(start, cut), :].astype(bf16)
+                refs[1][k, : shard - cut, :] = acc[
+                    pl.ds(pl.multiple_of(start + cut, 16), shard - cut), :
+                ].astype(bf16)
     normed[...] = lax.dot_general(
         pgrad[...], weight[...], nt, preferred_element_type=f32
     ).astype(bf16)
@@ -382,12 +398,20 @@
 
     middle = (groups + 1) // 2
     for low_group, high_group in ((0, middle), (middle, groups)):
-        pl.loop(low_group, high_group)(finish)
+        pl.loop(low_group, high_group, unroll=2)(finish)
         start = low_group * group
         count = min(high_group * group, size) - start
         here, there = pl.ds(start, count), pl.ds(me * patches_dev + offset + start, count)
+        now = max(0, min(start + count, size - carry) - start) if first else count
+        shift = 0 if first else carry
         for r in range(1, tm_count):
-            gone.append(bring(back.at[r, here], outs[r - 1].at[here]))
+            if now:
+                part = back.at[r, pl.ds(start, now)]
+                gone.append(bring(part, outs[r - 1].at[pl.ds(start + shift, now)]))
+            if now < count:
+                part = back.at[r, pl.ds(start + now, count - now)]
+                there_rest = pl.ds(start + now - (size - carry), count - now)
+                gone.append(bring(part, rests[r - 1].at[there_rest]))
         gone.append(bring(back.at[0, here, :, pl.ds(0, joined)], mixed_ref.at[there]))
         gone.append(bring(back.at[0, here, :, pl.ds(joined, width)], tokens_ref.at[there]))
     if not last:
@@ -402,22 +426,27 @@
             ],
             axis=0,
         ).astype(bf16)
-        for k, far in enumerate(halving_order(nz)):
-            owner = (z ^ far) * CORES
-            for refs, side in ((sums[:2], core), (sums[2:], 1 - core)):
-                start = pl.multiple_of((owner + side) * shard, shard)
-                refs[0][k] = acc[pl.ds(start, cut), :].astype(bf16)
-                refs[1][k, : shard - cut, :] = acc[
-                    pl.ds(pl.multiple_of(start + cut, 16), shard - cut), :
-                ].astype(bf16)
-                refs[1][k, shard - cut :, :width] = extra_rows
-                refs[1][k, shard - cut :, width:] = jnp.zeros((EXTRA, columns - width), bf16)
+        for k in range(nz):
+            for ref in (sums[1], sums[3]):
+                ref[k, shard - cut :, :width] = extra_rows
+                ref[k, shard - cut :, width:] = jnp.zeros((EXTRA, columns - width), bf16)
     for copy in gone:
         copy.wait()
 
 
 def chunk(
-    tm_count, dp_count, group, patches_dev, offset, first, last, facts, pieces, sources, before
+    tm_count,
+    dp_count,
+    group,
+    patches_dev,
+    offset,
+    carry,
+    first,
+    last,
+    facts,
+    pieces,
+    sources,
+    before,
 ):
     tokens_in, grads_in, blocks = sources
     size, frames, total = blocks[0].shape
@@ -426,7 +455,10 @@
     groups = -(-size // group)
     tokens = groups * group * frames * tm_count
     nz = dp_count // CORES
-    outs = [jax.ShapeDtypeStruct((size, frames, total), bf16)] * (tm_count - 1)
+    leaving = size - carry if first else size + carry
+    outs = [jax.ShapeDtypeStruct((leaving, frames, total), bf16)] * (tm_count - 1)
+    if first and carry:
+        outs += [jax.ShapeDtypeStruct((carry, frames, total), bf16)] * (tm_count - 1)
     outs += [
         jax.ShapeDtypeStruct(grads_in.shape, bf16),
         jax.ShapeDtypeStruct(tokens_in.shape, bf16),
@@ -461,7 +493,7 @@
         pltpu.VMEM((tokens, 128), f32),
         pltpu.VMEM((16, width), f32),
         pltpu.VMEM((tm_count * frames, tokens // groups), f32),
-        pltpu.SemaphoreType.DMA((3 * tm_count + 2 * dp_count + 14,)),
+        pltpu.SemaphoreType.DMA((6 * tm_count + 2 * dp_count + 14,)),
     ]
     return pl.pallas_call(
         functools.partial(
@@ -473,6 +505,7 @@
             groups,
             patches_dev,
             offset,
+            carry,
             first,
             last,
         ),
@@ -536,6 +569,7 @@
     gathered = [early, [swap(part, r + 1) for r, part in enumerate(late)]]
 
     facts = (frame_counts, clip_starts, frame_kept)
+    carry = patches_dev // CARRIED
     results, before = [], None
     for c in range(len(chunks)):
         blocks = gathered[c]
@@ -546,6 +580,7 @@
             group,
             patches_dev,
             offsets[c],
+            carry,
             first,
             last,
             facts,
@@ -557,8 +592,8 @@
         if first:
             leaving, gathered[1] = lax.optimization_barrier((leaving, gathered[1]))
         results.append([swap(part, r + 1) for r, part in enumerate(leaving)])
-        mixed, grads = got[tm_count - 1 : tm_count + 1]
-        before = (got[tm_count + 1], got[tm_count + 2], mixed, grads)
+        mixed, grads = got[-6:-4] if last else got[-4:-2]
+        before = list(got[tm_count - 1 : -4]) + [got[-2], got[-1], mixed, grads]
     keep, send = got[-4:-2], got[-2:]
 
     send, results[0] = lax.optimization_barrier((send, results[0]))
@@ -591,10 +626,9 @@
             r *= 2
         summed.append(half)
 
-    for c, blocks in enumerate(results):
-        mixed, grads = unpack(
-            tm_count, patches_dev, offsets[c], chunks[c], mixed, grads, blocks
-        )
+    lead = chunks[0] - carry
+    for start, size, blocks in zip((0, lead), (lead, patches_dev - lead), results):
+        mixed, grads = unpack(tm_count, patches_dev, start, size, mixed, grads, blocks)
     attended = mixed[:patches].transpose(1, 0, 2)[None]
     tokens_grad = grads[:patches].transpose(1, 0, 2)[None]
     rest = shard - summed[0].shape[0]

time: 115 us -> 113 us (0.983)
  Pallas kernels: 44.2 us -> 41.8 us
    ppermute x17, waiting for transfers between devices: 14.5 us -> 17.9 us  [swap(): return lax.ppermute(array, 'tm', partner(tm_count, r))]
    pallas_call x2, Pallas kernels: 34.1 us -> 31.7 us  [chunk(): pl.pallas_call(functools.partial(chunk_kernel, tm_count, dp_count, frames...]
    ppermute x10, waiting for transfers between devices: 21.2 us -> 19 us  [across(): return lax.ppermute(array, 'dp', partner(dp_count, k))]
  transfers between devices with their start and end apart: 27 -> 27, of which waited for: 12 -> 14; matrix products, arithmetic and copies ran while one was open for 2% -> 2% of each run, Pallas kernels for 36% -> 34%
where the time goes in v6:
time: 113 us
  Pallas kernels  41.8 us (37%)
  waiting for transfers between devices  36.8 us (33%)
  starting transfers between devices  28.7 us (25%)
  other arithmetic  2.44 us (2%)
  local copies, waits for them, and re-layouts  1.72 us (2%)
  between operations  1.65 us (1%)
    pallas_call x2, Pallas kernels, chunk(): pl.pallas_call(functools.partial(chunk_kernel, tm_count, dp_count, frames...  31.7 us
    ppermute x10, waiting for transfers between devices, across(): return lax.ppermute(array, 'dp', partner(dp_count, k))  19 us
    ppermute x17, starting transfers between devices, swap(): return lax.ppermute(array, 'tm', partner(tm_count, r))  18.9 us
    ppermute x17, waiting for transfers between devices, swap(): return lax.ppermute(array, 'tm', partner(tm_count, r))  17.9 us
    ppermute x10, starting transfers between devices, across(): return lax.ppermute(array, 'dp', partner(dp_count, k))  9.73 us
    pallas_call x2, Pallas kernels, pack(): pl.pallas_call(functools.partial(pack_kernel, tm_count, patches_dev, offs...  5.72 us
    pallas_call x2, Pallas kernels, unpack(): pl.pallas_call(functools.partial(unpack_kernel, tm_count, patches_dev, of...  4.36 us
  transfers between devices with their start and end apart: 27, of which 14 were waited for; matrix products, arithmetic and copies ran while one was open for 2% of the time, Pallas kernels for 34%

profile of v6, /device:TPU:0, one launch (start us, length us, event | category | flops | bytes accessed | tf_op | source)
XLA Modules:
  0.0 113.1 jit_solution(4888638511889955260)
XLA Ops:
  0.6 3.3 %shard_map.119 = (bf16[104,1152]{1,0:T(8,128)(2,1)}, bf16[25,8,1152]{2,1,0:T(8,128)(2,1)}, bf16[25,8,1152]{2,1,0:T(8,128)(2,1)}, bf16[25,8,1152]{2,1,0:T(8,128)(2,1)}) custom-call(bf16[196,8,768]{2,1,0:T(8,128)(2,1)} %bitcast.24, bf16[196,8,384]{2,1,0:T(8,128)(2,1)} %bitcast.29, bf16[96,1152]{1,0:T(8,128)(2,1)} %rest_0_.1, bf16[96]{0:T(256)(128)(2,1)} %rest_1_.1, ...), custom_call_target="tpu_custom_call" | custom-call | tf_op jit(solution)/shard_map/pallas_call | solution.py:91
  3.9 4.1 %collective-permute-start.1 = (bf16[104,1152]{1,0:T(8,128)(2,1)}, bf16[104,1152]{1,0:T(8,128)(2,1)S(1)}, u32[]{:S(2)}, u32[]{:S(2)}) collective-permute-start(bf16[104,1152]{1,0:T(8,128)(2,1)} %get-tuple-element.76.rest_0_), channel_id=1, source_target_pairs={{0,16},{4,20},{8,24},{12,28},{16,0},{20,4},{24,8},{28,12},{1,17},{... | collective-permute-start | bytes 718856 | tf_op jit(solution)/shard_map/ppermute | solution.py:554
  8.0 1.5 %collective-permute-start.3 = (bf16[25,8,1152]{2,1,0:T(8,128)(2,1)}, bf16[25,8,1152]{2,1,0:T(8,128)(2,1)S(1)}, u32[]{:S(2)}, u32[]{:S(2)}) collective-permute-start(bf16[25,8,1152]{2,1,0:T(8,128)(2,1)} %get-tuple-element.70), channel_id=1, source_target_pairs={{0,1},{1,0},{2,3},{3,2},{4,5},{5,4},{6,7},{7,6},{8,9},{9,8},{10,11... | collective-permute-start | bytes 1382408 | tf_op jit(solution)/shard_map/ppermute | solution.py:546
  9.5 1.5 %collective-permute-start.4 = (bf16[25,8,1152]{2,1,0:T(8,128)(2,1)}, bf16[25,8,1152]{2,1,0:T(8,128)(2,1)S(1)}, u32[]{:S(2)}, u32[]{:S(2)}) collective-permute-start(bf16[25,8,1152]{2,1,0:T(8,128)(2,1)} %get-tuple-element.71), channel_id=1, source_target_pairs={{0,2},{1,3},{2,0},{3,1},{4,6},{5,7},{6,4},{7,5},{8,10},{9,11},{10,... | collective-permute-start | bytes 1382408 | tf_op jit(solution)/shard_map/ppermute | solution.py:546
  11.5 1.6 %collective-permute-start = (bf16[104,1152]{1,0:T(8,128)(2,1)}, bf16[104,1152]{1,0:T(8,128)(2,1)S(1)}, u32[]{:S(2)}, u32[]{:S(2)}) collective-permute-start(bf16[104,1152]{1,0:T(8,128)(2,1)} %get-tuple-element.76.rest_0_), channel_id=1, source_target_pairs={{0,8},{4,12},{8,0},{12,4},{16,24},{20,28},{24,16},{28,20},{1,9},{5... | collective-permute-start | bytes 718856 | tf_op jit(solution)/shard_map/ppermute | solution.py:554
  13.1 6.2 %collective-permute-done.1.rest_2_ = bf16[104,1152]{1,0:T(8,128)(2,1)S(1)} collective-permute-done((bf16[104,1152]{1,0:T(8,128)(2,1)}, bf16[104,1152]{1,0:T(8,128)(2,1)S(1)}, u32[]{:S(2)}, u32[]{:S(2)}) %collective-permute-start.1) | collective-permute-done | bytes 239648 | tf_op jit(solution)/shard_map/ppermute | solution.py:554
  20.1 2.4 %shard_map.120 = (bf16[24,8,1152]{2,1,0:T(8,128)(2,1)}, bf16[24,8,1152]{2,1,0:T(8,128)(2,1)}, bf16[24,8,1152]{2,1,0:T(8,128)(2,1)}) custom-call(bf16[196,8,768]{2,1,0:T(8,128)(2,1)} %bitcast.25, bf16[196,8,384]{2,1,0:T(8,128)(2,1)} %bitcast.30), custom_call_target="tpu_custom_call" | custom-call | tf_op jit(solution)/shard_map/pallas_call | solution.py:91
  23.1 8.2 %collective-permute-done.4.rest_8_ = bf16[25,8,1152]{2,1,0:T(8,128)(2,1)S(1)} collective-permute-done((bf16[25,8,1152]{2,1,0:T(8,128)(2,1)}, bf16[25,8,1152]{2,1,0:T(8,128)(2,1)S(1)}, u32[]{:S(2)}, u32[]{:S(2)}) %collective-permute-start.4) | collective-permute-done | bytes 460832 | tf_op jit(solution)/shard_map/ppermute | solution.py:546
  33.8 1.4 %collective-permute-start.9 = (bf16[24,8,1152]{2,1,0:T(8,128)(2,1)}, bf16[24,8,1152]{2,1,0:T(8,128)(2,1)S(1)}, u32[]{:S(2)}, u32[]{:S(2)}) collective-permute-start(bf16[24,8,1152]{2,1,0:T(8,128)(2,1)} %get-tuple-element.88), channel_id=1, source_target_pairs={{0,3},{1,2},{2,1},{3,0},{4,7},{5,6},{6,5},{7,4},{8,11},{9,10},{10,... | collective-permute-start | bytes 1327112 | tf_op jit(solution)/shard_map/ppermute | solution.py:546
  36.9 16.2 %shard_map.121 = (bf16[22,8,1152]{2,1,0:T(8,128)(2,1)}, bf16[22,8,1152]{2,1,0:T(8,128)(2,1)}, bf16[22,8,1152]{2,1,0:T(8,128)(2,1)}, bf16[3,8,1152]{2,1,0:T(8,128...) custom-call(s32[1]{0:T(128)S(6)} %copy.25.count_ref, ...), custom_call_target="tpu_custom_call" | custom-call | tf_op jit(solution)/shard_map/pallas_call | solution.py:498
  53.4 1.5 %collective-permute-done.9.rest_9_ = bf16[24,8,1152]{2,1,0:T(8,128)(2,1)S(1)} collective-permute-done((bf16[24,8,1152]{2,1,0:T(8,128)(2,1)}, bf16[24,8,1152]{2,1,0:T(8,128)(2,1)S(1)}, u32[]{:S(2)}, u32[]{:S(2)}) %collective-permute-start.9) | collective-permute-done | bytes 442400 | tf_op jit(solution)/shard_map/ppermute | solution.py:546
  55.7 1.5 %collective-permute-start.11 = (bf16[22,8,1152]{2,1,0:T(8,128)(2,1)}, bf16[22,8,1152]{2,1,0:T(8,128)(2,1)S(1)}, u32[]{:S(2)}, u32[]{:S(2)}) collective-permute-start(bf16[22,8,1152]{2,1,0:T(8,128)(2,1)} %get-tuple-element.104), channel_id=1, source_target_pairs={{0,2},{1,3},{2,0},{3,1},{4,6},{5,7},{6,4},{7,5},{8,10},{9,11},{10,... | collective-permute-start | bytes 1216520 | tf_op jit(solution)/shard_map/ppermute | solution.py:546
  58.4 15.6 %shard_map.122 = (bf16[27,8,1152]{2,1,0:T(8,128)(2,1)}, bf16[27,8,1152]{2,1,0:T(8,128)(2,1)}, bf16[27,8,1152]{2,1,0:T(8,128)(2,1)}, bf16[196,8,384]{2,1,0:T(8,12...) custom-call(s32[1]{0:T(128)S(6)} %copy.25.count_ref, ...), custom_call_target="tpu_custom_call", output_to_operand_aliasing={{3}: (18, {}), {4}: (19, {})} | custom-call | tf_op jit(solution)/shard_map/pallas_call | solution.py:498
  75.6 1.4 %collective-permute-start.17 = (bf16[27,8,1152]{2,1,0:T(8,128)(2,1)}, bf16[27,8,1152]{2,1,0:T(8,128)(2,1)S(1)}, u32[]{:S(2)}, u32[]{:S(2)}) collective-permute-start(bf16[27,8,1152]{2,1,0:T(8,128)(2,1)} %get-tuple-element.118), channel_id=1, source_target_pairs={{0,1},{1,0},{2,3},{3,2},{4,5},{5,4},{6,7},{7,6},{8,9},{9,8},{10,11... | collective-permute-start | bytes 1493000 | tf_op jit(solution)/shard_map/ppermute | solution.py:546
  77.6 1.5 %collective-permute-start.19 = (bf16[27,8,1152]{2,1,0:T(8,128)(2,1)}, bf16[27,8,1152]{2,1,0:T(8,128)(2,1)S(1)}, u32[]{:S(2)}, u32[]{:S(2)}) collective-permute-start(bf16[27,8,1152]{2,1,0:T(8,128)(2,1)} %get-tuple-element.120), channel_id=1, source_target_pairs={{0,3},{1,2},{2,1},{3,0},{4,7},{5,6},{6,5},{7,4},{8,11},{9,10},{10,... | collective-permute-start | bytes 1493000 | tf_op jit(solution)/shard_map/ppermute | solution.py:546
  80.2 1.6 %collective-permute-start.15 = (bf16[2,48,1152]{2,1,0:T(8,128)(2,1)S(1)}, bf16[2,48,1152]{2,1,0:T(8,128)(2,1)S(1)}, u32[]{:S(2)}, u32[]{:S(2)}) collective-permute-start(bf16[2,48,1152]{2,1,0:T(8,128)(2,1)S(1)} %slice.74), channel_id=1, source_target_pairs={{0,8},{4,12},{8,0},{12,4},{16,24},{20,28},{24,16},{28,20},{1,9},{5... | collective-permute-start | bytes 663560 | tf_op jit(solution)/shard_map/ppermute | solution.py:554
  82.6 2.1 %shard_map.123 = (bf16[196,8,384]{2,1,0:T(8,128)(2,1)}, bf16[196,8,768]{2,1,0:T(8,128)(2,1)}) custom-call(bf16[196,8,384]{2,1,0:T(8,128)(2,1)} %get-tuple-element.99.refs_0_, bf16[196,8,768]{2,1,0:T(8,128)(2,1)} %get-tuple-element.100.refs_1_, bf16[22,8,1152]{2,1,0:T(8,128)(2,1)} %copy-done.15, ...), custom_call_target="tpu_custom_call", output_to_operand_aliasing={{0}: (0, {}), {1}: (1, {})} | custom-call | tf_op jit(solution)/shard_map/pallas_call | solution.py:124
  84.7 4.0 %collective-permute-done.15 = bf16[2,48,1152]{2,1,0:T(8,128)(2,1)S(1)} collective-permute-done((bf16[2,48,1152]{2,1,0:T(8,128)(2,1)S(1)}, bf16[2,48,1152]{2,1,0:T(8,128)(2,1)S(1)}, u32[]{:S(2)}, u32[]{:S(2)}) %collective-permute-start.15) | collective-permute-done | bytes 221216 | tf_op jit(solution)/shard_map/ppermute | solution.py:554
  89.2 5.5 %collective-permute-done.22 = bf16[2,56,1152]{2,1,0:T(8,128)(2,1)S(1)} collective-permute-done((bf16[2,56,1152]{2,1,0:T(8,128)(2,1)S(1)}, bf16[2,56,1152]{2,1,0:T(8,128)(2,1)S(1)}, u32[]{:S(2)}, u32[]{:S(2)}) %collective-permute-start.22) | collective-permute-done | bytes 258080 | tf_op jit(solution)/shard_map/ppermute | solution.py:554
  94.8 2.3 %collective-permute-done.16 = bf16[1,48,1152]{2,1,0:T(8,128)(2,1)S(1)} collective-permute-done((bf16[1,48,1152]{2,1,0:T(8,128)(2,1)S(1)}, bf16[1,48,1152]{2,1,0:T(8,128)(2,1)S(1)}, u32[]{:S(2)}, u32[]{:S(2)}) %collective-permute-start.16) | collective-permute-done | bytes 110624 | tf_op jit(solution)/shard_map/ppermute | solution.py:554
  97.2 3.8 %collective-permute-done.18.refs_3_ = bf16[27,8,1152]{2,1,0:T(8,128)(2,1)S(1)} collective-permute-done((bf16[27,8,1152]{2,1,0:T(8,128)(2,1)}, bf16[27,8,1152]{2,1,0:T(8,128)(2,1)S(1)}, u32[]{:S(2)}, u32[]{:S(2)}) %collective-permute-start.18) | collective-permute-done | bytes 497696 | tf_op jit(solution)/shard_map/ppermute | solution.py:546
  102.1 1.5 %collective-permute-start.24 = (bf16[56,1152]{1,0:T(8,128)(2,1)S(1)}, bf16[56,1152]{1,0:T(8,128)(2,1)S(1)}, u32[]{:S(2)}, u32[]{:S(2)}) collective-permute-start(bf16[56,1152]{1,0:T(8,128)(2,1)S(1)} %fusion.2), channel_id=1, source_target_pairs={{0,1},{1,0},{2,3},{3,2},{4,5},{5,4},{6,7},{7,6},{8,9},{9,8},{10,11... | collective-permute-start | bytes 387080 | tf_op jit(solution)/shard_map/ppermute | solution.py:546
  104.1 1.5 %collective-permute-start.26 = (bf16[56,1152]{1,0:T(8,128)(2,1)S(1)}, bf16[56,1152]{1,0:T(8,128)(2,1)S(1)}, u32[]{:S(2)}, u32[]{:S(2)}) collective-permute-start(bf16[56,1152]{1,0:T(8,128)(2,1)S(1)} %fusion.2), channel_id=1, source_target_pairs={{0,3},{1,2},{2,1},{3,0},{4,7},{5,6},{6,5},{7,4},{8,11},{9,10},{10,... | collective-permute-start | bytes 387080 | tf_op jit(solution)/shard_map/ppermute | solution.py:546
  107.6 2.2 %shard_map.124 = (bf16[196,8,384]{2,1,0:T(8,128)(2,1)}, bf16[196,8,768]{2,1,0:T(8,128)(2,1)}) custom-call(bf16[196,8,384]{2,1,0:T(8,128)(2,1)} %get-tuple-element.114.refs_0_, bf16[196,8,768]{2,1,0:T(8,128)(2,1)} %get-tuple-element.115.refs_1_, bf16[27,8,1152]{2,1,0:T(8,128)(2,1)} %copy-done.6, ...), custom_call_target="tpu_custom_call", output_to_operand_aliasing={{0}: (0, {}), {1}: (1, {})} | custom-call | tf_op jit(solution)/shard_map/pallas_call | solution.py:124
  (90 shorter events, 18.9 us)
Async XLA Ops:
  3.9 15.4 %collective-permute-start.1 = (bf16[104,1152]{1,0:T(8,128)(2,1)}, bf16[104,1152]{1,0:T(8,128)(2,1)S(1)}, u32[]{:S(2)}, u32[]{:S(2)}) collective-permute-start(bf16[104,1152]{1,0:T(8,128)(2,1)} %get-tuple-element.76.rest_0_), channel_id=1, source_target_pairs={{0,16},{4,20},{8,24},{12,28},{16,0},{20,4},{24,8},{28,12},{1,17},{... | collective-permute-start | bytes 718856 | tf_op jit(solution)/shard_map/ppermute | solution.py:554
  8.0 15.1 %collective-permute-start.3 = (bf16[25,8,1152]{2,1,0:T(8,128)(2,1)}, bf16[25,8,1152]{2,1,0:T(8,128)(2,1)S(1)}, u32[]{:S(2)}, u32[]{:S(2)}) collective-permute-start(bf16[25,8,1152]{2,1,0:T(8,128)(2,1)} %get-tuple-element.70), channel_id=1, source_target_pairs={{0,1},{1,0},{2,3},{3,2},{4,5},{5,4},{6,7},{7,6},{8,9},{9,8},{10,11... | collective-permute-start | bytes 1382408 | tf_op jit(solution)/shard_map/ppermute | solution.py:546
  9.5 21.8 %collective-permute-start.4 = (bf16[25,8,1152]{2,1,0:T(8,128)(2,1)}, bf16[25,8,1152]{2,1,0:T(8,128)(2,1)S(1)}, u32[]{:S(2)}, u32[]{:S(2)}) collective-permute-start(bf16[25,8,1152]{2,1,0:T(8,128)(2,1)} %get-tuple-element.71), channel_id=1, source_target_pairs={{0,2},{1,3},{2,0},{3,1},{4,6},{5,7},{6,4},{7,5},{8,10},{9,11},{10,... | collective-permute-start | bytes 1382408 | tf_op jit(solution)/shard_map/ppermute | solution.py:546
  11.1 20.3 %collective-permute-start.5 = (bf16[25,8,1152]{2,1,0:T(8,128)(2,1)}, bf16[25,8,1152]{2,1,0:T(8,128)(2,1)S(1)}, u32[]{:S(2)}, u32[]{:S(2)}) collective-permute-start(bf16[25,8,1152]{2,1,0:T(8,128)(2,1)} %get-tuple-element.72), channel_id=1, source_target_pairs={{0,3},{1,2},{2,1},{3,0},{4,7},{5,6},{6,5},{7,4},{8,11},{9,10},{10,... | collective-permute-start | bytes 1382408 | tf_op jit(solution)/shard_map/ppermute | solution.py:546
  11.5 11.6 %collective-permute-start = (bf16[104,1152]{1,0:T(8,128)(2,1)}, bf16[104,1152]{1,0:T(8,128)(2,1)S(1)}, u32[]{:S(2)}, u32[]{:S(2)}) collective-permute-start(bf16[104,1152]{1,0:T(8,128)(2,1)} %get-tuple-element.76.rest_0_), channel_id=1, source_target_pairs={{0,8},{4,12},{8,0},{12,4},{16,24},{20,28},{24,16},{28,20},{1,9},{5... | collective-permute-start | bytes 718856 | tf_op jit(solution)/shard_map/ppermute | solution.py:554
  19.3 12.1 %collective-permute-start.2 = (bf16[104,1152]{1,0:T(8,128)(2,1)S(1)}, bf16[104,1152]{1,0:T(8,128)(2,1)S(1)}, u32[]{:S(2)}, u32[]{:S(2)}) collective-permute-start(bf16[104,1152]{1,0:T(8,128)(2,1)S(1)} %collective-permute-done.1.rest_2_), channel_id=1, source_target_pairs={{0,8},{4,12},{8,0},{12,4},{16,24},{20,28},{24,16},{28,20},{1,9},{5... | collective-permute-start | bytes 718856 | tf_op jit(solution)/shard_map/ppermute | solution.py:554
  31.6 21.4 %collective-permute-start.7 = (bf16[24,8,1152]{2,1,0:T(8,128)(2,1)}, bf16[24,8,1152]{2,1,0:T(8,128)(2,1)S(1)}, u32[]{:S(2)}, u32[]{:S(2)}) collective-permute-start(bf16[24,8,1152]{2,1,0:T(8,128)(2,1)} %get-tuple-element.86), channel_id=1, source_target_pairs={{0,1},{1,0},{2,3},{3,2},{4,5},{5,4},{6,7},{7,6},{8,9},{9,8},{10,11... | collective-permute-start | bytes 1327112 | tf_op jit(solution)/shard_map/ppermute | solution.py:546
  32.9 20.4 %collective-permute-start.8 = (bf16[24,8,1152]{2,1,0:T(8,128)(2,1)}, bf16[24,8,1152]{2,1,0:T(8,128)(2,1)S(1)}, u32[]{:S(2)}, u32[]{:S(2)}) collective-permute-start(bf16[24,8,1152]{2,1,0:T(8,128)(2,1)} %get-tuple-element.87), channel_id=1, source_target_pairs={{0,2},{1,3},{2,0},{3,1},{4,6},{5,7},{6,4},{7,5},{8,10},{9,11},{10,... | collective-permute-start | bytes 1327112 | tf_op jit(solution)/shard_map/ppermute | solution.py:546
  33.8 21.1 %collective-permute-start.9 = (bf16[24,8,1152]{2,1,0:T(8,128)(2,1)}, bf16[24,8,1152]{2,1,0:T(8,128)(2,1)S(1)}, u32[]{:S(2)}, u32[]{:S(2)}) collective-permute-start(bf16[24,8,1152]{2,1,0:T(8,128)(2,1)} %get-tuple-element.88), channel_id=1, source_target_pairs={{0,3},{1,2},{2,1},{3,0},{4,7},{5,6},{6,5},{7,4},{8,11},{9,10},{10,... | collective-permute-start | bytes 1327112 | tf_op jit(solution)/shard_map/ppermute | solution.py:546
  54.9 19.1 %collective-permute-start.10 = (bf16[22,8,1152]{2,1,0:T(8,128)(2,1)}, bf16[22,8,1152]{2,1,0:T(8,128)(2,1)S(1)}, u32[]{:S(2)}, u32[]{:S(2)}) collective-permute-start(bf16[22,8,1152]{2,1,0:T(8,128)(2,1)} %get-tuple-element.103), channel_id=1, source_target_pairs={{0,1},{1,0},{2,3},{3,2},{4,5},{5,4},{6,7},{7,6},{8,9},{9,8},{10,11... | collective-permute-start | bytes 1216520 | tf_op jit(solution)/shard_map/ppermute | solution.py:546
  55.7 19.3 %collective-permute-start.11 = (bf16[22,8,1152]{2,1,0:T(8,128)(2,1)}, bf16[22,8,1152]{2,1,0:T(8,128)(2,1)S(1)}, u32[]{:S(2)}, u32[]{:S(2)}) collective-permute-start(bf16[22,8,1152]{2,1,0:T(8,128)(2,1)} %get-tuple-element.104), channel_id=1, source_target_pairs={{0,2},{1,3},{2,0},{3,1},{4,6},{5,7},{6,4},{7,5},{8,10},{9,11},{10,... | collective-permute-start | bytes 1216520 | tf_op jit(solution)/shard_map/ppermute | solution.py:546
  57.3 17.8 %collective-permute-start.12 = (bf16[22,8,1152]{2,1,0:T(8,128)(2,1)}, bf16[22,8,1152]{2,1,0:T(8,128)(2,1)S(1)}, u32[]{:S(2)}, u32[]{:S(2)}) collective-permute-start(bf16[22,8,1152]{2,1,0:T(8,128)(2,1)} %get-tuple-element.105), channel_id=1, source_target_pairs={{0,3},{1,2},{2,1},{3,0},{4,7},{5,6},{6,5},{7,4},{8,11},{9,10},{10,... | collective-permute-start | bytes 1216520 | tf_op jit(solution)/shard_map/ppermute | solution.py:546
  75.6 21.5 %collective-permute-start.17 = (bf16[27,8,1152]{2,1,0:T(8,128)(2,1)}, bf16[27,8,1152]{2,1,0:T(8,128)(2,1)S(1)}, u32[]{:S(2)}, u32[]{:S(2)}) collective-permute-start(bf16[27,8,1152]{2,1,0:T(8,128)(2,1)} %get-tuple-element.118), channel_id=1, source_target_pairs={{0,1},{1,0},{2,3},{3,2},{4,5},{5,4},{6,7},{7,6},{8,9},{9,8},{10,11... | collective-permute-start | bytes 1493000 | tf_op jit(solution)/shard_map/ppermute | solution.py:546
  77.0 23.9 %collective-permute-start.18 = (bf16[27,8,1152]{2,1,0:T(8,128)(2,1)}, bf16[27,8,1152]{2,1,0:T(8,128)(2,1)S(1)}, u32[]{:S(2)}, u32[]{:S(2)}) collective-permute-start(bf16[27,8,1152]{2,1,0:T(8,128)(2,1)} %get-tuple-element.119), channel_id=1, source_target_pairs={{0,2},{1,3},{2,0},{3,1},{4,6},{5,7},{6,4},{7,5},{8,10},{9,11},{10,... | collective-permute-start | bytes 1493000 | tf_op jit(solution)/shard_map/ppermute | solution.py:546
  77.6 23.4 %collective-permute-start.19 = (bf16[27,8,1152]{2,1,0:T(8,128)(2,1)}, bf16[27,8,1152]{2,1,0:T(8,128)(2,1)S(1)}, u32[]{:S(2)}, u32[]{:S(2)}) collective-permute-start(bf16[27,8,1152]{2,1,0:T(8,128)(2,1)} %get-tuple-element.120), channel_id=1, source_target_pairs={{0,3},{1,2},{2,1},{3,0},{4,7},{5,6},{6,5},{7,4},{8,11},{9,10},{10,... | collective-permute-start | bytes 1493000 | tf_op jit(solution)/shard_map/ppermute | solution.py:546
  80.2 8.4 %collective-permute-start.15 = (bf16[2,48,1152]{2,1,0:T(8,128)(2,1)S(1)}, bf16[2,48,1152]{2,1,0:T(8,128)(2,1)S(1)}, u32[]{:S(2)}, u32[]{:S(2)}) collective-permute-start(bf16[2,48,1152]{2,1,0:T(8,128)(2,1)S(1)} %slice.74), channel_id=1, source_target_pairs={{0,8},{4,12},{8,0},{12,4},{16,24},{20,28},{24,16},{28,20},{1,9},{5... | collective-permute-start | bytes 663560 | tf_op jit(solution)/shard_map/ppermute | solution.py:554
  82.1 12.6 %collective-permute-start.22 = (bf16[2,56,1152]{2,1,0:T(8,128)(2,1)S(1)}, bf16[2,56,1152]{2,1,0:T(8,128)(2,1)S(1)}, u32[]{:S(2)}, u32[]{:S(2)}) collective-permute-start(bf16[2,56,1152]{2,1,0:T(8,128)(2,1)S(1)} %slice.73), channel_id=1, source_target_pairs={{0,8},{4,12},{8,0},{12,4},{16,24},{20,28},{24,16},{28,20},{1,9},{5... | collective-permute-start | bytes 774152 | tf_op jit(solution)/shard_map/ppermute | solution.py:554
  88.7 8.4 %collective-permute-start.16 = (bf16[1,48,1152]{2,1,0:T(8,128)(2,1)S(1)}, bf16[1,48,1152]{2,1,0:T(8,128)(2,1)S(1)}, u32[]{:S(2)}, u32[]{:S(2)}) collective-permute-start(bf16[1,48,1152]{2,1,0:T(8,128)(2,1)S(1)} %slice.76), channel_id=1, source_target_pairs={{0,16},{4,20},{8,24},{12,28},{16,0},{20,4},{24,8},{28,12},{1,17},{... | collective-permute-start | bytes 331784 | tf_op jit(solution)/shard_map/ppermute | solution.py:554
  94.7 7.3 %collective-permute-start.23 = (bf16[1,56,1152]{2,1,0:T(8,128)(2,1)S(1)}, bf16[1,56,1152]{2,1,0:T(8,128)(2,1)S(1)}, u32[]{:S(2)}, u32[]{:S(2)}) collective-permute-start(bf16[1,56,1152]{2,1,0:T(8,128)(2,1)S(1)} %slice.75), channel_id=1, source_target_pairs={{0,16},{4,20},{8,24},{12,28},{16,0},{20,4},{24,8},{28,12},{1,17},{... | collective-permute-start | bytes 387080 | tf_op jit(solution)/shard_map/ppermute | solution.py:554
  101.0 5.8 %collective-permute-start.20 = (bf16[48,1152]{1,0:T(8,128)(2,1)S(1)}, bf16[48,1152]{1,0:T(8,128)(2,1)S(1)}, u32[]{:S(2)}, u32[]{:S(2)}) collective-permute-start(bf16[48,1152]{1,0:T(8,128)(2,1)S(1)} %fusion.1), channel_id=1, source_target_pairs={{0,1},{1,0},{2,3},{3,2},{4,5},{5,4},{6,7},{7,6},{8,9},{9,8},{10,11... | collective-permute-start | bytes 331784 | tf_op jit(solution)/shard_map/ppermute | solution.py:546
  102.1 7.8 %collective-permute-start.24 = (bf16[56,1152]{1,0:T(8,128)(2,1)S(1)}, bf16[56,1152]{1,0:T(8,128)(2,1)S(1)}, u32[]{:S(2)}, u32[]{:S(2)}) collective-permute-start(bf16[56,1152]{1,0:T(8,128)(2,1)S(1)} %fusion.2), channel_id=1, source_target_pairs={{0,1},{1,0},{2,3},{3,2},{4,5},{5,4},{6,7},{7,6},{8,9},{9,8},{10,11... | collective-permute-start | bytes 387080 | tf_op jit(solution)/shard_map/ppermute | solution.py:546
  103.6 7.5 %collective-permute-start.25 = (bf16[56,1152]{1,0:T(8,128)(2,1)S(1)}, bf16[56,1152]{1,0:T(8,128)(2,1)S(1)}, u32[]{:S(2)}, u32[]{:S(2)}) collective-permute-start(bf16[56,1152]{1,0:T(8,128)(2,1)S(1)} %fusion.2), channel_id=1, source_target_pairs={{0,2},{1,3},{2,0},{3,1},{4,6},{5,7},{6,4},{7,5},{8,10},{9,11},{10,... | collective-permute-start | bytes 387080 | tf_op jit(solution)/shard_map/ppermute | solution.py:546
  104.1 7.0 %collective-permute-start.26 = (bf16[56,1152]{1,0:T(8,128)(2,1)S(1)}, bf16[56,1152]{1,0:T(8,128)(2,1)S(1)}, u32[]{:S(2)}, u32[]{:S(2)}) collective-permute-start(bf16[56,1152]{1,0:T(8,128)(2,1)S(1)} %fusion.2), channel_id=1, source_target_pairs={{0,3},{1,2},{2,1},{3,0},{4,7},{5,6},{6,5},{7,4},{8,11},{9,10},{10,... | collective-permute-start | bytes 387080 | tf_op jit(solution)/shard_map/ppermute | solution.py:546
  106.9 5.4 %collective-permute-start.21 = (bf16[48,1152]{1,0:T(8,128)(2,1)S(1)}, bf16[48,1152]{1,0:T(8,128)(2,1)S(1)}, u32[]{:S(2)}, u32[]{:S(2)}) collective-permute-start(bf16[48,1152]{1,0:T(8,128)(2,1)S(1)} %add_convert_fusion), channel_id=1, source_target_pairs={{0,2},{1,3},{2,0},{3,1},{4,6},{5,7},{6,4},{7,5},{8,10},{9,11},{10,... | collective-permute-start | bytes 331784 | tf_op jit(solution)/shard_map/ppermute | solution.py:546
  (21 other events, 159.6 us)

commit v7 on v6

--- a/solution.py
+++ b/solution.py
@@ -11,7 +11,7 @@
 BLOCK = 16
 CORES = 2
 EXTRA = 8
-CARRIED = 16
+CARRIED = 12
 
 masked_value = -1e30
 epsilon = 1e-05
@@ -610,7 +610,7 @@
             half = half[:left] + got.astype(f32)
             bit *= 2
         halves.append(half[0])
-    halves[0], results[-1] = lax.optimization_barrier((halves[0], results[-1]))
+    halves[0], results[-1][:-1] = lax.optimization_barrier((halves[0], results[-1][:-1]))
     summed = []
     for side, half in enumerate(halves):
         r = 1

time: 113 us -> 112 us (level)
  waiting for transfers between devices: 36.8 us -> 35.5 us
    ppermute x17, waiting for transfers between devices: 17.9 us -> 16.5 us  [swap(): return lax.ppermute(array, 'tm', partner(tm_count, r))]
  transfers between devices with their start and end apart: 27 -> 27, of which waited for: 14 -> 14; matrix products, arithmetic and copies ran while one was open for 2% -> 2% of each run, Pallas kernels for 34% -> 35%
where the time goes in v7:
time: 112 us; the launch traced here: 111 us
  Pallas kernels  41.8 us (37%)
  waiting for transfers between devices  35.5 us (32%)
  starting transfers between devices  28.2 us (25%)
  other arithmetic  2.44 us (2%)
  local copies, waits for them, and re-layouts  1.72 us (2%)
  between operations  1.65 us (1%)
    pallas_call x2, Pallas kernels, chunk(): pl.pallas_call(functools.partial(chunk_kernel, tm_count, dp_count, frames...  31.7 us
    ppermute x10, waiting for transfers between devices, across(): return lax.ppermute(array, 'dp', partner(dp_count, k))  19.1 us
    ppermute x17, starting transfers between devices, swap(): return lax.ppermute(array, 'tm', partner(tm_count, r))  18.5 us
    ppermute x17, waiting for transfers between devices, swap(): return lax.ppermute(array, 'tm', partner(tm_count, r))  16.5 us
    ppermute x10, starting transfers between devices, across(): return lax.ppermute(array, 'dp', partner(dp_count, k))  9.73 us
    pallas_call x2, Pallas kernels, pack(): pl.pallas_call(functools.partial(pack_kernel, tm_count, patches_dev, offs...  5.72 us
    pallas_call x2, Pallas kernels, unpack(): pl.pallas_call(functools.partial(unpack_kernel, tm_count, patches_dev, of...  4.36 us
  transfers between devices with their start and end apart: 27, of which 14 were waited for; matrix products, arithmetic and copies ran while one was open for 2% of the time, Pallas kernels for 35%

profile of v7, /device:TPU:0, one launch (start us, length us, event | category | flops | bytes accessed | tf_op | source)
XLA Modules:
  0.0 111.4 jit_solution(14456063007857589973)
XLA Ops:
  0.6 3.3 %shard_map.119 = (bf16[104,1152]{1,0:T(8,128)(2,1)}, bf16[25,8,1152]{2,1,0:T(8,128)(2,1)}, bf16[25,8,1152]{2,1,0:T(8,128)(2,1)}, bf16[25,8,1152]{2,1,0:T(8,128)(2,1)}) custom-call(bf16[196,8,768]{2,1,0:T(8,128)(2,1)} %bitcast.24, bf16[196,8,384]{2,1,0:T(8,128)(2,1)} %bitcast.29, bf16[96,1152]{1,0:T(8,128)(2,1)} %rest_0_.1, bf16[96]{0:T(256)(128)(2,1)} %rest_1_.1, ...), custom_call_target="tpu_custom_call" | custom-call | tf_op jit(solution)/shard_map/pallas_call | solution.py:91
  3.9 4.1 %collective-permute-start.1 = (bf16[104,1152]{1,0:T(8,128)(2,1)}, bf16[104,1152]{1,0:T(8,128)(2,1)S(1)}, u32[]{:S(2)}, u32[]{:S(2)}) collective-permute-start(bf16[104,1152]{1,0:T(8,128)(2,1)} %get-tuple-element.75.rest_0_), channel_id=1, source_target_pairs={{0,16},{4,20},{8,24},{12,28},{16,0},{20,4},{24,8},{28,12},{1,17},{... | collective-permute-start | bytes 718856 | tf_op jit(solution)/shard_map/ppermute | solution.py:554
  8.0 1.5 %collective-permute-start.3 = (bf16[25,8,1152]{2,1,0:T(8,128)(2,1)}, bf16[25,8,1152]{2,1,0:T(8,128)(2,1)S(1)}, u32[]{:S(2)}, u32[]{:S(2)}) collective-permute-start(bf16[25,8,1152]{2,1,0:T(8,128)(2,1)} %get-tuple-element.69), channel_id=1, source_target_pairs={{0,1},{1,0},{2,3},{3,2},{4,5},{5,4},{6,7},{7,6},{8,9},{9,8},{10,11... | collective-permute-start | bytes 1382408 | tf_op jit(solution)/shard_map/ppermute | solution.py:546
  9.5 1.5 %collective-permute-start.4 = (bf16[25,8,1152]{2,1,0:T(8,128)(2,1)}, bf16[25,8,1152]{2,1,0:T(8,128)(2,1)S(1)}, u32[]{:S(2)}, u32[]{:S(2)}) collective-permute-start(bf16[25,8,1152]{2,1,0:T(8,128)(2,1)} %get-tuple-element.70), channel_id=1, source_target_pairs={{0,2},{1,3},{2,0},{3,1},{4,6},{5,7},{6,4},{7,5},{8,10},{9,11},{10,... | collective-permute-start | bytes 1382408 | tf_op jit(solution)/shard_map/ppermute | solution.py:546
  11.5 1.6 %collective-permute-start = (bf16[104,1152]{1,0:T(8,128)(2,1)}, bf16[104,1152]{1,0:T(8,128)(2,1)S(1)}, u32[]{:S(2)}, u32[]{:S(2)}) collective-permute-start(bf16[104,1152]{1,0:T(8,128)(2,1)} %get-tuple-element.75.rest_0_), channel_id=1, source_target_pairs={{0,8},{4,12},{8,0},{12,4},{16,24},{20,28},{24,16},{28,20},{1,9},{5... | collective-permute-start | bytes 718856 | tf_op jit(solution)/shard_map/ppermute | solution.py:554
  13.1 6.2 %collective-permute-done.1.rest_2_ = bf16[104,1152]{1,0:T(8,128)(2,1)S(1)} collective-permute-done((bf16[104,1152]{1,0:T(8,128)(2,1)}, bf16[104,1152]{1,0:T(8,128)(2,1)S(1)}, u32[]{:S(2)}, u32[]{:S(2)}) %collective-permute-start.1) | collective-permute-done | bytes 239648 | tf_op jit(solution)/shard_map/ppermute | solution.py:554
  20.1 2.4 %shard_map.120 = (bf16[24,8,1152]{2,1,0:T(8,128)(2,1)}, bf16[24,8,1152]{2,1,0:T(8,128)(2,1)}, bf16[24,8,1152]{2,1,0:T(8,128)(2,1)}) custom-call(bf16[196,8,768]{2,1,0:T(8,128)(2,1)} %bitcast.25, bf16[196,8,384]{2,1,0:T(8,128)(2,1)} %bitcast.30), custom_call_target="tpu_custom_call" | custom-call | tf_op jit(solution)/shard_map/pallas_call | solution.py:91
  23.1 8.2 %collective-permute-done.4.rest_8_ = bf16[25,8,1152]{2,1,0:T(8,128)(2,1)S(1)} collective-permute-done((bf16[25,8,1152]{2,1,0:T(8,128)(2,1)}, bf16[25,8,1152]{2,1,0:T(8,128)(2,1)S(1)}, u32[]{:S(2)}, u32[]{:S(2)}) %collective-permute-start.4) | collective-permute-done | bytes 460832 | tf_op jit(solution)/shard_map/ppermute | solution.py:546
  33.8 1.4 %collective-permute-start.9 = (bf16[24,8,1152]{2,1,0:T(8,128)(2,1)}, bf16[24,8,1152]{2,1,0:T(8,128)(2,1)S(1)}, u32[]{:S(2)}, u32[]{:S(2)}) collective-permute-start(bf16[24,8,1152]{2,1,0:T(8,128)(2,1)} %get-tuple-element.87), channel_id=1, source_target_pairs={{0,3},{1,2},{2,1},{3,0},{4,7},{5,6},{6,5},{7,4},{8,11},{9,10},{10,... | collective-permute-start | bytes 1327112 | tf_op jit(solution)/shard_map/ppermute | solution.py:546
  36.9 16.2 %shard_map.121 = (bf16[21,8,1152]{2,1,0:T(8,128)(2,1)}, bf16[21,8,1152]{2,1,0:T(8,128)(2,1)}, bf16[21,8,1152]{2,1,0:T(8,128)(2,1)}, bf16[4,8,1152]{2,1,0:T(8,128...) custom-call(s32[1]{0:T(128)S(6)} %copy.25.count_ref, ...), custom_call_target="tpu_custom_call" | custom-call | tf_op jit(solution)/shard_map/pallas_call | solution.py:498
  53.4 1.5 %collective-permute-done.9.rest_9_ = bf16[24,8,1152]{2,1,0:T(8,128)(2,1)S(1)} collective-permute-done((bf16[24,8,1152]{2,1,0:T(8,128)(2,1)}, bf16[24,8,1152]{2,1,0:T(8,128)(2,1)S(1)}, u32[]{:S(2)}, u32[]{:S(2)}) %collective-permute-start.9) | collective-permute-done | bytes 442400 | tf_op jit(solution)/shard_map/ppermute | solution.py:546
  55.7 1.5 %collective-permute-start.11 = (bf16[21,8,1152]{2,1,0:T(8,128)(2,1)}, bf16[21,8,1152]{2,1,0:T(8,128)(2,1)S(1)}, u32[]{:S(2)}, u32[]{:S(2)}) collective-permute-start(bf16[21,8,1152]{2,1,0:T(8,128)(2,1)} %get-tuple-element.103), channel_id=1, source_target_pairs={{0,2},{1,3},{2,0},{3,1},{4,6},{5,7},{6,4},{7,5},{8,10},{9,11},{10,... | collective-permute-start | bytes 1161224 | tf_op jit(solution)/shard_map/ppermute | solution.py:546
  58.4 15.6 %shard_map.122 = (bf16[28,8,1152]{2,1,0:T(8,128)(2,1)}, bf16[28,8,1152]{2,1,0:T(8,128)(2,1)}, bf16[28,8,1152]{2,1,0:T(8,128)(2,1)}, bf16[196,8,384]{2,1,0:T(8,12...) custom-call(s32[1]{0:T(128)S(6)} %copy.25.count_ref, ...), custom_call_target="tpu_custom_call", output_to_operand_aliasing={{3}: (18, {}), {4}: (19, {})} | custom-call | tf_op jit(solution)/shard_map/pallas_call | solution.py:498
  74.8 1.4 %collective-permute-start.17 = (bf16[28,8,1152]{2,1,0:T(8,128)(2,1)}, bf16[28,8,1152]{2,1,0:T(8,128)(2,1)S(1)}, u32[]{:S(2)}, u32[]{:S(2)}) collective-permute-start(bf16[28,8,1152]{2,1,0:T(8,128)(2,1)} %get-tuple-element.117), channel_id=1, source_target_pairs={{0,1},{1,0},{2,3},{3,2},{4,5},{5,4},{6,7},{7,6},{8,9},{9,8},{10,11... | collective-permute-start | bytes 1548296 | tf_op jit(solution)/shard_map/ppermute | solution.py:546
  77.0 1.3 %collective-permute-start.20 = (bf16[28,8,1152]{2,1,0:T(8,128)(2,1)}, bf16[28,8,1152]{2,1,0:T(8,128)(2,1)S(1)}, u32[]{:S(2)}, u32[]{:S(2)}) collective-permute-start(bf16[28,8,1152]{2,1,0:T(8,128)(2,1)} %get-tuple-element.122), channel_id=1, source_target_pairs={{0,3},{1,2},{2,1},{3,0},{4,7},{5,6},{6,5},{7,4},{8,11},{9,10},{10,... | collective-permute-start | bytes 1548296 | tf_op jit(solution)/shard_map/ppermute | solution.py:546
  79.5 1.6 %collective-permute-start.15 = (bf16[2,48,1152]{2,1,0:T(8,128)(2,1)S(1)}, bf16[2,48,1152]{2,1,0:T(8,128)(2,1)S(1)}, u32[]{:S(2)}, u32[]{:S(2)}) collective-permute-start(bf16[2,48,1152]{2,1,0:T(8,128)(2,1)S(1)} %slice.74), channel_id=1, source_target_pairs={{0,8},{4,12},{8,0},{12,4},{16,24},{20,28},{24,16},{28,20},{1,9},{5... | collective-permute-start | bytes 663560 | tf_op jit(solution)/shard_map/ppermute | solution.py:554
  81.8 2.1 %shard_map.123 = (bf16[196,8,384]{2,1,0:T(8,128)(2,1)}, bf16[196,8,768]{2,1,0:T(8,128)(2,1)}) custom-call(bf16[196,8,384]{2,1,0:T(8,128)(2,1)} %get-tuple-element.98.refs_0_, bf16[196,8,768]{2,1,0:T(8,128)(2,1)} %get-tuple-element.99.refs_1_, bf16[21,8,1152]{2,1,0:T(8,128)(2,1)} %copy-done.15, ...), custom_call_target="tpu_custom_call", output_to_operand_aliasing={{0}: (0, {}), {1}: (1, {})} | custom-call | tf_op jit(solution)/shard_map/pallas_call | solution.py:124
  83.9 4.0 %collective-permute-done.15 = bf16[2,48,1152]{2,1,0:T(8,128)(2,1)S(1)} collective-permute-done((bf16[2,48,1152]{2,1,0:T(8,128)(2,1)S(1)}, bf16[2,48,1152]{2,1,0:T(8,128)(2,1)S(1)}, u32[]{:S(2)}, u32[]{:S(2)}) %collective-permute-start.15) | collective-permute-done | bytes 221216 | tf_op jit(solution)/shard_map/ppermute | solution.py:554
  88.4 5.5 %collective-permute-done.22 = bf16[2,56,1152]{2,1,0:T(8,128)(2,1)S(1)} collective-permute-done((bf16[2,56,1152]{2,1,0:T(8,128)(2,1)S(1)}, bf16[2,56,1152]{2,1,0:T(8,128)(2,1)S(1)}, u32[]{:S(2)}, u32[]{:S(2)}) %collective-permute-start.22) | collective-permute-done | bytes 258080 | tf_op jit(solution)/shard_map/ppermute | solution.py:554
  94.0 2.3 %collective-permute-done.16 = bf16[1,48,1152]{2,1,0:T(8,128)(2,1)S(1)} collective-permute-done((bf16[1,48,1152]{2,1,0:T(8,128)(2,1)S(1)}, bf16[1,48,1152]{2,1,0:T(8,128)(2,1)S(1)}, u32[]{:S(2)}, u32[]{:S(2)}) %collective-permute-start.16) | collective-permute-done | bytes 110624 | tf_op jit(solution)/shard_map/ppermute | solution.py:554
  96.4 4.3 %collective-permute-done.18.refs_3_ = bf16[28,8,1152]{2,1,0:T(8,128)(2,1)S(1)} collective-permute-done((bf16[28,8,1152]{2,1,0:T(8,128)(2,1)}, bf16[28,8,1152]{2,1,0:T(8,128)(2,1)S(1)}, u32[]{:S(2)}, u32[]{:S(2)}) %collective-permute-start.18) | collective-permute-done | bytes 516128 | tf_op jit(solution)/shard_map/ppermute | solution.py:546
  101.3 1.5 %collective-permute-start.24 = (bf16[56,1152]{1,0:T(8,128)(2,1)S(1)}, bf16[56,1152]{1,0:T(8,128)(2,1)S(1)}, u32[]{:S(2)}, u32[]{:S(2)}) collective-permute-start(bf16[56,1152]{1,0:T(8,128)(2,1)S(1)} %fusion.2), channel_id=1, source_target_pairs={{0,1},{1,0},{2,3},{3,2},{4,5},{5,4},{6,7},{7,6},{8,9},{9,8},{10,11... | collective-permute-start | bytes 387080 | tf_op jit(solution)/shard_map/ppermute | solution.py:546
  103.5 1.3 %collective-permute-start.26 = (bf16[56,1152]{1,0:T(8,128)(2,1)S(1)}, bf16[56,1152]{1,0:T(8,128)(2,1)S(1)}, u32[]{:S(2)}, u32[]{:S(2)}) collective-permute-start(bf16[56,1152]{1,0:T(8,128)(2,1)S(1)} %fusion.2), channel_id=1, source_target_pairs={{0,3},{1,2},{2,1},{3,0},{4,7},{5,6},{6,5},{7,4},{8,11},{9,10},{10,... | collective-permute-start | bytes 387080 | tf_op jit(solution)/shard_map/ppermute | solution.py:546
  106.2 2.3 %shard_map.124 = (bf16[196,8,384]{2,1,0:T(8,128)(2,1)}, bf16[196,8,768]{2,1,0:T(8,128)(2,1)}) custom-call(bf16[196,8,384]{2,1,0:T(8,128)(2,1)} %get-tuple-element.113.refs_0_, bf16[196,8,768]{2,1,0:T(8,128)(2,1)} %get-tuple-element.114.refs_1_, bf16[28,8,1152]{2,1,0:T(8,128)(2,1)} %copy-done.5, ...), custom_call_target="tpu_custom_call", output_to_operand_aliasing={{0}: (0, {}), {1}: (1, {})} | custom-call | tf_op jit(solution)/shard_map/pallas_call | solution.py:124
  (90 shorter events, 17.0 us)
Async XLA Ops:
  3.9 15.4 %collective-permute-start.1 = (bf16[104,1152]{1,0:T(8,128)(2,1)}, bf16[104,1152]{1,0:T(8,128)(2,1)S(1)}, u32[]{:S(2)}, u32[]{:S(2)}) collective-permute-start(bf16[104,1152]{1,0:T(8,128)(2,1)} %get-tuple-element.75.rest_0_), channel_id=1, source_target_pairs={{0,16},{4,20},{8,24},{12,28},{16,0},{20,4},{24,8},{28,12},{1,17},{... | collective-permute-start | bytes 718856 | tf_op jit(solution)/shard_map/ppermute | solution.py:554
  8.0 15.1 %collective-permute-start.3 = (bf16[25,8,1152]{2,1,0:T(8,128)(2,1)}, bf16[25,8,1152]{2,1,0:T(8,128)(2,1)S(1)}, u32[]{:S(2)}, u32[]{:S(2)}) collective-permute-start(bf16[25,8,1152]{2,1,0:T(8,128)(2,1)} %get-tuple-element.69), channel_id=1, source_target_pairs={{0,1},{1,0},{2,3},{3,2},{4,5},{5,4},{6,7},{7,6},{8,9},{9,8},{10,11... | collective-permute-start | bytes 1382408 | tf_op jit(solution)/shard_map/ppermute | solution.py:546
  9.5 21.8 %collective-permute-start.4 = (bf16[25,8,1152]{2,1,0:T(8,128)(2,1)}, bf16[25,8,1152]{2,1,0:T(8,128)(2,1)S(1)}, u32[]{:S(2)}, u32[]{:S(2)}) collective-permute-start(bf16[25,8,1152]{2,1,0:T(8,128)(2,1)} %get-tuple-element.70), channel_id=1, source_target_pairs={{0,2},{1,3},{2,0},{3,1},{4,6},{5,7},{6,4},{7,5},{8,10},{9,11},{10,... | collective-permute-start | bytes 1382408 | tf_op jit(solution)/shard_map/ppermute | solution.py:546
  11.1 20.3 %collective-permute-start.5 = (bf16[25,8,1152]{2,1,0:T(8,128)(2,1)}, bf16[25,8,1152]{2,1,0:T(8,128)(2,1)S(1)}, u32[]{:S(2)}, u32[]{:S(2)}) collective-permute-start(bf16[25,8,1152]{2,1,0:T(8,128)(2,1)} %get-tuple-element.71), channel_id=1, source_target_pairs={{0,3},{1,2},{2,1},{3,0},{4,7},{5,6},{6,5},{7,4},{8,11},{9,10},{10,... | collective-permute-start | bytes 1382408 | tf_op jit(solution)/shard_map/ppermute | solution.py:546
  11.5 11.6 %collective-permute-start = (bf16[104,1152]{1,0:T(8,128)(2,1)}, bf16[104,1152]{1,0:T(8,128)(2,1)S(1)}, u32[]{:S(2)}, u32[]{:S(2)}) collective-permute-start(bf16[104,1152]{1,0:T(8,128)(2,1)} %get-tuple-element.75.rest_0_), channel_id=1, source_target_pairs={{0,8},{4,12},{8,0},{12,4},{16,24},{20,28},{24,16},{28,20},{1,9},{5... | collective-permute-start | bytes 718856 | tf_op jit(solution)/shard_map/ppermute | solution.py:554
  19.3 12.1 %collective-permute-start.2 = (bf16[104,1152]{1,0:T(8,128)(2,1)S(1)}, bf16[104,1152]{1,0:T(8,128)(2,1)S(1)}, u32[]{:S(2)}, u32[]{:S(2)}) collective-permute-start(bf16[104,1152]{1,0:T(8,128)(2,1)S(1)} %collective-permute-done.1.rest_2_), channel_id=1, source_target_pairs={{0,8},{4,12},{8,0},{12,4},{16,24},{20,28},{24,16},{28,20},{1,9},{5... | collective-permute-start | bytes 718856 | tf_op jit(solution)/shard_map/ppermute | solution.py:554
  31.6 21.4 %collective-permute-start.7 = (bf16[24,8,1152]{2,1,0:T(8,128)(2,1)}, bf16[24,8,1152]{2,1,0:T(8,128)(2,1)S(1)}, u32[]{:S(2)}, u32[]{:S(2)}) collective-permute-start(bf16[24,8,1152]{2,1,0:T(8,128)(2,1)} %get-tuple-element.85), channel_id=1, source_target_pairs={{0,1},{1,0},{2,3},{3,2},{4,5},{5,4},{6,7},{7,6},{8,9},{9,8},{10,11... | collective-permute-start | bytes 1327112 | tf_op jit(solution)/shard_map/ppermute | solution.py:546
  32.9 20.4 %collective-permute-start.8 = (bf16[24,8,1152]{2,1,0:T(8,128)(2,1)}, bf16[24,8,1152]{2,1,0:T(8,128)(2,1)S(1)}, u32[]{:S(2)}, u32[]{:S(2)}) collective-permute-start(bf16[24,8,1152]{2,1,0:T(8,128)(2,1)} %get-tuple-element.86), channel_id=1, source_target_pairs={{0,2},{1,3},{2,0},{3,1},{4,6},{5,7},{6,4},{7,5},{8,10},{9,11},{10,... | collective-permute-start | bytes 1327112 | tf_op jit(solution)/shard_map/ppermute | solution.py:546
  33.8 21.1 %collective-permute-start.9 = (bf16[24,8,1152]{2,1,0:T(8,128)(2,1)}, bf16[24,8,1152]{2,1,0:T(8,128)(2,1)S(1)}, u32[]{:S(2)}, u32[]{:S(2)}) collective-permute-start(bf16[24,8,1152]{2,1,0:T(8,128)(2,1)} %get-tuple-element.87), channel_id=1, source_target_pairs={{0,3},{1,2},{2,1},{3,0},{4,7},{5,6},{6,5},{7,4},{8,11},{9,10},{10,... | collective-permute-start | bytes 1327112 | tf_op jit(solution)/shard_map/ppermute | solution.py:546
  54.9 19.1 %collective-permute-start.10 = (bf16[21,8,1152]{2,1,0:T(8,128)(2,1)}, bf16[21,8,1152]{2,1,0:T(8,128)(2,1)S(1)}, u32[]{:S(2)}, u32[]{:S(2)}) collective-permute-start(bf16[21,8,1152]{2,1,0:T(8,128)(2,1)} %get-tuple-element.102), channel_id=1, source_target_pairs={{0,1},{1,0},{2,3},{3,2},{4,5},{5,4},{6,7},{7,6},{8,9},{9,8},{10,11... | collective-permute-start | bytes 1161224 | tf_op jit(solution)/shard_map/ppermute | solution.py:546
  55.7 18.5 %collective-permute-start.11 = (bf16[21,8,1152]{2,1,0:T(8,128)(2,1)}, bf16[21,8,1152]{2,1,0:T(8,128)(2,1)S(1)}, u32[]{:S(2)}, u32[]{:S(2)}) collective-permute-start(bf16[21,8,1152]{2,1,0:T(8,128)(2,1)} %get-tuple-element.103), channel_id=1, source_target_pairs={{0,2},{1,3},{2,0},{3,1},{4,6},{5,7},{6,4},{7,5},{8,10},{9,11},{10,... | collective-permute-start | bytes 1161224 | tf_op jit(solution)/shard_map/ppermute | solution.py:546
  57.3 17.0 %collective-permute-start.12 = (bf16[21,8,1152]{2,1,0:T(8,128)(2,1)}, bf16[21,8,1152]{2,1,0:T(8,128)(2,1)S(1)}, u32[]{:S(2)}, u32[]{:S(2)}) collective-permute-start(bf16[21,8,1152]{2,1,0:T(8,128)(2,1)} %get-tuple-element.104), channel_id=1, source_target_pairs={{0,3},{1,2},{2,1},{3,0},{4,7},{5,6},{6,5},{7,4},{8,11},{9,10},{10,... | collective-permute-start | bytes 1161224 | tf_op jit(solution)/shard_map/ppermute | solution.py:546
  74.8 21.5 %collective-permute-start.17 = (bf16[28,8,1152]{2,1,0:T(8,128)(2,1)}, bf16[28,8,1152]{2,1,0:T(8,128)(2,1)S(1)}, u32[]{:S(2)}, u32[]{:S(2)}) collective-permute-start(bf16[28,8,1152]{2,1,0:T(8,128)(2,1)} %get-tuple-element.117), channel_id=1, source_target_pairs={{0,1},{1,0},{2,3},{3,2},{4,5},{5,4},{6,7},{7,6},{8,9},{9,8},{10,11... | collective-permute-start | bytes 1548296 | tf_op jit(solution)/shard_map/ppermute | solution.py:546
  76.3 24.4 %collective-permute-start.18 = (bf16[28,8,1152]{2,1,0:T(8,128)(2,1)}, bf16[28,8,1152]{2,1,0:T(8,128)(2,1)S(1)}, u32[]{:S(2)}, u32[]{:S(2)}) collective-permute-start(bf16[28,8,1152]{2,1,0:T(8,128)(2,1)} %get-tuple-element.118), channel_id=1, source_target_pairs={{0,2},{1,3},{2,0},{3,1},{4,6},{5,7},{6,4},{7,5},{8,10},{9,11},{10,... | collective-permute-start | bytes 1548296 | tf_op jit(solution)/shard_map/ppermute | solution.py:546
  77.0 27.9 %collective-permute-start.20 = (bf16[28,8,1152]{2,1,0:T(8,128)(2,1)}, bf16[28,8,1152]{2,1,0:T(8,128)(2,1)S(1)}, u32[]{:S(2)}, u32[]{:S(2)}) collective-permute-start(bf16[28,8,1152]{2,1,0:T(8,128)(2,1)} %get-tuple-element.122), channel_id=1, source_target_pairs={{0,3},{1,2},{2,1},{3,0},{4,7},{5,6},{6,5},{7,4},{8,11},{9,10},{10,... | collective-permute-start | bytes 1548296 | tf_op jit(solution)/shard_map/ppermute | solution.py:546
  79.5 8.4 %collective-permute-start.15 = (bf16[2,48,1152]{2,1,0:T(8,128)(2,1)S(1)}, bf16[2,48,1152]{2,1,0:T(8,128)(2,1)S(1)}, u32[]{:S(2)}, u32[]{:S(2)}) collective-permute-start(bf16[2,48,1152]{2,1,0:T(8,128)(2,1)S(1)} %slice.74), channel_id=1, source_target_pairs={{0,8},{4,12},{8,0},{12,4},{16,24},{20,28},{24,16},{28,20},{1,9},{5... | collective-permute-start | bytes 663560 | tf_op jit(solution)/shard_map/ppermute | solution.py:554
  81.3 12.6 %collective-permute-start.22 = (bf16[2,56,1152]{2,1,0:T(8,128)(2,1)S(1)}, bf16[2,56,1152]{2,1,0:T(8,128)(2,1)S(1)}, u32[]{:S(2)}, u32[]{:S(2)}) collective-permute-start(bf16[2,56,1152]{2,1,0:T(8,128)(2,1)S(1)} %slice.73), channel_id=1, source_target_pairs={{0,8},{4,12},{8,0},{12,4},{16,24},{20,28},{24,16},{28,20},{1,9},{5... | collective-permute-start | bytes 774152 | tf_op jit(solution)/shard_map/ppermute | solution.py:554
  88.0 8.4 %collective-permute-start.16 = (bf16[1,48,1152]{2,1,0:T(8,128)(2,1)S(1)}, bf16[1,48,1152]{2,1,0:T(8,128)(2,1)S(1)}, u32[]{:S(2)}, u32[]{:S(2)}) collective-permute-start(bf16[1,48,1152]{2,1,0:T(8,128)(2,1)S(1)} %slice.76), channel_id=1, source_target_pairs={{0,16},{4,20},{8,24},{12,28},{16,0},{20,4},{24,8},{28,12},{1,17},{... | collective-permute-start | bytes 331784 | tf_op jit(solution)/shard_map/ppermute | solution.py:554
  94.0 7.3 %collective-permute-start.23 = (bf16[1,56,1152]{2,1,0:T(8,128)(2,1)S(1)}, bf16[1,56,1152]{2,1,0:T(8,128)(2,1)S(1)}, u32[]{:S(2)}, u32[]{:S(2)}) collective-permute-start(bf16[1,56,1152]{2,1,0:T(8,128)(2,1)S(1)} %slice.75), channel_id=1, source_target_pairs={{0,16},{4,20},{8,24},{12,28},{16,0},{20,4},{24,8},{28,12},{1,17},{... | collective-permute-start | bytes 387080 | tf_op jit(solution)/shard_map/ppermute | solution.py:554
  100.7 4.7 %collective-permute-start.19 = (bf16[48,1152]{1,0:T(8,128)(2,1)S(1)}, bf16[48,1152]{1,0:T(8,128)(2,1)S(1)}, u32[]{:S(2)}, u32[]{:S(2)}) collective-permute-start(bf16[48,1152]{1,0:T(8,128)(2,1)S(1)} %fusion.1), channel_id=1, source_target_pairs={{0,1},{1,0},{2,3},{3,2},{4,5},{5,4},{6,7},{7,6},{8,9},{9,8},{10,11... | collective-permute-start | bytes 331784 | tf_op jit(solution)/shard_map/ppermute | solution.py:546
  101.3 7.2 %collective-permute-start.24 = (bf16[56,1152]{1,0:T(8,128)(2,1)S(1)}, bf16[56,1152]{1,0:T(8,128)(2,1)S(1)}, u32[]{:S(2)}, u32[]{:S(2)}) collective-permute-start(bf16[56,1152]{1,0:T(8,128)(2,1)S(1)} %fusion.2), channel_id=1, source_target_pairs={{0,1},{1,0},{2,3},{3,2},{4,5},{5,4},{6,7},{7,6},{8,9},{9,8},{10,11... | collective-permute-start | bytes 387080 | tf_op jit(solution)/shard_map/ppermute | solution.py:546
  102.8 5.7 %collective-permute-start.25 = (bf16[56,1152]{1,0:T(8,128)(2,1)S(1)}, bf16[56,1152]{1,0:T(8,128)(2,1)S(1)}, u32[]{:S(2)}, u32[]{:S(2)}) collective-permute-start(bf16[56,1152]{1,0:T(8,128)(2,1)S(1)} %fusion.2), channel_id=1, source_target_pairs={{0,2},{1,3},{2,0},{3,1},{4,6},{5,7},{6,4},{7,5},{8,10},{9,11},{10,... | collective-permute-start | bytes 387080 | tf_op jit(solution)/shard_map/ppermute | solution.py:546
  103.5 5.9 %collective-permute-start.26 = (bf16[56,1152]{1,0:T(8,128)(2,1)S(1)}, bf16[56,1152]{1,0:T(8,128)(2,1)S(1)}, u32[]{:S(2)}, u32[]{:S(2)}) collective-permute-start(bf16[56,1152]{1,0:T(8,128)(2,1)S(1)} %fusion.2), channel_id=1, source_target_pairs={{0,3},{1,2},{2,1},{3,0},{4,7},{5,6},{6,5},{7,4},{8,11},{9,10},{10,... | collective-permute-start | bytes 387080 | tf_op jit(solution)/shard_map/ppermute | solution.py:546
  105.4 5.1 %collective-permute-start.21 = (bf16[48,1152]{1,0:T(8,128)(2,1)S(1)}, bf16[48,1152]{1,0:T(8,128)(2,1)S(1)}, u32[]{:S(2)}, u32[]{:S(2)}) collective-permute-start(bf16[48,1152]{1,0:T(8,128)(2,1)S(1)} %add_convert_fusion), channel_id=1, source_target_pairs={{0,2},{1,3},{2,0},{3,1},{4,6},{5,7},{6,4},{7,5},{8,10},{9,11},{10,... | collective-permute-start | bytes 331784 | tf_op jit(solution)/shard_map/ppermute | solution.py:546
  (21 other events, 151.2 us)
